TPU v7x, 1024 devices: a whole 4x4x32 slice. The times are simulated.
1024 devices in a mesh: gx: 16 (over z_hi, y), gy: 16 (over z_lo, core), gz: 4 (over x).
Axes of the slice: x: 4, y: 4, z: 32 (z_hi: 4, z_lo: 8; z = z_hi * 8 + z_lo), core: 2. Of those that a mesh axis runs over, the one named last changes fastest.
Arguments:
- initial: float32 [128, 512, 2048], P('gz', 'gx', 'gy'), may hold values from -6 to 6
- source: float32 [128, 512, 2048], P('gz', 'gx', 'gy'), may hold values from -24 to 24
- permeability: float32 [128, 512, 2048], P('gz', 'gx', 'gy'), may hold values from 0.5 to 4
- velocity: bfloat16 [3, 128, 512, 2048], P(None, 'gz', 'gx', 'gy'), may hold values from -4 to 4
Outputs:
- updated: float32 [128, 512, 2048], P('gz', 'gx', 'gy')
All inputs are finite; a program needn't handle non-finite values.
Results may differ from a plain program's by a relative error of at most 0.0003.
Values sent between devices are 32-bit elements; how exact they have to be, the bound alone decides.
No kernel may reach another device: no remote copies, remote signals or barrier semaphores. Data moves between devices by JAX's collectives and lax.ppermute only.
A program may use at most 64 MiB of HBM per device.

v0:
```python
import jax
import jax.numpy as jnp
from jax import lax
from jax.sharding import PartitionSpec as P

FACTOR = 8
DEGREE = 4
SWEEPS = 4


THETA = 1.15
DELTA = 0.85
OMEGA = 0.8


def with_halo(block, sides, width):
    for axis, dim in sides:
        count = lax.axis_size(axis)
        forward = [(i, i + 1) for i in range(count - 1)]
        backward = [(target, source) for source, target in forward]
        low = lax.ppermute(
            lax.slice_in_dim(block, block.shape[dim] - width, None, axis=dim), axis, forward
        )
        high = lax.ppermute(lax.slice_in_dim(block, 0, width, axis=dim), axis, backward)
        block = jnp.concatenate([low, block, high], axis=dim)
    return block


def stencil(padded, field, permeability, speeds):
    lows = [padded[:-2, 1:-1, 1:-1], padded[1:-1, :-2, 1:-1], padded[1:-1, 1:-1, :-2]]
    highs = [padded[2:, 1:-1, 1:-1], padded[1:-1, 2:, 1:-1], padded[1:-1, 1:-1, 2:]]
    total = permeability * (
        6.0 * field - (lows[0] + highs[0] + lows[1] + highs[1] + lows[2] + highs[2])
    )
    for axis_k in range(3):
        speed = speeds[axis_k]
        total = (
            total
            + jnp.maximum(speed, 0.0) * (field - lows[axis_k])
            + jnp.minimum(speed, 0.0) * (highs[axis_k] - field)
        )
    return total


def coarse_sweep(padded, errors, coarse_res, coarse_perm):
    beside_all = (
        padded[:-2, 1:-1, 1:-1]
        + padded[2:, 1:-1, 1:-1]
        + padded[1:-1, :-2, 1:-1]
        + padded[1:-1, 2:, 1:-1]
        + padded[1:-1, 1:-1, :-2]
        + padded[1:-1, 1:-1, 2:]
    )
    applied = coarse_perm * (6.0 * errors - beside_all)
    return errors + OMEGA * (coarse_res - applied) / (6.0 * coarse_perm)


def block_sum(field):
    depth, width, length = field.shape
    return field.reshape(
        depth // FACTOR, FACTOR, width // FACTOR, FACTOR, length // FACTOR, FACTOR
    ).sum(axis=(1, 3, 5))


def prolong(coarse):
    depth, width, length = coarse.shape
    wide = jnp.broadcast_to(
        coarse[:, None, :, None, :, None], (depth, FACTOR, width, FACTOR, length, FACTOR)
    )
    return wide.reshape(depth * FACTOR, width * FACTOR, length * FACTOR)


def per_device(initial, source, permeability, velocity):
    speeds = velocity.astype(jnp.float32)
    sigma = THETA / DELTA
    jacobi_diag = 6.0 * permeability + jnp.abs(speeds[0]) + jnp.abs(speeds[1]) + jnp.abs(speeds[2])

    def operate(field):
        padded = with_halo(field, (("gz", 0), ("gx", 1), ("gy", 2)), 1)
        return stencil(padded, field, permeability, speeds)

    start_res = source - operate(initial)
    rho = 1.0 / sigma
    residual = start_res
    direction = residual / (THETA * jacobi_diag)
    smooth = jnp.zeros_like(initial)
    for degree_index in range(DEGREE):
        smooth = smooth + direction
        if degree_index + 1 < DEGREE:
            residual = residual - operate(direction)
            rho_new = 1.0 / (2.0 * sigma - rho)
            direction = rho_new * rho * direction + 2.0 * rho_new / DELTA * residual / jacobi_diag
            rho = rho_new
    coarse_res = block_sum(start_res)
    coarse_perm = block_sum(permeability) * (64.0 / (FACTOR * FACTOR * FACTOR))
    first_errors = OMEGA * coarse_res / (6.0 * coarse_perm)
    errors = first_errors
    for sweep_index in range(SWEEPS - 1):
        padded = with_halo(errors, (("gz", 0), ("gx", 1), ("gy", 2)), 1)
        errors = coarse_sweep(padded, errors, coarse_res, coarse_perm)
    return initial + smooth + prolong(errors)


def solution(mesh):
    placed = (
        P("gz", "gx", "gy"),
        P("gz", "gx", "gy"),
        P("gz", "gx", "gy"),
        P(None, "gz", "gx", "gy"),
    )
    return jax.shard_map(
        per_device, mesh=mesh, in_specs=placed, out_specs=P("gz", "gx", "gy"), check_vma=False
    )
```

profile of v0, /device:TPU:871, one launch (start us, length us, event | category | flops | bytes accessed | tf_op | source)
XLA Modules:
  0.0 288.8 jit_solution(10109440202717713816)
XLA Ops:
  7.2 10.6 %collective-permute-start.3 = (f32[34,1,128]{2,1,0:T(1,128)S(1)}, f32[34,1,128]{2,1,0:T(1,128)S(1)}, u32[]{:S(2)}, u32[]{:S(2)}) collective-permute-start(f32[34,1,128]{2,1,0:T(1,128)S(1)} %get-tuple-element.27), channel_id=1, source_target_pairs={{64,0},{128,64},{192,128},{256,192},{320,256},{384,320},{448,384},... | collective-permute-start | bytes 52232 | tf_op jit(solution)/shard_map/ppermute | solution.py:24
  19.8 13.5 %collective-permute-done.2 = f32[34,1,128]{2,1,0:T(1,128)S(1)} collective-permute-done((f32[34,1,128]{2,1,0:T(1,128)S(1)}, f32[34,1,128]{2,1,0:T(1,128)S(1)}, u32[]{:S(2)}, u32[]{:S(2)}) %collective-permute-start.2) | collective-permute-done | bytes 17440 | tf_op jit(solution)/shard_map/ppermute | solution.py:21
  34.0 5.0 %collective-permute-start.5 = (f32[34,34,1]{1,2,0:T(1,128)S(1)}, f32[34,34,1]{1,2,0:T(1,128)S(1)}, u32[]{:S(2)}, u32[]{:S(2)}) collective-permute-start(f32[34,34,1]{1,2,0:T(1,128)S(1)} %copy.7), channel_id=1, source_target_pairs={{4,0},{8,4},{12,8},{16,12},{20,16},{24,20},{28,24},{32,28},{36,32}... | collective-permute-start | bytes 13880 | tf_op jit(solution)/shard_map/ppermute | solution.py:24
  42.0 6.2 %reshape.26 = f32[4,8,4,8,16,8]{5,4,3,2,1,0:T(8,128)} reshape(f32[32,32,128]{2,1,0:T(8,128)S(1)} %copy-done) | data formatting | bytes 1048576 | tf_op jit(solution)/shard_map/reshape | solution.py:60
  54.7 4.5 %multiply_divide_fusion = (f32[32,32,128]{2,1,0:T(8,128)S(1)}, f32[32,32,128]{2,1,0:T(8,128)}, f32[32,32,128]{2,1,0:T(8,128)S(1)}) fusion(f32[3,32,32,128]{3,2,1,0:T(8,128)S(1)} %convert_element_type.3, f32[32,32,128]{2,1,0:T(8,128)S(1)} %copy-done, f32[32,32,128]{2,1,0:T(8,128)} %param.5, f32[32,32,128]{2,1,0:T(8,128)} %param.4, f32[34,34,1]{2,1,0:T(8,128)} %copy.8, ...), kind=kLoop, calls=%fused_computation.172 | loop fusion | flops 6815744 | bytes 5352480 | tf_op jit(solution)/shard_map/div | solution.py:85
  59.3 6.2 %reshape.25 = f32[4,8,4,8,16,8]{5,4,3,2,1,0:T(8,128)} reshape(f32[32,32,128]{2,1,0:T(8,128)S(1)} %get-tuple-element.11) | data formatting | bytes 1048576 | tf_op jit(solution)/shard_map/reshape | solution.py:60
  65.5 4.0 %reduce_sum.18 = f32[4,4,16]{2,1,0:T(4,128)S(1)} reduce(f32[4,8,4,8,16,8]{5,4,3,2,1,0:T(8,128)} %reshape.25, f32[]{:T(128)} %constant.1.clone.1), dimensions={1,3,5}, to_apply=%region_0.0 | reduce | flops 130816 | bytes 525316 | tf_op jit(solution)/shard_map/reduce_sum | solution.py:62
  69.5 4.1 %collective-permute-start.25 = (f32[1,4,16]{2,1,0:T(4,128)S(1)}, f32[1,4,16]{2,1,0:T(4,128)S(1)}, u32[]{:S(2)}, u32[]{:S(2)}) collective-permute-start(f32[1,4,16]{2,1,0:T(4,128)S(1)} %get-tuple-element.53), channel_id=1, source_target_pairs={{1,0},{2,1},{3,2},{5,4},{6,5},{7,6},{9,8},{10,9},{11,10},{13,12},{... | collective-permute-start | bytes 776 | tf_op jit(solution)/shard_map/ppermute | solution.py:24
  83.3 11.8 %collective-permute-done.26 = f32[6,1,16]{2,1,0:T(1,128)S(1)} collective-permute-done((f32[6,1,16]{2,1,0:T(1,128)S(1)}, f32[6,1,16]{2,1,0:T(1,128)S(1)}, u32[]{:S(2)}, u32[]{:S(2)}) %collective-permute-start.26) | collective-permute-done | bytes 416 | tf_op jit(solution)/shard_map/ppermute | solution.py:21
  95.1 4.2 %collective-permute-start.29 = (f32[6,6,1]{2,1,0:T(8,128)S(1)}, f32[6,6,1]{2,1,0:T(8,128)S(1)}, u32[]{:S(2)}, u32[]{:S(2)}) collective-permute-start(f32[6,6,1]{2,1,0:T(8,128)S(1)} %get-tuple-element.41), channel_id=1, source_target_pairs={{4,0},{8,4},{12,8},{16,12},{20,16},{24,20},{28,24},{32,28},{36,32}... | collective-permute-start | bytes 440 | tf_op jit(solution)/shard_map/ppermute | solution.py:24
  117.5 12.7 %collective-permute-start.9 = (f32[34,1,128]{2,1,0:T(1,128)S(1)}, f32[34,1,128]{2,1,0:T(1,128)S(1)}, u32[]{:S(2)}, u32[]{:S(2)}) collective-permute-start(f32[34,1,128]{2,1,0:T(1,128)S(1)} %get-tuple-element.25), channel_id=1, source_target_pairs={{64,0},{128,64},{192,128},{256,192},{320,256},{384,320},{448,384},... | collective-permute-start | bytes 52232 | tf_op jit(solution)/shard_map/ppermute | solution.py:24
  132.3 13.3 %collective-permute-done.8 = f32[34,1,128]{2,1,0:T(1,128)S(1)} collective-permute-done((f32[34,1,128]{2,1,0:T(1,128)S(1)}, f32[34,1,128]{2,1,0:T(1,128)S(1)}, u32[]{:S(2)}, u32[]{:S(2)}) %collective-permute-start.8) | collective-permute-done | bytes 17440 | tf_op jit(solution)/shard_map/ppermute | solution.py:21
  148.4 6.0 %collective-permute-start.11 = (f32[34,34,1]{1,2,0:T(1,128)S(1)}, f32[34,34,1]{1,2,0:T(1,128)S(1)}, u32[]{:S(2)}, u32[]{:S(2)}) collective-permute-start(f32[34,34,1]{1,2,0:T(1,128)S(1)} %copy.11), channel_id=1, source_target_pairs={{4,0},{8,4},{12,8},{16,12},{20,16},{24,20},{28,24},{32,28},{36,32}... | collective-permute-start | bytes 13880 | tf_op jit(solution)/shard_map/ppermute | solution.py:24
  161.8 4.9 %collective-permute-start.34 = (f32[6,6,1]{2,1,0:T(8,128)S(1)}, f32[6,6,1]{2,1,0:T(8,128)S(1)}, u32[]{:S(2)}, u32[]{:S(2)}) collective-permute-start(f32[6,6,1]{2,1,0:T(8,128)S(1)} %get-tuple-element.38), channel_id=1, source_target_pairs={{0,4},{4,8},{8,12},{12,16},{16,20},{20,24},{24,28},{28,32},{32,36}... | collective-permute-start | bytes 440 | tf_op jit(solution)/shard_map/ppermute | solution.py:21
  172.5 4.3 %collective-permute-start.13 = (f32[1,32,128]{2,1,0:T(8,128)S(1)}, f32[1,32,128]{2,1,0:T(8,128)S(1)}, u32[]{:S(2)}, u32[]{:S(2)}) collective-permute-start(f32[1,32,128]{2,1,0:T(8,128)S(1)} %get-tuple-element.31), channel_id=1, source_target_pairs={{1,0},{2,1},{3,2},{5,4},{6,5},{7,6},{9,8},{10,9},{11,10},{13,12},{... | collective-permute-start | bytes 49160 | tf_op jit(solution)/shard_map/ppermute | solution.py:24
  190.1 9.1 %collective-permute-done.14 = f32[34,1,128]{2,1,0:T(1,128)S(1)} collective-permute-done((f32[34,1,128]{2,1,0:T(1,128)S(1)}, f32[34,1,128]{2,1,0:T(1,128)S(1)}, u32[]{:S(2)}, u32[]{:S(2)}) %collective-permute-start.14) | collective-permute-done | bytes 17440 | tf_op jit(solution)/shard_map/ppermute | solution.py:21
  204.6 4.4 %collective-permute-start.16 = (f32[34,34,1]{1,2,0:T(1,128)S(1)}, f32[34,34,1]{1,2,0:T(1,128)S(1)}, u32[]{:S(2)}, u32[]{:S(2)}) collective-permute-start(f32[34,34,1]{1,2,0:T(1,128)S(1)} %copy.13), channel_id=1, source_target_pairs={{0,4},{4,8},{8,12},{12,16},{16,20},{20,24},{24,28},{28,32},{32,36}... | collective-permute-start | bytes 13880 | tf_op jit(solution)/shard_map/ppermute | solution.py:21
  228.9 14.2 %collective-permute-start.21 = (f32[34,1,128]{2,1,0:T(1,128)S(1)}, f32[34,1,128]{2,1,0:T(1,128)S(1)}, u32[]{:S(2)}, u32[]{:S(2)}) collective-permute-start(f32[34,1,128]{2,1,0:T(1,128)S(1)} %get-tuple-element.21), channel_id=1, source_target_pairs={{64,0},{128,64},{192,128},{256,192},{320,256},{384,320},{448,384},... | collective-permute-start | bytes 52232 | tf_op jit(solution)/shard_map/ppermute | solution.py:24
  247.0 5.0 %collective-permute-start.40 = (f32[6,6,1]{2,1,0:T(8,128)S(1)}, f32[6,6,1]{2,1,0:T(8,128)S(1)}, u32[]{:S(2)}, u32[]{:S(2)}) collective-permute-start(f32[6,6,1]{2,1,0:T(8,128)S(1)} %get-tuple-element.36), channel_id=1, source_target_pairs={{0,4},{4,8},{8,12},{12,16},{16,20},{20,24},{24,28},{28,32},{32,36}... | collective-permute-start | bytes 440 | tf_op jit(solution)/shard_map/ppermute | solution.py:21
  252.1 7.7 %collective-permute-done.20 = f32[34,1,128]{2,1,0:T(1,128)S(1)} collective-permute-done((f32[34,1,128]{2,1,0:T(1,128)S(1)}, f32[34,1,128]{2,1,0:T(1,128)S(1)}, u32[]{:S(2)}, u32[]{:S(2)}) %collective-permute-start.20) | collective-permute-done | bytes 17440 | tf_op jit(solution)/shard_map/ppermute | solution.py:21
  266.4 4.3 %collective-permute-start.22 = (f32[34,34,1]{1,2,0:T(1,128)S(1)}, f32[34,34,1]{1,2,0:T(1,128)S(1)}, u32[]{:S(2)}, u32[]{:S(2)}) collective-permute-start(f32[34,34,1]{1,2,0:T(1,128)S(1)} %copy.17), channel_id=1, source_target_pairs={{0,4},{4,8},{8,12},{12,16},{16,20},{20,24},{24,28},{28,32},{32,36}... | collective-permute-start | bytes 13880 | tf_op jit(solution)/shard_map/ppermute | solution.py:21
  270.9 4.1 %broadcast_in_dim.2 = f32[4,8,4,8,16,8]{5,4,3,2,1,0:T(8,128)} broadcast(f32[4,4,16]{2,1,0:T(4,128)S(1)} %fusion.94), dimensions={0,2,4} | broadcast | bytes 525312 | tf_op jit(solution)/shard_map/broadcast_in_dim | solution.py:67
  275.0 7.1 %reshape.27 = f32[32,32,128]{2,1,0:T(8,128)} reshape(f32[4,8,4,8,16,8]{5,4,3,2,1,0:T(8,128)} %broadcast_in_dim.2) | data formatting | bytes 1048576 | tf_op jit(solution)/shard_map/reshape | solution.py:70
  284.5 4.3 %add_add_fusion = f32[32,32,128]{2,1,0:T(8,128)} fusion(f32[32,32,128]{2,1,0:T(8,128)} %reshape.27, f32[32,32,128]{2,1,0:T(8,128)} %param.4, f32[32,32,128]{2,1,0:T(8,128)} %get-tuple-element.10, f32[32,32,128]{2,1,0:T(8,128)} %get-tuple-element.6, f32[32,32,128]{2,1,0:T(8,128)S(1)} %get-tuple-element.5, f32[32,32,128]{2,1,0:T(8,128)S(1)} %copy-done, ...), kind=kLoop, calls=%fused_computation.169 | loop fusion | flops 8126464 | bytes 6368288 | tf_op jit(solution)/shard_map/add | solution.py:101
  (130 shorter events, 116.5 us)
Async XLA Ops:
  7.2 12.6 %collective-permute-start.3 = (f32[34,1,128]{2,1,0:T(1,128)S(1)}, f32[34,1,128]{2,1,0:T(1,128)S(1)}, u32[]{:S(2)}, u32[]{:S(2)}) collective-permute-start(f32[34,1,128]{2,1,0:T(1,128)S(1)} %get-tuple-element.27), channel_id=1, source_target_pairs={{64,0},{128,64},{192,128},{256,192},{320,256},{384,320},{448,384},... | collective-permute-start | bytes 52232 | tf_op jit(solution)/shard_map/ppermute | solution.py:24
  17.8 15.5 %collective-permute-start.2 = (f32[34,1,128]{2,1,0:T(1,128)S(1)}, f32[34,1,128]{2,1,0:T(1,128)S(1)}, u32[]{:S(2)}, u32[]{:S(2)}) collective-permute-start(f32[34,1,128]{2,1,0:T(1,128)S(1)} %get-tuple-element.26), channel_id=1, source_target_pairs={{0,64},{64,128},{128,192},{192,256},{256,320},{320,384},{384,448},... | collective-permute-start | bytes 52232 | tf_op jit(solution)/shard_map/ppermute | solution.py:21
  34.0 18.3 %collective-permute-start.5 = (f32[34,34,1]{1,2,0:T(1,128)S(1)}, f32[34,34,1]{1,2,0:T(1,128)S(1)}, u32[]{:S(2)}, u32[]{:S(2)}) collective-permute-start(f32[34,34,1]{1,2,0:T(1,128)S(1)} %copy.7), channel_id=1, source_target_pairs={{4,0},{8,4},{12,8},{16,12},{20,16},{24,20},{28,24},{32,28},{36,32}... | collective-permute-start | bytes 13880 | tf_op jit(solution)/shard_map/ppermute | solution.py:24
  39.3 14.2 %collective-permute-start.4 = (f32[34,34,1]{1,2,0:T(1,128)S(1)}, f32[34,34,1]{1,2,0:T(1,128)S(1)}, u32[]{:S(2)}, u32[]{:S(2)}) collective-permute-start(f32[34,34,1]{1,2,0:T(1,128)S(1)} %copy.5), channel_id=1, source_target_pairs={{0,4},{4,8},{8,12},{12,16},{16,20},{20,24},{24,28},{28,32},{32,36}... | collective-permute-start | bytes 13880 | tf_op jit(solution)/shard_map/ppermute | solution.py:21
  79.9 15.2 %collective-permute-start.26 = (f32[6,1,16]{2,1,0:T(1,128)S(1)}, f32[6,1,16]{2,1,0:T(1,128)S(1)}, u32[]{:S(2)}, u32[]{:S(2)}) collective-permute-start(f32[6,1,16]{2,1,0:T(1,128)S(1)} %get-tuple-element.46), channel_id=1, source_target_pairs={{0,64},{64,128},{128,192},{192,256},{256,320},{320,384},{384,448},... | collective-permute-start | bytes 1160 | tf_op jit(solution)/shard_map/ppermute | solution.py:21
  112.2 20.0 %collective-permute-start.33 = (f32[6,1,16]{2,1,0:T(1,128)S(1)}, f32[6,1,16]{2,1,0:T(1,128)S(1)}, u32[]{:S(2)}, u32[]{:S(2)}) collective-permute-start(f32[6,1,16]{2,1,0:T(1,128)S(1)} %get-tuple-element.45), channel_id=1, source_target_pairs={{64,0},{128,64},{192,128},{256,192},{320,256},{384,320},{448,384},... | collective-permute-start | bytes 1160 | tf_op jit(solution)/shard_map/ppermute | solution.py:24
  114.1 18.1 %collective-permute-start.32 = (f32[6,1,16]{2,1,0:T(1,128)S(1)}, f32[6,1,16]{2,1,0:T(1,128)S(1)}, u32[]{:S(2)}, u32[]{:S(2)}) collective-permute-start(f32[6,1,16]{2,1,0:T(1,128)S(1)} %get-tuple-element.44), channel_id=1, source_target_pairs={{0,64},{64,128},{128,192},{192,256},{256,320},{320,384},{384,448},... | collective-permute-start | bytes 1160 | tf_op jit(solution)/shard_map/ppermute | solution.py:21
  117.5 14.7 %collective-permute-start.9 = (f32[34,1,128]{2,1,0:T(1,128)S(1)}, f32[34,1,128]{2,1,0:T(1,128)S(1)}, u32[]{:S(2)}, u32[]{:S(2)}) collective-permute-start(f32[34,1,128]{2,1,0:T(1,128)S(1)} %get-tuple-element.25), channel_id=1, source_target_pairs={{64,0},{128,64},{192,128},{256,192},{320,256},{384,320},{448,384},... | collective-permute-start | bytes 52232 | tf_op jit(solution)/shard_map/ppermute | solution.py:24
  130.3 15.3 %collective-permute-start.8 = (f32[34,1,128]{2,1,0:T(1,128)S(1)}, f32[34,1,128]{2,1,0:T(1,128)S(1)}, u32[]{:S(2)}, u32[]{:S(2)}) collective-permute-start(f32[34,1,128]{2,1,0:T(1,128)S(1)} %get-tuple-element.24), channel_id=1, source_target_pairs={{0,64},{64,128},{128,192},{192,256},{256,320},{320,384},{384,448},... | collective-permute-start | bytes 52232 | tf_op jit(solution)/shard_map/ppermute | solution.py:21
  148.4 18.2 %collective-permute-start.11 = (f32[34,34,1]{1,2,0:T(1,128)S(1)}, f32[34,34,1]{1,2,0:T(1,128)S(1)}, u32[]{:S(2)}, u32[]{:S(2)}) collective-permute-start(f32[34,34,1]{1,2,0:T(1,128)S(1)} %copy.11), channel_id=1, source_target_pairs={{4,0},{8,4},{12,8},{16,12},{20,16},{24,20},{28,24},{32,28},{36,32}... | collective-permute-start | bytes 13880 | tf_op jit(solution)/shard_map/ppermute | solution.py:24
  159.8 18.3 %collective-permute-start.35 = (f32[6,6,1]{2,1,0:T(8,128)S(1)}, f32[6,6,1]{2,1,0:T(8,128)S(1)}, u32[]{:S(2)}, u32[]{:S(2)}) collective-permute-start(f32[6,6,1]{2,1,0:T(8,128)S(1)} %get-tuple-element.39), channel_id=1, source_target_pairs={{4,0},{8,4},{12,8},{16,12},{20,16},{24,20},{28,24},{32,28},{36,32}... | collective-permute-start | bytes 440 | tf_op jit(solution)/shard_map/ppermute | solution.py:24
  161.8 16.3 %collective-permute-start.34 = (f32[6,6,1]{2,1,0:T(8,128)S(1)}, f32[6,6,1]{2,1,0:T(8,128)S(1)}, u32[]{:S(2)}, u32[]{:S(2)}) collective-permute-start(f32[6,6,1]{2,1,0:T(8,128)S(1)} %get-tuple-element.38), channel_id=1, source_target_pairs={{0,4},{4,8},{8,12},{12,16},{16,20},{20,24},{24,28},{28,32},{32,36}... | collective-permute-start | bytes 440 | tf_op jit(solution)/shard_map/ppermute | solution.py:21
  183.2 16.0 %collective-permute-start.14 = (f32[34,1,128]{2,1,0:T(1,128)S(1)}, f32[34,1,128]{2,1,0:T(1,128)S(1)}, u32[]{:S(2)}, u32[]{:S(2)}) collective-permute-start(f32[34,1,128]{2,1,0:T(1,128)S(1)} %get-tuple-element.22), channel_id=1, source_target_pairs={{0,64},{64,128},{128,192},{192,256},{256,320},{320,384},{384,448},... | collective-permute-start | bytes 52232 | tf_op jit(solution)/shard_map/ppermute | solution.py:21
  186.6 22.3 %collective-permute-start.37 = (f32[1,4,16]{2,1,0:T(4,128)S(1)}, f32[1,4,16]{2,1,0:T(4,128)S(1)}, u32[]{:S(2)}, u32[]{:S(2)}) collective-permute-start(f32[1,4,16]{2,1,0:T(4,128)S(1)} %get-tuple-element.49), channel_id=1, source_target_pairs={{1,0},{2,1},{3,2},{5,4},{6,5},{7,6},{9,8},{10,9},{11,10},{13,12},{... | collective-permute-start | bytes 776 | tf_op jit(solution)/shard_map/ppermute | solution.py:24
  188.8 20.2 %collective-permute-start.36 = (f32[1,4,16]{2,1,0:T(4,128)S(1)}, f32[1,4,16]{2,1,0:T(4,128)S(1)}, u32[]{:S(2)}, u32[]{:S(2)}) collective-permute-start(f32[1,4,16]{2,1,0:T(4,128)S(1)} %get-tuple-element.48), channel_id=1, source_target_pairs={{0,1},{1,2},{2,3},{4,5},{5,6},{6,7},{8,9},{9,10},{10,11},{12,13},{... | collective-permute-start | bytes 776 | tf_op jit(solution)/shard_map/ppermute | solution.py:21
  201.8 12.7 %collective-permute-start.17 = (f32[34,34,1]{1,2,0:T(1,128)S(1)}, f32[34,34,1]{1,2,0:T(1,128)S(1)}, u32[]{:S(2)}, u32[]{:S(2)}) collective-permute-start(f32[34,34,1]{1,2,0:T(1,128)S(1)} %copy.15), channel_id=1, source_target_pairs={{4,0},{8,4},{12,8},{16,12},{20,16},{24,20},{28,24},{32,28},{36,32}... | collective-permute-start | bytes 13880 | tf_op jit(solution)/shard_map/ppermute | solution.py:24
  209.0 16.7 %collective-permute-start.39 = (f32[6,1,16]{2,1,0:T(1,128)S(1)}, f32[6,1,16]{2,1,0:T(1,128)S(1)}, u32[]{:S(2)}, u32[]{:S(2)}) collective-permute-start(f32[6,1,16]{2,1,0:T(1,128)S(1)} %get-tuple-element.43), channel_id=1, source_target_pairs={{64,0},{128,64},{192,128},{256,192},{320,256},{384,320},{448,384},... | collective-permute-start | bytes 1160 | tf_op jit(solution)/shard_map/ppermute | solution.py:24
  212.6 15.2 %collective-permute-start.38 = (f32[6,1,16]{2,1,0:T(1,128)S(1)}, f32[6,1,16]{2,1,0:T(1,128)S(1)}, u32[]{:S(2)}, u32[]{:S(2)}) collective-permute-start(f32[6,1,16]{2,1,0:T(1,128)S(1)} %get-tuple-element.42), channel_id=1, source_target_pairs={{0,64},{64,128},{128,192},{192,256},{256,320},{320,384},{384,448},... | collective-permute-start | bytes 1160 | tf_op jit(solution)/shard_map/ppermute | solution.py:21
  228.9 23.2 %collective-permute-start.21 = (f32[34,1,128]{2,1,0:T(1,128)S(1)}, f32[34,1,128]{2,1,0:T(1,128)S(1)}, u32[]{:S(2)}, u32[]{:S(2)}) collective-permute-start(f32[34,1,128]{2,1,0:T(1,128)S(1)} %get-tuple-element.21), channel_id=1, source_target_pairs={{64,0},{128,64},{192,128},{256,192},{320,256},{384,320},{448,384},... | collective-permute-start | bytes 52232 | tf_op jit(solution)/shard_map/ppermute | solution.py:24
  243.1 16.6 %collective-permute-start.20 = (f32[34,1,128]{2,1,0:T(1,128)S(1)}, f32[34,1,128]{2,1,0:T(1,128)S(1)}, u32[]{:S(2)}, u32[]{:S(2)}) collective-permute-start(f32[34,1,128]{2,1,0:T(1,128)S(1)} %get-tuple-element.20), channel_id=1, source_target_pairs={{0,64},{64,128},{128,192},{192,256},{256,320},{320,384},{384,448},... | collective-permute-start | bytes 52232 | tf_op jit(solution)/shard_map/ppermute | solution.py:21
  245.1 25.7 %collective-permute-start.41 = (f32[6,6,1]{2,1,0:T(8,128)S(1)}, f32[6,6,1]{2,1,0:T(8,128)S(1)}, u32[]{:S(2)}, u32[]{:S(2)}) collective-permute-start(f32[6,6,1]{2,1,0:T(8,128)S(1)} %get-tuple-element.37), channel_id=1, source_target_pairs={{4,0},{8,4},{12,8},{16,12},{20,16},{24,20},{28,24},{32,28},{36,32}... | collective-permute-start | bytes 440 | tf_op jit(solution)/shard_map/ppermute | solution.py:24
  247.0 23.8 %collective-permute-start.40 = (f32[6,6,1]{2,1,0:T(8,128)S(1)}, f32[6,6,1]{2,1,0:T(8,128)S(1)}, u32[]{:S(2)}, u32[]{:S(2)}) collective-permute-start(f32[6,6,1]{2,1,0:T(8,128)S(1)} %get-tuple-element.36), channel_id=1, source_target_pairs={{0,4},{4,8},{8,12},{12,16},{16,20},{20,24},{24,28},{28,32},{32,36}... | collective-permute-start | bytes 440 | tf_op jit(solution)/shard_map/ppermute | solution.py:21
  262.6 19.5 %collective-permute-start.23 = (f32[34,34,1]{1,2,0:T(1,128)S(1)}, f32[34,34,1]{1,2,0:T(1,128)S(1)}, u32[]{:S(2)}, u32[]{:S(2)}) collective-permute-start(f32[34,34,1]{1,2,0:T(1,128)S(1)} %copy.19), channel_id=1, source_target_pairs={{4,0},{8,4},{12,8},{16,12},{20,16},{24,20},{28,24},{32,28},{36,32}... | collective-permute-start | bytes 13880 | tf_op jit(solution)/shard_map/ppermute | solution.py:24
  266.4 16.9 %collective-permute-start.22 = (f32[34,34,1]{1,2,0:T(1,128)S(1)}, f32[34,34,1]{1,2,0:T(1,128)S(1)}, u32[]{:S(2)}, u32[]{:S(2)}) collective-permute-start(f32[34,34,1]{1,2,0:T(1,128)S(1)} %copy.17), channel_id=1, source_target_pairs={{0,4},{4,8},{8,12},{12,16},{16,20},{20,24},{24,28},{28,32},{32,36}... | collective-permute-start | bytes 13880 | tf_op jit(solution)/shard_map/ppermute | solution.py:21
  (22 other events, 171.7 us)
where the time goes:
time: 291 us; the launch traced here: 289 us
  starting transfers between devices  150 us (52%)
  waiting for transfers between devices  65.6 us (23%)
  local copies, waits for them, and re-layouts  47.6 us (16%)
  other arithmetic  24.8 us (9%)
    ppermute x21, starting transfers between devices, with_halo(): lax.ppermute(lax.slice_in_dim(block, 0, width, axis=dim), axis, backward)  95.8 us
    ppermute x21, waiting for transfers between devices, with_halo(): lax.ppermute(lax.slice_in_dim(block, block.shape[dim] - width, None, axis...  65.6 us
    ppermute x21, starting transfers between devices, with_halo(): lax.ppermute(lax.slice_in_dim(block, block.shape[dim] - width, None, axis...  54.4 us
    reshape x2, local copies, waits for them, and re-layouts, block_sum(): field.reshape(depth // FACTOR, FACTOR, width // FACTOR, FACTOR, length //...  12.4 us
    reduce_sum x2, other arithmetic, block_sum(): return field.reshape(depth // FACTOR, FACTOR, width // FACTOR, FACTOR, le...  8.03 us
    slice x18, local copies, waits for them, and re-layouts, with_halo(): lax.slice_in_dim(block, block.shape[dim] - width, None, axis=dim)  7.74 us
    reshape x1, local copies, waits for them, and re-layouts, prolong(): return wide.reshape(depth * FACTOR, width * FACTOR, length * FACTOR)  7.06 us
    add x2, other arithmetic, per_device(): rho_new * rho * direction + 2.0 * rho_new / DELTA * residual / jacobi_diag  6.8 us
  transfers between devices with their start and end apart: 42, of which 10 were waited for; matrix products, arithmetic and copies ran while one was open for 16% of the time, Pallas kernels for 0%

commit v1 on v0

v1 whole, which is shorter than its diff:
```python
import jax
import jax.numpy as jnp
from jax import lax
from jax.experimental import pallas as pl
from jax.experimental.pallas import tpu as pltpu
from jax.sharding import PartitionSpec as P

THETA = 1.15
DELTA = 0.85
OMEGA = 0.8
F32 = jnp.float32

NZ, NX, NY = 32, 32, 128
FULL = (NZ, NX, NY)

SIGMA = THETA / DELTA
RHO0 = 1.0 / SIGMA
RHO1 = 1.0 / (2.0 * SIGMA - RHO0)
RHO2 = 1.0 / (2.0 * SIGMA - RHO1)
RHO3 = 1.0 / (2.0 * SIGMA - RHO2)
A = (RHO1 * RHO0, RHO2 * RHO1, RHO3 * RHO2)
B = (2.0 * RHO1 / DELTA, 2.0 * RHO2 / DELTA, 2.0 * RHO3 / DELTA)

ZM1 = 136
YM1 = 40
XM1 = 104
ZM2 = 80
YM2 = 48
XM2 = 88


def iota(shape, dim):
    return lax.broadcasted_iota(jnp.int32, shape, dim)


def plane():
    return iota((NX, NY), 0), iota((NX, NY), 1)


def parity(axis):
    return lax.rem(lax.axis_index(axis), 2)


def put_out(stage, even, odd, axis):
    odd_one = parity(axis)
    even[...] = stage[1 - odd_one]
    odd[...] = stage[odd_one]


def take_in(halo, even, odd, axis):
    odd_one = parity(axis)
    halo[1 - odd_one] = even[...]
    halo[odd_one] = odd[...]


def to_column(row_values):
    row, lane = plane()
    spread = jnp.where(lane == row, jnp.broadcast_to(row_values, (NX, NY)), 0.0)
    return jnp.sum(spread, axis=1, keepdims=True)


def shift_lanes(x, amount):
    return pltpu.roll(x, amount % NY if isinstance(amount, int) else amount, 1)


def own_neighbours(field, g, z):
    here = field[z]
    total = g[0, z] * field[jnp.maximum(z - 1, 0)] + g[1, z] * field[jnp.minimum(z + 1, NZ - 1)]
    total += g[2, z] * pltpu.roll(here, 1, 0) + g[3, z] * pltpu.roll(here, NX - 1, 0)
    total += g[4, z] * pltpu.roll(here, 1, 1) + g[5, z] * pltpu.roll(here, NY - 1, 1)
    return total


def from_faces(z, zp, xp, yp):
    row, lane = plane()
    total = jnp.where(lane == 0, pltpu.roll(yp[0], lax.rem(NY - z, NY), 1), 0.0)
    total = jnp.where(lane == NY - 1, pltpu.roll(yp[1], NY - 1 - z, 1), total)
    total += jnp.where(row == 0, xp[0, pl.ds(z, 1), :], 0.0)
    total += jnp.where(row == NX - 1, xp[1, pl.ds(z, 1), :], 0.0)
    total += jnp.where(z == 0, zp[0], 0.0) + jnp.where(z == NZ - 1, zp[1], 0.0)
    return total


def pack(into, values, z, source, base):
    _, lane = plane()
    return jnp.where(lane == base + z, pltpu.roll(values, lax.rem(base + z + NY - source, NY), 1), into)


def first_kernel(u, f, p, w, g, diag, s, perm_sum, gzf, even, odd, yp, xp, stage):
    row, lane = plane()
    row8, lane8 = iota((8, NY), 0), iota((8, NY), 1)
    perm_sum[...] = jnp.zeros_like(perm_sum)

    def couplings(z):
        perm = p[z]
        speeds = [w[k, z].astype(F32) for k in range(3)]
        total = 6.0 * perm + jnp.abs(speeds[0]) + jnp.abs(speeds[1]) + jnp.abs(speeds[2])
        inverse = 1.0 / total
        pairs = []
        for speed in speeds:
            pairs.append((perm + jnp.maximum(speed, 0.0)) * inverse)
            pairs.append((perm - jnp.minimum(speed, 0.0)) * inverse)
        return perm, total, inverse, pairs

    def layer(z, carry):
        ylo, yhi, elo0, elo1, ehi0, ehi1 = carry
        perm, total, inverse, c = couplings(z)
        g[0, z] = jnp.where(z == 0, 0.0, c[0])
        g[1, z] = jnp.where(z == NZ - 1, 0.0, c[1])
        g[2, z] = jnp.where(row == 0, 0.0, c[2])
        g[3, z] = jnp.where(row == NX - 1, 0.0, c[3])
        g[4, z] = jnp.where(lane == 0, 0.0, c[4])
        g[5, z] = jnp.where(lane == NY - 1, 0.0, c[5])
        diag[z] = total
        here = u[z]
        res = f[z] * inverse - here + own_neighbours(u, g, z)
        s[z] = res
        perm_sum[z // 8] += perm
        for side, r, coupling in ((0, 0, c[2]), (1, NX - 1, c[3])):
            xp[side, pl.ds(z, 1), :] = here[r : r + 1]
            xp[side, pl.ds(NZ + z, 1), :] = res[r : r + 1]
            xp[side, pl.ds(2 * NZ + z, 1), :] = coupling[r : r + 1]
        for base, values, coupling in ((0, here, None), (32, res, None), (64, None, c)):
            ylo = pack(ylo, coupling[4] if coupling else values, z, 0, base)
            yhi = pack(yhi, coupling[5] if coupling else values, z, NY - 1, base)
        to_lo, to_hi = z, lax.rem(z + 1, NY)
        pick = lane8 == z
        elo0 = jnp.where(pick, pltpu.roll(c[2][0:8], to_lo, 1), elo0)
        elo1 = jnp.where(pick, pltpu.roll(c[3][NX - 8 :], to_lo, 1), elo1)
        ehi0 = jnp.where(pick, pltpu.roll(c[2][0:8], to_hi, 1), ehi0)
        ehi1 = jnp.where(pick, pltpu.roll(c[3][NX - 8 :], to_hi, 1), ehi1)
        return ylo, yhi, elo0, elo1, ehi0, ehi1

    zero, zero8 = jnp.zeros((NX, NY), F32), jnp.zeros((8, NY), F32)
    ylo, yhi, elo0, elo1, ehi0, ehi1 = lax.fori_loop(0, NZ, layer, (zero, zero, zero8, zero8, zero8, zero8))
    for side, body, first, last in ((0, ylo, elo0, elo1), (1, yhi, ehi0, ehi1)):
        yp[side, 0:NX, :] = body
        yp[side, NX:YM1, :] = jnp.where(row8 == 0, first[0:1], 0.0) + jnp.where(row8 == 1, last[7:8], 0.0)
        xp[side, 3 * NZ : XM1, :] = zero8
    for side, z in ((0, 0), (1, NZ - 1)):
        _, _, _, c = couplings(z)
        gzf[side] = c[side]
        stage[side, 0:32, :] = u[z]
        stage[side, 32:64, :] = s[z]
        stage[side, 64:96, :] = c[side]
        edges = jnp.where(lane == 0, c[4], 0.0) + jnp.where(lane == 1, pltpu.roll(c[5], 2, 1), 0.0)
        stage[side, 96:128, :] = edges
        stage[side, 128:136, :] = jnp.where(row8 == 0, c[2][0:1], 0.0) + jnp.where(row8 == 1, c[3][NX - 1 :], 0.0)
    put_out(stage, even, odd, "gz")


def y_body(yp, gzf, zh, side):
    _, lane = plane()
    source = 0 if side == 0 else NY - 1
    body = yp[side, 0:NX, :]
    for end, at in ((0, 32), (1, 63)):
        halo = zh[end, 0:32, :]
        body += jnp.where(lane == at, shift_lanes(gzf[end] * halo, at - source), 0.0)
        body = jnp.where(lane == 96 + end, shift_lanes(halo, 96 + end - source), body)
    return body


def first_y_kernel(zeven, zodd, gzf, yp, zh, even, odd, stage):
    take_in(zh, zeven, zodd, "gz")
    for side in (0, 1):
        stage[side, 0:NX, :] = y_body(yp, gzf, zh, side)
        stage[side, NX:YM1, :] = yp[side, NX:YM1, :]
    put_out(stage, even, odd, "gy")


def x_rows(xp, side, gzf, gy, zh, yh):
    row, lane = plane()
    row8 = iota((8, NY), 0)
    x = 0 if side == 0 else NX - 1
    res = xp[side, 32:64, :]
    lines = jnp.zeros((8, NY), F32)
    for end, at in ((0, 0), (1, NZ - 1)):
        line = zh[end, x : x + 1, :]
        res += jnp.where(row == at, gzf[end, x : x + 1, :] * line, 0.0)
        lines = jnp.where(row8 == end, line, lines)
    for end, at in ((0, 0), (1, NY - 1)):
        line = yh[end, x : x + 1, :]
        res += jnp.where(lane == at, to_column(gy[end][x : x + 1] * line), 0.0)
        lines = jnp.where(row8 == 2 + end, line, lines)
    return res, lines


def y_couplings(yp):
    return [shift_lanes(yp[side, 0:NX, :], 64) for side in (0, 1)]


def first_x_kernel(yeven, yodd, gzf, yp, xp, zh, yh, even, odd, stage):
    take_in(yh, yeven, yodd, "gy")
    gy = y_couplings(yp)
    for side in (0, 1):
        res, lines = x_rows(xp, side, gzf, gy, zh, yh)
        stage[side, 0:32, :] = xp[side, 0:32, :]
        stage[side, 32:64, :] = res
        stage[side, 64:96, :] = xp[side, 64:96, :]
        stage[side, 96:104, :] = lines
    put_out(stage, even, odd, "gx")


def z_halo_residual(side, res, zh1, xh, lines, yh, mine):
    row, lane = plane()
    x_edges = zh1[side, 128:136, :]
    y_edges = zh1[side, 96:128, :]
    total = res + zh1[side, 64:96, :] * mine
    total += jnp.where(row == 0, x_edges[0:1] * xh[0, lines + side : lines + side + 1, :], 0.0)
    total += jnp.where(row == NX - 1, x_edges[1:2] * xh[1, lines + side : lines + side + 1, :], 0.0)
    low = y_edges[:, 0:1] * yh[0, 0:NX, 96 + side : 97 + side]
    high = y_edges[:, 1:2] * yh[1, 0:NX, 96 + side : 97 + side]
    return total + jnp.where(lane == 0, low, 0.0) + jnp.where(lane == NY - 1, high, 0.0)


def y_halo_residual(side, res, yh1, xh, lines, mine):
    row, _ = plane()
    total = res + shift_lanes(yh1[side, 0:NX, :], 64) * mine
    at = lines + 2 + side
    total += jnp.where(row == 0, yh1[side, NX : NX + 1, :] * xh[0, at : at + 1, :], 0.0)
    total += jnp.where(row == NX - 1, yh1[side, NX + 1 : NX + 2, :] * xh[1, at : at + 1, :], 0.0)
    return total


def group_sums(x):
    return jnp.sum(x.reshape(4, 8, NY), axis=1)


def exact_dot(a, b):
    return jnp.dot(a, b, precision=lax.Precision.HIGHEST, preferred_element_type=F32)


def second_kernel(
    u, g, diag, s1, perm_sum, gzf, yp, xp, zh, yh, xeven, xodd,
    xh, s, d, acc, b, yp2, xp2, even, odd,
    s0, d0, cross, cross2, rsum, rows, stage,
):
    row, lane = plane()
    take_in(xh, xeven, xodd, "gx")
    gy = y_couplings(yp)
    zp, yq, zp2, yq2 = [], [], [], []
    for side, z in ((0, 0), (1, NZ - 1)):
        zp.append(gzf[side] * zh[side, 0:32, :])
        yq.append(gy[side] * yh[side, 0:NX, :])
        gx = xp[side, 64:96, :]
        cross[side] = gx * xh[side, 0:32, :]
        dz = z_halo_residual(side, zh[side, 32:64, :], zh, xh, 96, yh, u[z]) * (1.0 / THETA)
        dy = y_halo_residual(side, shift_lanes(yh[side, 0:NX, :], 96), yh, xh, 96, yp[side, 0:NX, :]) * (1.0 / THETA)
        dx = (xh[side, 32:64, :] + xh[side, 64:96, :] * xp[side, 0:32, :]) * (1.0 / THETA)
        zp2.append(gzf[side] * dz)
        yq2.append(gy[side] * dy)
        cross2[side] = gx * dx
    rsum[...] = jnp.zeros_like(rsum)

    def start(z, carry):
        res = s1[z] + from_faces(z, zp, cross, yq)
        s0[z] = res
        d0[z] = res * (1.0 / THETA)
        rsum[z // 8] += res * diag[z]
        return carry

    lax.fori_loop(0, NZ, start, 0)
    for block in range(4):
        rows[0, 4 * block : 4 * block + 4, :] = group_sums(rsum[block])
        rows[1, 4 * block : 4 * block + 4, :] = group_sums(perm_sum[block])
    select = jnp.where(iota((NY, NY), 0) // 8 == iota((NY, NY), 1), 1.0, 0.0)
    lane16 = iota((16, NY), 1)
    weights = jnp.where(lane16 < 16, exact_dot(rows[1], select), 1.0)
    rhs = jnp.where(lane16 < 16, (OMEGA * 8.0 / 6.0) * exact_dot(rows[0], select) / weights, 0.0)
    b[...] = rhs

    def step(z, carry):
        before = d0[z]
        res = s0[z] - before + own_neighbours(d0, g, z) + from_faces(z, zp2, cross2, yq2)
        after = A[0] * before + B[0] * res
        s0[z] = res
        d[z] = after
        acc[z] = u[z] + before + after
        return carry

    lax.fori_loop(0, NZ, step, 0)

    def partial(z, carry):
        ylo, yhi = carry
        here = d[z]
        res = s0[z] - here + own_neighbours(d, g, z)
        s[z] = res
        for side, r in ((0, 0), (1, NX - 1)):
            xp2[side, pl.ds(z, 1), :] = here[r : r + 1]
            xp2[side, pl.ds(NZ + z, 1), :] = res[r : r + 1]
        for base, values in ((0, here), (32, res)):
            ylo = pack(ylo, values, z, 0, base)
            yhi = pack(yhi, values, z, NY - 1, base)
        return ylo, yhi

    zero = jnp.zeros((NX, NY), F32)
    ylo, yhi = lax.fori_loop(0, NZ, partial, (zero, zero))
    yp2[0] = ylo
    yp2[1] = yhi
    for side, z in ((0, 0), (1, NZ - 1)):
        stage[side, 0:32, :] = d[z]
        stage[side, 32:64, :] = s[z]
        stage[side, 64:80, :] = rhs
    put_out(stage, even, odd, "gz")


def second_y_kernel(zeven, zodd, gzf, yp2, b, zh2, even, odd, b3, stage):
    take_in(zh2, zeven, zodd, "gz")
    lane16 = iota((16, NY), 1)
    wide = jnp.where(lane16 < 32, b[...], 0.0)
    for end in (0, 1):
        base = 32 * (end + 1)
        inside = (lane16 >= base) & (lane16 < base + 16)
        wide = jnp.where(inside, pltpu.roll(zh2[end, 64:80, :], base, 1), wide)
    b3[...] = wide
    for side in (0, 1):
        stage[side, 0:NX, :] = y_body(yp2, gzf, zh2, side)
        stage[side, NX:YM2, :] = wide
    put_out(stage, even, odd, "gy")


def second_x_kernel(yeven, yodd, gzf, yp, xp2, b3, zh2, yh2, even, odd, bw, stage):
    take_in(yh2, yeven, yodd, "gy")
    gy = y_couplings(yp)
    within = lax.rem(iota((16, NY), 1), 32)
    wide = jnp.where((within >= 3) & (within < 19), pltpu.roll(b3[...], 3, 1), 0.0)
    wide = jnp.where(within < 3, pltpu.roll(yh2[0, NX:YM2, :], NY - 13, 1), wide)
    wide = jnp.where((within >= 19) & (within < 22), pltpu.roll(yh2[1, NX:YM2, :], 19, 1), wide)
    bw[...] = wide
    for side in (0, 1):
        res, lines = x_rows(xp2, side, gzf, gy, zh2, yh2)
        stage[side, 0:32, :] = xp2[side, 0:32, :]
        stage[side, 32:64, :] = res
        stage[side, 64:72, :] = lines
        stage[side, 72:88, :] = wide
    put_out(stage, even, odd, "gx")


def coarse_solve(bw, xh2, ext, err, spread):
    ext[...] = jnp.zeros_like(ext)
    lane4 = iota((4, NY), 1)

    def blocks(values, z):
        if z < 3:
            at, shift = 4 * (z + 1), 32
        elif z < 7:
            at, shift = 4 * (z - 3), 0
        else:
            at, shift = 4 * (z - 7), 64
        rows = values[at : at + 4]
        rows = pltpu.roll(rows, NY - shift, 1) if shift else rows
        return jnp.where(lane4 < 22, rows, 0.0)

    mine, low, high = bw[...], xh2[0, 72:88, :], xh2[1, 72:88, :]
    for z in range(10):
        ext[z, 0:3, :] = blocks(low, z)[1:4]
        ext[z, 3:7, :] = blocks(mine, z)
        ext[z, 7:10, :] = blocks(high, z)[0:3]
    x, y = iota((16, NY), 0), iota((16, NY), 1)
    at_z, at_x, at_y = lax.axis_index("gz"), lax.axis_index("gx"), lax.axis_index("gy")
    last_z, last_x, last_y = lax.axis_size("gz") - 1, lax.axis_size("gx") - 1, lax.axis_size("gy") - 1
    inside = (x < 10) & (y < 22)
    inside &= ((x >= 3) | (at_x > 0)) & ((x < 7) | (at_x < last_x))
    inside &= ((y >= 3) | (at_y > 0)) & ((y < 19) | (at_y < last_y))
    keep = jnp.where(inside, 1.0, 0.0)
    keep_low = jnp.where(at_z > 0, keep, 0.0)
    keep_high = jnp.where(at_z < last_z, keep, 0.0)
    rhs = [ext[z] for z in range(10)]
    e = rhs
    for sweep in range(3):
        lo, hi = sweep + 1, 9 - sweep
        new = []
        for z in range(10):
            if z < lo or z >= hi:
                new.append(e[z])
                continue
            c = e[z]
            beside = e[z - 1] + e[z + 1] + pltpu.roll(c, 1, 0) + pltpu.roll(c, 15, 0) + pltpu.roll(c, 1, 1) + pltpu.roll(c, NY - 1, 1)
            v = (1.0 - OMEGA) * c + (OMEGA / 6.0) * beside + rhs[z]
            new.append(v * (keep_low if z < 3 else keep_high if z >= 7 else keep))
        e = new
    for z in range(4):
        err[4 * z : 4 * z + 4, :] = e[z + 3][3:7]
    select = jnp.where(iota((NY, NY), 0) == iota((NY, NY), 1) // 8 + 3, 1.0, 0.0)
    fine = exact_dot(err[...], select)
    for z in range(4):
        spread[z] = jnp.broadcast_to(fine[4 * z : 4 * z + 4][:, None, :], (4, 8, NY)).reshape(NX, NY)


def third_kernel(
    g, s2, d1, acc, gzf, yp, xp, zh, yh, xh, yp2, xp2, zh2, yh2, bw, xeven, xodd,
    out,
    xh2, s, d, cross, cross2, ext, err, spread,
):
    take_in(xh2, xeven, xodd, "gx")
    gy = y_couplings(yp)
    zp, yq, zp2, yq2 = [], [], [], []
    for side, z in ((0, 0), (1, NZ - 1)):
        zu, yu, xu = zh2[side, 0:32, :], yh2[side, 0:NX, :], xh2[side, 0:32, :]
        zp.append(gzf[side] * zu)
        yq.append(gy[side] * yu)
        gx = xp[side, 64:96, :]
        cross[side] = gx * xu
        dz = A[1] * zu + B[1] * z_halo_residual(side, zh2[side, 32:64, :], zh, xh2, 64, yh2, d1[z])
        dy = A[1] * yu + B[1] * y_halo_residual(side, shift_lanes(yu, 96), yh, xh2, 64, yp2[side])
        dx = A[1] * xu + B[1] * (xh2[side, 32:64, :] + xh[side, 64:96, :] * xp2[side, 0:32, :])
        zp2.append(gzf[side] * dz)
        yq2.append(gy[side] * dy)
        cross2[side] = gx * dx
    coarse_solve(bw, xh2, ext, err, spread)

    def step(z, carry):
        res = s2[z] + from_faces(z, zp, cross, yq)
        s[z] = res
        d[z] = A[1] * d1[z] + B[1] * res
        return carry

    lax.fori_loop(0, NZ, step, 0)

    def finish(z, carry):
        before = d[z]
        res = s[z] - before + own_neighbours(d, g, z) + from_faces(z, zp2, cross2, yq2)
        out[z] = acc[z] + before + (A[2] * before + B[2] * res) + spread[z // 8]
        return carry

    lax.fori_loop(0, NZ, finish, 0)


VM = pl.BlockSpec(memory_space=pltpu.VMEM)


def call(kernel, name, n_in, outs, scratch):
    return pl.pallas_call(
        kernel,
        out_shape=[jax.ShapeDtypeStruct(shape, F32) for shape in outs],
        in_specs=[VM] * n_in,
        out_specs=[VM] * len(outs),
        scratch_shapes=[pltpu.VMEM(shape, F32) for shape in scratch],
        compiler_params=pltpu.CompilerParams(vmem_limit_bytes=32 * 2**20),
        name=name,
    )


def swap(even, odd, axis):
    count = lax.axis_size(axis)
    results = []
    for first, values in ((0, even), (1, odd)):
        pairs = []
        for i in range(first, count - 1, 2):
            pairs += [(i, i + 1), (i + 1, i)]
        results.append(lax.ppermute(values, axis, pairs))
    return results


def per_device(u, f, p, w):
    face = (2, 32, NY)
    g, diag, s, perm_sum, gzf, even, odd, yp, xp = call(
        first_kernel, "faces", 4,
        [(6,) + FULL, FULL, FULL, (4, NX, NY), face, (ZM1, NY), (ZM1, NY), (2, YM1, NY), (2, XM1, NY)],
        [(2, ZM1, NY)],
    )(u, f, p, w)
    even, odd = swap(even, odd, "gz")
    zh, even, odd = call(
        first_y_kernel, "y_message", 4, [(2, ZM1, NY), (YM1, NY), (YM1, NY)], [(2, YM1, NY)]
    )(even, odd, gzf, yp)
    even, odd = swap(even, odd, "gy")
    yh, even, odd = call(
        first_x_kernel, "x_message", 6, [(2, YM1, NY), (XM1, NY), (XM1, NY)], [(2, XM1, NY)]
    )(even, odd, gzf, yp, xp, zh)
    even, odd = swap(even, odd, "gx")
    xh, s, d1, acc, b, yp2, xp2, even, odd = call(
        second_kernel, "two_steps", 12,
        [(2, XM1, NY), FULL, FULL, FULL, (16, NY), (2, NX, NY), (2, 64, NY), (ZM2, NY), (ZM2, NY)],
        [FULL, FULL, face, face, (4, NX, NY), (2, 16, NY), (2, ZM2, NY)],
    )(u, g, diag, s, perm_sum, gzf, yp, xp, zh, yh, even, odd)
    even, odd = swap(even, odd, "gz")
    zh2, even, odd, b3 = call(
        second_y_kernel, "y_message_2", 5, [(2, ZM2, NY), (YM2, NY), (YM2, NY), (16, NY)], [(2, YM2, NY)]
    )(even, odd, gzf, yp2, b)
    even, odd = swap(even, odd, "gy")
    yh2, even, odd, bw = call(
        second_x_kernel, "x_message_2", 7, [(2, YM2, NY), (XM2, NY), (XM2, NY), (16, NY)], [(2, XM2, NY)]
    )(even, odd, gzf, yp, xp2, b3, zh2)
    even, odd = swap(even, odd, "gx")
    (out,) = call(
        third_kernel, "last_steps", 17, [FULL],
        [(2, XM2, NY), FULL, FULL, face, face, (10, 16, NY), (16, NY), (4, NX, NY)],
    )(g, s, d1, acc, gzf, yp, xp, zh, yh, xh, yp2, xp2, zh2, yh2, bw, even, odd)
    return out


def solution(mesh):
    placed = (
        P("gz", "gx", "gy"),
        P("gz", "gx", "gy"),
        P("gz", "gx", "gy"),
        P(None, "gz", "gx", "gy"),
    )
    return jax.shard_map(
        per_device, mesh=mesh, in_specs=placed, out_specs=P("gz", "gx", "gy"), check_vma=False
    )
```

time: 291 us -> 110 us (0.38)
  the two profiles are of different devices: /device:TPU:871 before, /device:TPU:644 now
where the time goes in v1:
time: 110 us; the launch traced here: 109 us
  waiting for transfers between devices  42.9 us (39%)
  starting transfers between devices  38.2 us (35%)
  Pallas kernels  23.5 us (21%)
  local copies, waits for them, and re-layouts  4.26 us (4%)
    ppermute x12, waiting for transfers between devices, swap(): results.append(lax.ppermute(values, axis, pairs))  42.9 us
    ppermute x12, starting transfers between devices, swap(): results.append(lax.ppermute(values, axis, pairs))  38.2 us
    pallas_call x1, Pallas kernels, per_device(): call(second_kernel, 'two_steps', 12, [(2, XM1, NY), FULL, FULL, FULL, (16...  10.9 us
    pallas_call x1, Pallas kernels, per_device(): call(third_kernel, 'last_steps', 17, [FULL], [(2, XM2, NY), FULL, FULL, f...  6.91 us
    pallas_call x1, Pallas kernels, per_device(): call(first_kernel, 'faces', 4, [(6,) + FULL, FULL, FULL, (4, NX, NY), fac...  5.06 us
    unnamed x10, local copies, waits for them, and re-layouts  4.26 us
  transfers between devices with their start and end apart: 12, of which 9 were waited for; matrix products, arithmetic and copies ran while one was open for 0% of the time, Pallas kernels for 0%

profile of v1, /device:TPU:644, one launch (start us, length us, event | category | flops | bytes accessed | tf_op | source)
XLA Modules:
  0.0 109.0 jit_solution(2774844822283802101)
XLA Ops:
  1.0 1.1 %copy-done.2 = bf16[3,32,32,128]{3,2,1,0:T(8,128)(2,1)S(1)} copy-done((bf16[3,32,32,128]{3,2,1,0:T(8,128)(2,1)S(1)}, bf16[3,32,32,128]{3,2,1,0:T(8,128)(2,1)}, u32[]{:S(2)}) %copy-start.2) | copy-done | bytes 786456
  4.3 5.1 %faces.1 = (f32[6,32,32,128]{3,2,1,0:T(8,128)S(1)}, f32[32,32,128]{2,1,0:T(8,128)S(1)}, f32[32,32,128]{2,1,0:T(8,128)S(1)}, f32[4,32,128]{2,1,0:T(8,128)S(1)}, f...) custom-call(f32[32,32,128]{2,1,0:T(8,128)S(1)} %copy-done, ...), custom_call_target="tpu_custom_call" | custom-call | tf_op jit(solution)/shard_map/faces/pallas_call | solution.py:457
  9.3 3.1 %collective-permute-start = (f32[136,128]{1,0:T(8,128)S(1)}, f32[136,128]{1,0:T(8,128)S(1)}, u32[]{:S(2)}, u32[]{:S(2)}) collective-permute-start(f32[136,128]{1,0:T(8,128)S(1)} %get-tuple-element.44), channel_id=1, source_target_pairs={{0,1},{1,0},{2,3},{3,2},{4,5},{5,4},{6,7},{7,6},{8,9},{9,8},{10,11... | collective-permute-start | bytes 208904 | tf_op jit(solution)/shard_map/ppermute | solution.py:451
  12.4 1.9 %collective-permute-start.1 = (f32[136,128]{1,0:T(8,128)S(1)}, f32[136,128]{1,0:T(8,128)S(1)}, u32[]{:S(2)}, u32[]{:S(2)}) collective-permute-start(f32[136,128]{1,0:T(8,128)S(1)} %get-tuple-element.45), channel_id=1, source_target_pairs={{1,2},{2,1},{5,6},{6,5},{9,10},{10,9},{13,14},{14,13},{17,18},{18,... | collective-permute-start | bytes 208904 | tf_op jit(solution)/shard_map/ppermute | solution.py:451
  14.4 1.2 %collective-permute-done.zeven = f32[136,128]{1,0:T(8,128)S(1)} collective-permute-done((f32[136,128]{1,0:T(8,128)S(1)}, f32[136,128]{1,0:T(8,128)S(1)}, u32[]{:S(2)}, u32[]{:S(2)}) %collective-permute-start) | collective-permute-done | bytes 69664 | tf_op jit(solution)/shard_map/ppermute | solution.py:451
  15.5 3.1 %collective-permute-done.1.zodd = f32[136,128]{1,0:T(8,128)S(1)} collective-permute-done((f32[136,128]{1,0:T(8,128)S(1)}, f32[136,128]{1,0:T(8,128)S(1)}, u32[]{:S(2)}, u32[]{:S(2)}) %collective-permute-start.1) | collective-permute-done | bytes 69664 | tf_op jit(solution)/shard_map/ppermute | solution.py:451
  18.8 1.9 %collective-permute-start.2 = (f32[40,128]{1,0:T(8,128)S(1)}, f32[40,128]{1,0:T(8,128)S(1)}, u32[]{:S(2)}, u32[]{:S(2)}) collective-permute-start(f32[40,128]{1,0:T(8,128)S(1)} %get-tuple-element.47), channel_id=1, source_target_pairs={{0,4},{4,0},{8,12},{12,8},{16,20},{20,16},{24,28},{28,24},{32,36},... | collective-permute-start | bytes 61448 | tf_op jit(solution)/shard_map/ppermute | solution.py:451
  20.7 4.2 %collective-permute-start.3 = (f32[40,128]{1,0:T(8,128)S(1)}, f32[40,128]{1,0:T(8,128)S(1)}, u32[]{:S(2)}, u32[]{:S(2)}) collective-permute-start(f32[40,128]{1,0:T(8,128)S(1)} %get-tuple-element.48), channel_id=1, source_target_pairs={{4,8},{8,4},{12,16},{16,12},{20,24},{24,20},{28,32},{32,28},{36,40... | collective-permute-start | bytes 61448 | tf_op jit(solution)/shard_map/ppermute | solution.py:451
  24.9 2.1 %collective-permute-done.3.yodd = f32[40,128]{1,0:T(8,128)S(1)} collective-permute-done((f32[40,128]{1,0:T(8,128)S(1)}, f32[40,128]{1,0:T(8,128)S(1)}, u32[]{:S(2)}, u32[]{:S(2)}) %collective-permute-start.3) | collective-permute-done | bytes 20512 | tf_op jit(solution)/shard_map/ppermute | solution.py:451
  27.2 3.5 %collective-permute-start.4 = (f32[104,128]{1,0:T(8,128)S(1)}, f32[104,128]{1,0:T(8,128)S(1)}, u32[]{:S(2)}, u32[]{:S(2)}) collective-permute-start(f32[104,128]{1,0:T(8,128)S(1)} %get-tuple-element.50), channel_id=1, source_target_pairs={{0,64},{64,0},{128,192},{192,128},{256,320},{320,256},{384,448},{4... | collective-permute-start | bytes 159752 | tf_op jit(solution)/shard_map/ppermute | solution.py:451
  30.7 5.3 %collective-permute-start.5 = (f32[104,128]{1,0:T(8,128)S(1)}, f32[104,128]{1,0:T(8,128)S(1)}, u32[]{:S(2)}, u32[]{:S(2)}) collective-permute-start(f32[104,128]{1,0:T(8,128)S(1)} %get-tuple-element.51), channel_id=1, source_target_pairs={{64,128},{128,64},{192,256},{256,192},{320,384},{384,320},{448,512... | collective-permute-start | bytes 159752 | tf_op jit(solution)/shard_map/ppermute | solution.py:451
  35.9 13.3 %collective-permute-done.5.xodd = f32[104,128]{1,0:T(8,128)S(1)} collective-permute-done((f32[104,128]{1,0:T(8,128)S(1)}, f32[104,128]{1,0:T(8,128)S(1)}, u32[]{:S(2)}, u32[]{:S(2)}) %collective-permute-start.5) | collective-permute-done | bytes 53280 | tf_op jit(solution)/shard_map/ppermute | solution.py:451
  49.3 10.9 %two_steps.1 = (f32[2,104,128]{2,1,0:T(8,128)S(1)}, f32[32,32,128]{2,1,0:T(8,128)S(1)}, f32[32,32,128]{2,1,0:T(8,128)S(1)}, f32[32,32,128]{2,1,0:T(8,128)S(1)}, ...) custom-call(f32[32,32,128]{2,1,0:T(8,128)S(1)} %copy-done.1, ...), custom_call_target="tpu_custom_call" | custom-call | tf_op jit(solution)/shard_map/two_steps/pallas_call | solution.py:471
  60.2 1.9 %collective-permute-start.6 = (f32[80,128]{1,0:T(8,128)S(1)}, f32[80,128]{1,0:T(8,128)S(1)}, u32[]{:S(2)}, u32[]{:S(2)}) collective-permute-start(f32[80,128]{1,0:T(8,128)S(1)} %get-tuple-element.58), channel_id=1, source_target_pairs={{0,1},{1,0},{2,3},{3,2},{4,5},{5,4},{6,7},{7,6},{8,9},{9,8},{10,11... | collective-permute-start | bytes 122888 | tf_op jit(solution)/shard_map/ppermute | solution.py:451
  62.1 1.9 %collective-permute-start.7 = (f32[80,128]{1,0:T(8,128)S(1)}, f32[80,128]{1,0:T(8,128)S(1)}, u32[]{:S(2)}, u32[]{:S(2)}) collective-permute-start(f32[80,128]{1,0:T(8,128)S(1)} %get-tuple-element.59), channel_id=1, source_target_pairs={{1,2},{2,1},{5,6},{6,5},{9,10},{10,9},{13,14},{14,13},{17,18},{18,... | collective-permute-start | bytes 122888 | tf_op jit(solution)/shard_map/ppermute | solution.py:451
  64.0 2.0 %collective-permute-done.6.zeven = f32[80,128]{1,0:T(8,128)S(1)} collective-permute-done((f32[80,128]{1,0:T(8,128)S(1)}, f32[80,128]{1,0:T(8,128)S(1)}, u32[]{:S(2)}, u32[]{:S(2)}) %collective-permute-start.6) | collective-permute-done | bytes 40992 | tf_op jit(solution)/shard_map/ppermute | solution.py:451
  66.1 1.9 %collective-permute-done.7.zodd = f32[80,128]{1,0:T(8,128)S(1)} collective-permute-done((f32[80,128]{1,0:T(8,128)S(1)}, f32[80,128]{1,0:T(8,128)S(1)}, u32[]{:S(2)}, u32[]{:S(2)}) %collective-permute-start.7) | collective-permute-done | bytes 40992 | tf_op jit(solution)/shard_map/ppermute | solution.py:451
  68.1 1.9 %collective-permute-start.8 = (f32[48,128]{1,0:T(8,128)S(1)}, f32[48,128]{1,0:T(8,128)S(1)}, u32[]{:S(2)}, u32[]{:S(2)}) collective-permute-start(f32[48,128]{1,0:T(8,128)S(1)} %get-tuple-element.62), channel_id=1, source_target_pairs={{0,4},{4,0},{8,12},{12,8},{16,20},{20,16},{24,28},{28,24},{32,36},... | collective-permute-start | bytes 73736 | tf_op jit(solution)/shard_map/ppermute | solution.py:451
  70.1 6.8 %collective-permute-start.9 = (f32[48,128]{1,0:T(8,128)S(1)}, f32[48,128]{1,0:T(8,128)S(1)}, u32[]{:S(2)}, u32[]{:S(2)}) collective-permute-start(f32[48,128]{1,0:T(8,128)S(1)} %get-tuple-element.63), channel_id=1, source_target_pairs={{4,8},{8,4},{12,16},{16,12},{20,24},{24,20},{28,32},{32,28},{36,40... | collective-permute-start | bytes 73736 | tf_op jit(solution)/shard_map/ppermute | solution.py:451
  76.9 1.5 %collective-permute-done.9.yodd = f32[48,128]{1,0:T(8,128)S(1)} collective-permute-done((f32[48,128]{1,0:T(8,128)S(1)}, f32[48,128]{1,0:T(8,128)S(1)}, u32[]{:S(2)}, u32[]{:S(2)}) %collective-permute-start.9) | collective-permute-done | bytes 24608 | tf_op jit(solution)/shard_map/ppermute | solution.py:451
  78.6 1.9 %collective-permute-start.10 = (f32[88,128]{1,0:T(8,128)S(1)}, f32[88,128]{1,0:T(8,128)S(1)}, u32[]{:S(2)}, u32[]{:S(2)}) collective-permute-start(f32[88,128]{1,0:T(8,128)S(1)} %get-tuple-element.67), channel_id=1, source_target_pairs={{0,64},{64,0},{128,192},{192,128},{256,320},{320,256},{384,448},{4... | collective-permute-start | bytes 135176 | tf_op jit(solution)/shard_map/ppermute | solution.py:451
  80.5 3.8 %collective-permute-start.11 = (f32[88,128]{1,0:T(8,128)S(1)}, f32[88,128]{1,0:T(8,128)S(1)}, u32[]{:S(2)}, u32[]{:S(2)}) collective-permute-start(f32[88,128]{1,0:T(8,128)S(1)} %get-tuple-element.68), channel_id=1, source_target_pairs={{64,128},{128,64},{192,256},{256,192},{320,384},{384,320},{448,512... | collective-permute-start | bytes 135176 | tf_op jit(solution)/shard_map/ppermute | solution.py:451
  84.5 17.6 %collective-permute-done.11.xodd = f32[88,128]{1,0:T(8,128)S(1)} collective-permute-done((f32[88,128]{1,0:T(8,128)S(1)}, f32[88,128]{1,0:T(8,128)S(1)}, u32[]{:S(2)}, u32[]{:S(2)}) %collective-permute-start.11) | collective-permute-done | bytes 45088 | tf_op jit(solution)/shard_map/ppermute | solution.py:451
  102.1 6.9 %last_steps.1 = f32[32,32,128]{2,1,0:T(8,128)} custom-call(f32[6,32,32,128]{3,2,1,0:T(8,128)S(1)} %get-tuple-element.37.g, f32[32,32,128]{2,1,0:T(8,128)S(1)} %get-tuple-element.52.s2, f32[32,32,128]{2,1,0:T(8,128)S(1)} %get-tuple-element.53.d1, f32[32,32,128]{2,1,0:T(8,128)S(1)} %get-tuple-element.54.acc, f32[2,32,128]{2,1,0:T(8,128)S(1)} %get-tuple-element.41.gzf, ...), custom_call_target="tpu_custom_call" | custom-call | tf_op jit(solution)/shard_map/last_steps/pallas_call | solution.py:485
  (17 shorter events, 3.9 us)
Async XLA Ops:
  0.0 1.0 copy-start
  1.0 1.1 %copy-start.2 = (bf16[3,32,32,128]{3,2,1,0:T(8,128)(2,1)S(1)}, bf16[3,32,32,128]{3,2,1,0:T(8,128)(2,1)}, u32[]{:S(2)}) copy-start(bf16[3,32,32,128]{3,2,1,0:T(8,128)(2,1)} %w.1) | copy-start | bytes 2359300
  2.2 1.0 copy-start.3
  3.2 1.0 copy-start.4
  4.3 45.0 %copy-start.1 = (f32[32,32,128]{2,1,0:T(8,128)S(1)}, f32[32,32,128]{2,1,0:T(8,128)}, u32[]{:S(2)}) copy-start(f32[32,32,128]{2,1,0:T(8,128)} %u.3) | copy-start | bytes 1572868
  9.3 6.2 %collective-permute-start = (f32[136,128]{1,0:T(8,128)S(1)}, f32[136,128]{1,0:T(8,128)S(1)}, u32[]{:S(2)}, u32[]{:S(2)}) collective-permute-start(f32[136,128]{1,0:T(8,128)S(1)} %get-tuple-element.44), channel_id=1, source_target_pairs={{0,1},{1,0},{2,3},{3,2},{4,5},{5,4},{6,7},{7,6},{8,9},{9,8},{10,11... | collective-permute-start | bytes 208904 | tf_op jit(solution)/shard_map/ppermute | solution.py:451
  12.4 6.2 %collective-permute-start.1 = (f32[136,128]{1,0:T(8,128)S(1)}, f32[136,128]{1,0:T(8,128)S(1)}, u32[]{:S(2)}, u32[]{:S(2)}) collective-permute-start(f32[136,128]{1,0:T(8,128)S(1)} %get-tuple-element.45), channel_id=1, source_target_pairs={{1,2},{2,1},{5,6},{6,5},{9,10},{10,9},{13,14},{14,13},{17,18},{18,... | collective-permute-start | bytes 208904 | tf_op jit(solution)/shard_map/ppermute | solution.py:451
  18.8 6.2 %collective-permute-start.2 = (f32[40,128]{1,0:T(8,128)S(1)}, f32[40,128]{1,0:T(8,128)S(1)}, u32[]{:S(2)}, u32[]{:S(2)}) collective-permute-start(f32[40,128]{1,0:T(8,128)S(1)} %get-tuple-element.47), channel_id=1, source_target_pairs={{0,4},{4,0},{8,12},{12,8},{16,20},{20,16},{24,28},{28,24},{32,36},... | collective-permute-start | bytes 61448 | tf_op jit(solution)/shard_map/ppermute | solution.py:451
  20.7 6.3 %collective-permute-start.3 = (f32[40,128]{1,0:T(8,128)S(1)}, f32[40,128]{1,0:T(8,128)S(1)}, u32[]{:S(2)}, u32[]{:S(2)}) collective-permute-start(f32[40,128]{1,0:T(8,128)S(1)} %get-tuple-element.48), channel_id=1, source_target_pairs={{4,8},{8,4},{12,16},{16,12},{20,24},{24,20},{28,32},{32,28},{36,40... | collective-permute-start | bytes 61448 | tf_op jit(solution)/shard_map/ppermute | solution.py:451
  27.2 8.8 %collective-permute-start.4 = (f32[104,128]{1,0:T(8,128)S(1)}, f32[104,128]{1,0:T(8,128)S(1)}, u32[]{:S(2)}, u32[]{:S(2)}) collective-permute-start(f32[104,128]{1,0:T(8,128)S(1)} %get-tuple-element.50), channel_id=1, source_target_pairs={{0,64},{64,0},{128,192},{192,128},{256,320},{320,256},{384,448},{4... | collective-permute-start | bytes 159752 | tf_op jit(solution)/shard_map/ppermute | solution.py:451
  30.7 18.6 %collective-permute-start.5 = (f32[104,128]{1,0:T(8,128)S(1)}, f32[104,128]{1,0:T(8,128)S(1)}, u32[]{:S(2)}, u32[]{:S(2)}) collective-permute-start(f32[104,128]{1,0:T(8,128)S(1)} %get-tuple-element.51), channel_id=1, source_target_pairs={{64,128},{128,64},{192,256},{256,192},{320,384},{384,320},{448,512... | collective-permute-start | bytes 159752 | tf_op jit(solution)/shard_map/ppermute | solution.py:451
  60.2 5.9 %collective-permute-start.6 = (f32[80,128]{1,0:T(8,128)S(1)}, f32[80,128]{1,0:T(8,128)S(1)}, u32[]{:S(2)}, u32[]{:S(2)}) collective-permute-start(f32[80,128]{1,0:T(8,128)S(1)} %get-tuple-element.58), channel_id=1, source_target_pairs={{0,1},{1,0},{2,3},{3,2},{4,5},{5,4},{6,7},{7,6},{8,9},{9,8},{10,11... | collective-permute-start | bytes 122888 | tf_op jit(solution)/shard_map/ppermute | solution.py:451
  62.1 5.9 %collective-permute-start.7 = (f32[80,128]{1,0:T(8,128)S(1)}, f32[80,128]{1,0:T(8,128)S(1)}, u32[]{:S(2)}, u32[]{:S(2)}) collective-permute-start(f32[80,128]{1,0:T(8,128)S(1)} %get-tuple-element.59), channel_id=1, source_target_pairs={{1,2},{2,1},{5,6},{6,5},{9,10},{10,9},{13,14},{14,13},{17,18},{18,... | collective-permute-start | bytes 122888 | tf_op jit(solution)/shard_map/ppermute | solution.py:451
  68.1 8.8 %collective-permute-start.8 = (f32[48,128]{1,0:T(8,128)S(1)}, f32[48,128]{1,0:T(8,128)S(1)}, u32[]{:S(2)}, u32[]{:S(2)}) collective-permute-start(f32[48,128]{1,0:T(8,128)S(1)} %get-tuple-element.62), channel_id=1, source_target_pairs={{0,4},{4,0},{8,12},{12,8},{16,20},{20,16},{24,28},{28,24},{32,36},... | collective-permute-start | bytes 73736 | tf_op jit(solution)/shard_map/ppermute | solution.py:451
  70.1 8.3 %collective-permute-start.9 = (f32[48,128]{1,0:T(8,128)S(1)}, f32[48,128]{1,0:T(8,128)S(1)}, u32[]{:S(2)}, u32[]{:S(2)}) collective-permute-start(f32[48,128]{1,0:T(8,128)S(1)} %get-tuple-element.63), channel_id=1, source_target_pairs={{4,8},{8,4},{12,16},{16,12},{20,24},{24,20},{28,32},{32,28},{36,40... | collective-permute-start | bytes 73736 | tf_op jit(solution)/shard_map/ppermute | solution.py:451
  78.6 5.9 %collective-permute-start.10 = (f32[88,128]{1,0:T(8,128)S(1)}, f32[88,128]{1,0:T(8,128)S(1)}, u32[]{:S(2)}, u32[]{:S(2)}) collective-permute-start(f32[88,128]{1,0:T(8,128)S(1)} %get-tuple-element.67), channel_id=1, source_target_pairs={{0,64},{64,0},{128,192},{192,128},{256,320},{320,256},{384,448},{4... | collective-permute-start | bytes 135176 | tf_op jit(solution)/shard_map/ppermute | solution.py:451
  80.5 21.6 %collective-permute-start.11 = (f32[88,128]{1,0:T(8,128)S(1)}, f32[88,128]{1,0:T(8,128)S(1)}, u32[]{:S(2)}, u32[]{:S(2)}) collective-permute-start(f32[88,128]{1,0:T(8,128)S(1)} %get-tuple-element.68), channel_id=1, source_target_pairs={{64,128},{128,64},{192,256},{256,192},{320,384},{384,320},{448,512... | collective-permute-start | bytes 135176 | tf_op jit(solution)/shard_map/ppermute | solution.py:451

commit v2 on v1

--- a/solution.py
+++ b/solution.py
@@ -86,25 +86,69 @@
     return jnp.where(lane == base + z, pltpu.roll(values, lax.rem(base + z + NY - source, NY), 1), into)
 
 
-def first_kernel(u, f, p, w, g, diag, s, perm_sum, gzf, even, odd, yp, xp, stage):
+def couplings(perm, speeds):
+    total = 6.0 * perm + jnp.abs(speeds[0]) + jnp.abs(speeds[1]) + jnp.abs(speeds[2])
+    inverse = 1.0 / total
+    pairs = []
+    for speed in speeds:
+        pairs.append((perm + jnp.maximum(speed, 0.0)) * inverse)
+        pairs.append((perm - jnp.minimum(speed, 0.0)) * inverse)
+    return total, inverse, pairs
+
+
+def face_kernel(u, f, p, w, gzf, even, odd, planes, speed_planes, stage, sems):
+    row, lane = plane()
+    row8 = iota((8, NY), 0)
+    copies = []
+    for side, z, inner in ((0, 0, 1), (1, NZ - 1, NZ - 2)):
+        for k, source in enumerate((u.at[z], u.at[inner], f.at[z], p.at[z])):
+            copies.append(pltpu.make_async_copy(source, planes.at[side, k], sems.at[side, k]))
+        for k in range(3):
+            copies.append(pltpu.make_async_copy(w.at[k, z], speed_planes.at[side, k], sems.at[side, 4 + k]))
+    for copy in copies:
+        copy.start()
+    for copy in copies:
+        copy.wait()
+    for side in (0, 1):
+        here, inner = planes[side, 0], planes[side, 1]
+        _, inverse, c = couplings(planes[side, 3], [speed_planes[side, k].astype(F32) for k in range(3)])
+        res = planes[side, 2] * inverse - here + c[1 - side] * inner
+        res += jnp.where(row == 0, 0.0, c[2]) * pltpu.roll(here, 1, 0)
+        res += jnp.where(row == NX - 1, 0.0, c[3]) * pltpu.roll(here, NX - 1, 0)
+        res += jnp.where(lane == 0, 0.0, c[4]) * pltpu.roll(here, 1, 1)
+        res += jnp.where(lane == NY - 1, 0.0, c[5]) * pltpu.roll(here, NY - 1, 1)
+        gzf[side] = c[side]
+        stage[side, 0:32, :] = here
+        stage[side, 32:64, :] = res
+        stage[side, 64:96, :] = c[side]
+        stage[side, 96:128, :] = jnp.where(lane == 0, c[4], 0.0) + jnp.where(lane == 1, pltpu.roll(c[5], 2, 1), 0.0)
+        stage[side, 128:136, :] = jnp.where(row8 == 0, c[2][0:1], 0.0) + jnp.where(row8 == 1, c[3][NX - 1 :], 0.0)
+    put_out(stage, even, odd, "gz")
+
+
+def first_kernel(u_far, f_far, p_far, w_far, g, diag, s, perm_sum, yp, xp, u, f, p, w, sems):
     row, lane = plane()
     row8, lane8 = iota((8, NY), 0), iota((8, NY), 1)
+    copies = []
+    for part in range(4):
+        rows = pl.ds(8 * part, 8)
+        copies.append([
+            pltpu.make_async_copy(u_far.at[rows], u.at[rows], sems.at[part, 0]),
+            pltpu.make_async_copy(f_far.at[rows], f.at[rows], sems.at[part, 1]),
+            pltpu.make_async_copy(p_far.at[rows], p.at[rows], sems.at[part, 2]),
+            pltpu.make_async_copy(w_far.at[:, rows], w.at[:, rows], sems.at[part, 3]),
+        ])
+    for part in range(4):
+        copies[part][0].start()
+    for part in range(4):
+        for copy in copies[part][1:]:
+            copy.start()
     perm_sum[...] = jnp.zeros_like(perm_sum)
-
-    def couplings(z):
-        perm = p[z]
-        speeds = [w[k, z].astype(F32) for k in range(3)]
-        total = 6.0 * perm + jnp.abs(speeds[0]) + jnp.abs(speeds[1]) + jnp.abs(speeds[2])
-        inverse = 1.0 / total
-        pairs = []
-        for speed in speeds:
-            pairs.append((perm + jnp.maximum(speed, 0.0)) * inverse)
-            pairs.append((perm - jnp.minimum(speed, 0.0)) * inverse)
-        return perm, total, inverse, pairs
 
     def layer(z, carry):
         ylo, yhi, elo0, elo1, ehi0, ehi1 = carry
-        perm, total, inverse, c = couplings(z)
+        perm = p[z]
+        total, inverse, c = couplings(perm, [w[k, z].astype(F32) for k in range(3)])
         g[0, z] = jnp.where(z == 0, 0.0, c[0])
         g[1, z] = jnp.where(z == NZ - 1, 0.0, c[1])
         g[2, z] = jnp.where(row == 0, 0.0, c[2])
@@ -132,21 +176,18 @@
         return ylo, yhi, elo0, elo1, ehi0, ehi1
 
     zero, zero8 = jnp.zeros((NX, NY), F32), jnp.zeros((8, NY), F32)
-    ylo, yhi, elo0, elo1, ehi0, ehi1 = lax.fori_loop(0, NZ, layer, (zero, zero, zero8, zero8, zero8, zero8))
+    start = (zero, zero, zero8, zero8, zero8, zero8)
+    for part in range(4):
+        copies[part][0].wait()
+    for part in range(4):
+        for copy in copies[part][1:]:
+            copy.wait()
+        start = lax.fori_loop(8 * part, 8 * part + 8, layer, start, unroll=4)
+    ylo, yhi, elo0, elo1, ehi0, ehi1 = start
     for side, body, first, last in ((0, ylo, elo0, elo1), (1, yhi, ehi0, ehi1)):
         yp[side, 0:NX, :] = body
         yp[side, NX:YM1, :] = jnp.where(row8 == 0, first[0:1], 0.0) + jnp.where(row8 == 1, last[7:8], 0.0)
         xp[side, 3 * NZ : XM1, :] = zero8
-    for side, z in ((0, 0), (1, NZ - 1)):
-        _, _, _, c = couplings(z)
-        gzf[side] = c[side]
-        stage[side, 0:32, :] = u[z]
-        stage[side, 32:64, :] = s[z]
-        stage[side, 64:96, :] = c[side]
-        edges = jnp.where(lane == 0, c[4], 0.0) + jnp.where(lane == 1, pltpu.roll(c[5], 2, 1), 0.0)
-        stage[side, 96:128, :] = edges
-        stage[side, 128:136, :] = jnp.where(row8 == 0, c[2][0:1], 0.0) + jnp.where(row8 == 1, c[3][NX - 1 :], 0.0)
-    put_out(stage, even, odd, "gz")
 
 
 def y_body(yp, gzf, zh, side):
@@ -232,7 +273,7 @@
 
 def second_kernel(
     u, g, diag, s1, perm_sum, gzf, yp, xp, zh, yh, xeven, xodd,
-    xh, s, d, acc, b, yp2, xp2, even, odd,
+    xh, s, d, acc, b, even, odd,
     s0, d0, cross, cross2, rsum, rows, stage,
 ):
     row, lane = plane()
@@ -259,7 +300,7 @@
         rsum[z // 8] += res * diag[z]
         return carry
 
-    lax.fori_loop(0, NZ, start, 0)
+    lax.fori_loop(0, NZ, start, 0, unroll=8)
     for block in range(4):
         rows[0, 4 * block : 4 * block + 4, :] = group_sums(rsum[block])
         rows[1, 4 * block : 4 * block + 4, :] = group_sums(perm_sum[block])
@@ -273,17 +314,25 @@
         before = d0[z]
         res = s0[z] - before + own_neighbours(d0, g, z) + from_faces(z, zp2, cross2, yq2)
         after = A[0] * before + B[0] * res
-        s0[z] = res
+        s[z] = res
         d[z] = after
         acc[z] = u[z] + before + after
         return carry
 
-    lax.fori_loop(0, NZ, step, 0)
-
+    lax.fori_loop(0, NZ, step, 0, unroll=8)
+
+    for side, z in ((0, 0), (1, NZ - 1)):
+        stage[side, 0:32, :] = d[z]
+        stage[side, 32:64, :] = s[z] - d[z] + own_neighbours(d, g, z)
+        stage[side, 64:80, :] = rhs
+    put_out(stage, even, odd, "gz")
+
+
+def partial_kernel(g, s1, d, s, yp2, xp2):
     def partial(z, carry):
         ylo, yhi = carry
         here = d[z]
-        res = s0[z] - here + own_neighbours(d, g, z)
+        res = s1[z] - here + own_neighbours(d, g, z)
         s[z] = res
         for side, r in ((0, 0), (1, NX - 1)):
             xp2[side, pl.ds(z, 1), :] = here[r : r + 1]
@@ -294,14 +343,9 @@
         return ylo, yhi
 
     zero = jnp.zeros((NX, NY), F32)
-    ylo, yhi = lax.fori_loop(0, NZ, partial, (zero, zero))
+    ylo, yhi = lax.fori_loop(0, NZ, partial, (zero, zero), unroll=8)
     yp2[0] = ylo
     yp2[1] = yhi
-    for side, z in ((0, 0), (1, NZ - 1)):
-        stage[side, 0:32, :] = d[z]
-        stage[side, 32:64, :] = s[z]
-        stage[side, 64:80, :] = rhs
-    put_out(stage, even, odd, "gz")
 
 
 def second_y_kernel(zeven, zodd, gzf, yp2, b, zh2, even, odd, b3, stage):
@@ -415,7 +459,7 @@
         d[z] = A[1] * d1[z] + B[1] * res
         return carry
 
-    lax.fori_loop(0, NZ, step, 0)
+    lax.fori_loop(0, NZ, step, 0, unroll=8)
 
     def finish(z, carry):
         before = d[z]
@@ -423,20 +467,22 @@
         out[z] = acc[z] + before + (A[2] * before + B[2] * res) + spread[z // 8]
         return carry
 
-    lax.fori_loop(0, NZ, finish, 0)
+    lax.fori_loop(0, NZ, finish, 0, unroll=8)
 
 
 VM = pl.BlockSpec(memory_space=pltpu.VMEM)
-
-
-def call(kernel, name, n_in, outs, scratch):
+HBM = pl.BlockSpec(memory_space=pltpu.HBM)
+
+
+def call(kernel, name, n_in, outs, scratch, us=0.2, place=VM, more=()):
     return pl.pallas_call(
         kernel,
         out_shape=[jax.ShapeDtypeStruct(shape, F32) for shape in outs],
-        in_specs=[VM] * n_in,
+        in_specs=[place] * n_in,
         out_specs=[VM] * len(outs),
-        scratch_shapes=[pltpu.VMEM(shape, F32) for shape in scratch],
+        scratch_shapes=[pltpu.VMEM(shape, F32) for shape in scratch] + list(more),
         compiler_params=pltpu.CompilerParams(vmem_limit_bytes=32 * 2**20),
+        cost_estimate=pl.CostEstimate(flops=0, transcendentals=0, bytes_accessed=int(us * 3e6)),
         name=name,
     )
 
@@ -444,21 +490,26 @@
 def swap(even, odd, axis):
     count = lax.axis_size(axis)
     results = []
-    for first, values in ((0, even), (1, odd)):
+    for first, values in ((1, odd), (0, even)):
         pairs = []
         for i in range(first, count - 1, 2):
             pairs += [(i, i + 1), (i + 1, i)]
         results.append(lax.ppermute(values, axis, pairs))
-    return results
+    return results[::-1]
 
 
 def per_device(u, f, p, w):
     face = (2, 32, NY)
-    g, diag, s, perm_sum, gzf, even, odd, yp, xp = call(
-        first_kernel, "faces", 4,
-        [(6,) + FULL, FULL, FULL, (4, NX, NY), face, (ZM1, NY), (ZM1, NY), (2, YM1, NY), (2, XM1, NY)],
-        [(2, ZM1, NY)],
-    )(u, f, p, w)
+    far = [pltpu.with_memory_space_constraint(x, pltpu.HBM) for x in (u, f, p, w)]
+    gzf, even, odd = call(
+        face_kernel, "z_faces", 4, [face, (ZM1, NY), (ZM1, NY)], [(2, 4, NX, NY)], 1.0, HBM,
+        [pltpu.VMEM((2, 3, NX, NY), jnp.bfloat16), pltpu.VMEM((2, ZM1, NY), F32), pltpu.SemaphoreType.DMA((2, 7))],
+    )(*far)
+    g, diag, s, perm_sum, yp, xp = call(
+        first_kernel, "block", 4,
+        [(6,) + FULL, FULL, FULL, (4, NX, NY), (2, YM1, NY), (2, XM1, NY)], [FULL, FULL, FULL], 3.0, HBM,
+        [pltpu.VMEM((3,) + FULL, jnp.bfloat16), pltpu.SemaphoreType.DMA((4, 4))],
+    )(*far)
     even, odd = swap(even, odd, "gz")
     zh, even, odd = call(
         first_y_kernel, "y_message", 4, [(2, ZM1, NY), (YM1, NY), (YM1, NY)], [(2, YM1, NY)]
@@ -468,11 +519,14 @@
         first_x_kernel, "x_message", 6, [(2, YM1, NY), (XM1, NY), (XM1, NY)], [(2, XM1, NY)]
     )(even, odd, gzf, yp, xp, zh)
     even, odd = swap(even, odd, "gx")
-    xh, s, d1, acc, b, yp2, xp2, even, odd = call(
+    xh, s, d1, acc, b, even, odd = call(
         second_kernel, "two_steps", 12,
-        [(2, XM1, NY), FULL, FULL, FULL, (16, NY), (2, NX, NY), (2, 64, NY), (ZM2, NY), (ZM2, NY)],
-        [FULL, FULL, face, face, (4, NX, NY), (2, 16, NY), (2, ZM2, NY)],
+        [(2, XM1, NY), FULL, FULL, FULL, (16, NY), (ZM2, NY), (ZM2, NY)],
+        [FULL, FULL, face, face, (4, NX, NY), (2, 16, NY), (2, ZM2, NY)], 3.0,
     )(u, g, diag, s, perm_sum, gzf, yp, xp, zh, yh, even, odd)
+    s, yp2, xp2 = call(
+        partial_kernel, "block_2", 3, [FULL, (2, NX, NY), (2, 64, NY)], [], 1.5
+    )(g, s, d1)
     even, odd = swap(even, odd, "gz")
     zh2, even, odd, b3 = call(
         second_y_kernel, "y_message_2", 5, [(2, ZM2, NY), (YM2, NY), (YM2, NY), (16, NY)], [(2, YM2, NY)]
@@ -484,7 +538,7 @@
     even, odd = swap(even, odd, "gx")
     (out,) = call(
         third_kernel, "last_steps", 17, [FULL],
-        [(2, XM2, NY), FULL, FULL, face, face, (10, 16, NY), (16, NY), (4, NX, NY)],
+        [(2, XM2, NY), FULL, FULL, face, face, (10, 16, NY), (16, NY), (4, NX, NY)], 3.0,
     )(g, s, d1, acc, gzf, yp, xp, zh, yh, xh, yp2, xp2, zh2, yh2, bw, even, odd)
     return out
 

time: 110 us -> 89.4 us (0.81)
  the two profiles are of different devices: /device:TPU:644 before, /device:TPU:642 now
where the time goes in v2:
time: 89.4 us; the launch traced here: 89 us
  starting transfers between devices  40 us (45%)
  waiting for transfers between devices  36.4 us (41%)
  Pallas kernels  12.4 us (14%)
    ppermute x12, starting transfers between devices, swap(): results.append(lax.ppermute(values, axis, pairs))  40 us
    ppermute x12, waiting for transfers between devices, swap(): results.append(lax.ppermute(values, axis, pairs))  36.4 us
    pallas_call x1, Pallas kernels, per_device(): call(first_kernel, 'block', 4, [(6,) + FULL, FULL, FULL, (4, NX, NY), (2,...  3.98 us
    pallas_call x1, Pallas kernels, per_device(): call(third_kernel, 'last_steps', 17, [FULL], [(2, XM2, NY), FULL, FULL, f...  2.7 us
    pallas_call x1, Pallas kernels, per_device(): call(second_kernel, 'two_steps', 12, [(2, XM1, NY), FULL, FULL, FULL, (16...  2.01 us
    pallas_call x1, Pallas kernels, per_device(): call(partial_kernel, 'block_2', 3, [FULL, (2, NX, NY), (2, 64, NY)], [],...  1.92 us
  transfers between devices with their start and end apart: 12, of which 6 were waited for; matrix products, arithmetic and copies ran while one was open for 0% of the time, Pallas kernels for 7%

profile of v2, /device:TPU:642, one launch (start us, length us, event | category | flops | bytes accessed | tf_op | source)
XLA Modules:
  0.0 89.0 jit_solution(13765116536283245430)
XLA Ops:
  0.0 1.2 %z_faces.1 = (f32[2,32,128]{2,1,0:T(8,128)S(1)}, f32[136,128]{1,0:T(8,128)S(1)}, f32[136,128]{1,0:T(8,128)S(1)}) custom-call(f32[32,32,128]{2,1,0:T(8,128)} %u.3, f32[32,32,128]{2,1,0:T(8,128)} %f.1, f32[32,32,128]{2,1,0:T(8,128)} %p.1, bf16[3,32,32,128]{3,2,1,0:T(8,128)(2,1)} %w.1), custom_call_target="tpu_custom_call" | custom-call | bytes 3000000 | tf_op jit(solution)/shard_map/z_faces/pallas_call | solution.py:504
  1.2 2.4 %collective-permute-start = (f32[136,128]{1,0:T(8,128)S(1)}, f32[136,128]{1,0:T(8,128)S(1)}, u32[]{:S(2)}, u32[]{:S(2)}) collective-permute-start(f32[136,128]{1,0:T(8,128)S(1)} %get-tuple-element.45), channel_id=1, source_target_pairs={{0,1},{1,0},{2,3},{3,2},{4,5},{5,4},{6,7},{7,6},{8,9},{9,8},{10,11... | collective-permute-start | bytes 208904 | tf_op jit(solution)/shard_map/ppermute | solution.py:497
  3.6 4.1 %collective-permute-start.1 = (f32[136,128]{1,0:T(8,128)S(1)}, f32[136,128]{1,0:T(8,128)S(1)}, u32[]{:S(2)}, u32[]{:S(2)}) collective-permute-start(f32[136,128]{1,0:T(8,128)S(1)} %get-tuple-element.46), channel_id=1, source_target_pairs={{1,2},{2,1},{5,6},{6,5},{9,10},{10,9},{13,14},{14,13},{17,18},{18,... | collective-permute-start | bytes 208904 | tf_op jit(solution)/shard_map/ppermute | solution.py:497
  7.7 4.0 %block.1 = (f32[6,32,32,128]{3,2,1,0:T(8,128)S(1)}, f32[32,32,128]{2,1,0:T(8,128)S(1)}, f32[32,32,128]{2,1,0:T(8,128)S(1)}, f32[4,32,128]{2,1,0:T(8,128)S(1)}, f...) custom-call(f32[32,32,128]{2,1,0:T(8,128)} %u.3, f32[32,32,128]{2,1,0:T(8,128)} %f.1, f32[32,32,128]{2,1,0:T(8,128)} %p.1, ...), custom_call_target="tpu_custom_call" | custom-call | bytes 9000000 | tf_op jit(solution)/shard_map/block/pallas_call | solution.py:508
  11.8 1.9 %collective-permute-start.2 = (f32[40,128]{1,0:T(8,128)S(1)}, f32[40,128]{1,0:T(8,128)S(1)}, u32[]{:S(2)}, u32[]{:S(2)}) collective-permute-start(f32[40,128]{1,0:T(8,128)S(1)} %get-tuple-element.48), channel_id=1, source_target_pairs={{0,4},{4,0},{8,12},{12,8},{16,20},{20,16},{24,28},{28,24},{32,36},... | collective-permute-start | bytes 61448 | tf_op jit(solution)/shard_map/ppermute | solution.py:497
  13.8 4.2 %collective-permute-start.3 = (f32[40,128]{1,0:T(8,128)S(1)}, f32[40,128]{1,0:T(8,128)S(1)}, u32[]{:S(2)}, u32[]{:S(2)}) collective-permute-start(f32[40,128]{1,0:T(8,128)S(1)} %get-tuple-element.49), channel_id=1, source_target_pairs={{4,8},{8,4},{12,16},{16,12},{20,24},{24,20},{28,32},{32,28},{36,40... | collective-permute-start | bytes 61448 | tf_op jit(solution)/shard_map/ppermute | solution.py:497
  18.0 2.1 %collective-permute-done.3.yodd = f32[40,128]{1,0:T(8,128)S(1)} collective-permute-done((f32[40,128]{1,0:T(8,128)S(1)}, f32[40,128]{1,0:T(8,128)S(1)}, u32[]{:S(2)}, u32[]{:S(2)}) %collective-permute-start.3) | collective-permute-done | bytes 20512 | tf_op jit(solution)/shard_map/ppermute | solution.py:497
  20.2 3.5 %collective-permute-start.4 = (f32[104,128]{1,0:T(8,128)S(1)}, f32[104,128]{1,0:T(8,128)S(1)}, u32[]{:S(2)}, u32[]{:S(2)}) collective-permute-start(f32[104,128]{1,0:T(8,128)S(1)} %get-tuple-element.51), channel_id=1, source_target_pairs={{0,64},{64,0},{128,192},{192,128},{256,320},{320,256},{384,448},{4... | collective-permute-start | bytes 159752 | tf_op jit(solution)/shard_map/ppermute | solution.py:497
  23.7 5.3 %collective-permute-start.5 = (f32[104,128]{1,0:T(8,128)S(1)}, f32[104,128]{1,0:T(8,128)S(1)}, u32[]{:S(2)}, u32[]{:S(2)}) collective-permute-start(f32[104,128]{1,0:T(8,128)S(1)} %get-tuple-element.52), channel_id=1, source_target_pairs={{64,128},{128,64},{192,256},{256,192},{320,384},{384,320},{448,512... | collective-permute-start | bytes 159752 | tf_op jit(solution)/shard_map/ppermute | solution.py:497
  29.0 13.3 %collective-permute-done.5.xodd = f32[104,128]{1,0:T(8,128)S(1)} collective-permute-done((f32[104,128]{1,0:T(8,128)S(1)}, f32[104,128]{1,0:T(8,128)S(1)}, u32[]{:S(2)}, u32[]{:S(2)}) %collective-permute-start.5) | collective-permute-done | bytes 53280 | tf_op jit(solution)/shard_map/ppermute | solution.py:497
  42.3 2.0 %two_steps.1 = (f32[2,104,128]{2,1,0:T(8,128)S(1)}, f32[32,32,128]{2,1,0:T(8,128)S(1)}, f32[32,32,128]{2,1,0:T(8,128)S(1)}, f32[32,32,128]{2,1,0:T(8,128)S(1)}, ...) custom-call(f32[32,32,128]{2,1,0:T(8,128)S(1)} %copy-done, ...), custom_call_target="tpu_custom_call" | custom-call | bytes 9000000 | tf_op jit(solution)/shard_map/two_steps/pallas_call | solution.py:522
  44.4 1.9 %collective-permute-start.6 = (f32[80,128]{1,0:T(8,128)S(1)}, f32[80,128]{1,0:T(8,128)S(1)}, u32[]{:S(2)}, u32[]{:S(2)}) collective-permute-start(f32[80,128]{1,0:T(8,128)S(1)} %get-tuple-element.60), channel_id=1, source_target_pairs={{0,1},{1,0},{2,3},{3,2},{4,5},{5,4},{6,7},{7,6},{8,9},{9,8},{10,11... | collective-permute-start | bytes 122888 | tf_op jit(solution)/shard_map/ppermute | solution.py:497
  46.3 2.2 %collective-permute-start.7 = (f32[80,128]{1,0:T(8,128)S(1)}, f32[80,128]{1,0:T(8,128)S(1)}, u32[]{:S(2)}, u32[]{:S(2)}) collective-permute-start(f32[80,128]{1,0:T(8,128)S(1)} %get-tuple-element.61), channel_id=1, source_target_pairs={{1,2},{2,1},{5,6},{6,5},{9,10},{10,9},{13,14},{14,13},{17,18},{18,... | collective-permute-start | bytes 122888 | tf_op jit(solution)/shard_map/ppermute | solution.py:497
  48.5 1.9 %block_2.1 = (f32[32,32,128]{2,1,0:T(8,128)S(1)}, f32[2,32,128]{2,1,0:T(8,128)S(1)}, f32[2,64,128]{2,1,0:T(8,128)S(1)}) custom-call(f32[6,32,32,128]{3,2,1,0:T(8,128)S(1)} %get-tuple-element.38.g, f32[32,32,128]{2,1,0:T(8,128)S(1)} %get-tuple-element.53.s1, f32[32,32,128]{2,1,0:T(8,128)S(1)} %get-tuple-element.54.d.d1), custom_call_target="tpu_custom_call" | custom-call | bytes 4500000 | tf_op jit(solution)/shard_map/block_2/pallas_call | solution.py:527
  50.4 1.8 %collective-permute-done.7.zodd = f32[80,128]{1,0:T(8,128)S(1)} collective-permute-done((f32[80,128]{1,0:T(8,128)S(1)}, f32[80,128]{1,0:T(8,128)S(1)}, u32[]{:S(2)}, u32[]{:S(2)}) %collective-permute-start.7) | collective-permute-done | bytes 40992 | tf_op jit(solution)/shard_map/ppermute | solution.py:497
  52.3 1.9 %collective-permute-start.8 = (f32[48,128]{1,0:T(8,128)S(1)}, f32[48,128]{1,0:T(8,128)S(1)}, u32[]{:S(2)}, u32[]{:S(2)}) collective-permute-start(f32[48,128]{1,0:T(8,128)S(1)} %get-tuple-element.64), channel_id=1, source_target_pairs={{0,4},{4,0},{8,12},{12,8},{16,20},{20,16},{24,28},{28,24},{32,36},... | collective-permute-start | bytes 73736 | tf_op jit(solution)/shard_map/ppermute | solution.py:497
  54.2 6.8 %collective-permute-start.9 = (f32[48,128]{1,0:T(8,128)S(1)}, f32[48,128]{1,0:T(8,128)S(1)}, u32[]{:S(2)}, u32[]{:S(2)}) collective-permute-start(f32[48,128]{1,0:T(8,128)S(1)} %get-tuple-element.65), channel_id=1, source_target_pairs={{4,8},{8,4},{12,16},{16,12},{20,24},{24,20},{28,32},{32,28},{36,40... | collective-permute-start | bytes 73736 | tf_op jit(solution)/shard_map/ppermute | solution.py:497
  61.1 1.5 %collective-permute-done.9.yodd = f32[48,128]{1,0:T(8,128)S(1)} collective-permute-done((f32[48,128]{1,0:T(8,128)S(1)}, f32[48,128]{1,0:T(8,128)S(1)}, u32[]{:S(2)}, u32[]{:S(2)}) %collective-permute-start.9) | collective-permute-done | bytes 24608 | tf_op jit(solution)/shard_map/ppermute | solution.py:497
  62.6 0.2 x_message_2.1
  62.7 1.9 %collective-permute-start.10 = (f32[88,128]{1,0:T(8,128)S(1)}, f32[88,128]{1,0:T(8,128)S(1)}, u32[]{:S(2)}, u32[]{:S(2)}) collective-permute-start(f32[88,128]{1,0:T(8,128)S(1)} %get-tuple-element.69), channel_id=1, source_target_pairs={{0,64},{64,0},{128,192},{192,128},{256,320},{320,256},{384,448},{4... | collective-permute-start | bytes 135176 | tf_op jit(solution)/shard_map/ppermute | solution.py:497
  64.7 3.8 %collective-permute-start.11 = (f32[88,128]{1,0:T(8,128)S(1)}, f32[88,128]{1,0:T(8,128)S(1)}, u32[]{:S(2)}, u32[]{:S(2)}) collective-permute-start(f32[88,128]{1,0:T(8,128)S(1)} %get-tuple-element.70), channel_id=1, source_target_pairs={{64,128},{128,64},{192,256},{256,192},{320,384},{384,320},{448,512... | collective-permute-start | bytes 135176 | tf_op jit(solution)/shard_map/ppermute | solution.py:497
  68.5 0.2 collective-permute-done.10.xeven
  68.7 17.6 %collective-permute-done.11.xodd = f32[88,128]{1,0:T(8,128)S(1)} collective-permute-done((f32[88,128]{1,0:T(8,128)S(1)}, f32[88,128]{1,0:T(8,128)S(1)}, u32[]{:S(2)}, u32[]{:S(2)}) %collective-permute-start.11) | collective-permute-done | bytes 45088 | tf_op jit(solution)/shard_map/ppermute | solution.py:497
  86.3 2.7 %last_steps.1 = f32[32,32,128]{2,1,0:T(8,128)} custom-call(f32[6,32,32,128]{3,2,1,0:T(8,128)S(1)} %get-tuple-element.38.g, f32[32,32,128]{2,1,0:T(8,128)S(1)} %get-tuple-element.55.s2, f32[32,32,128]{2,1,0:T(8,128)S(1)} %get-tuple-element.54.d.d1, f32[32,32,128]{2,1,0:T(8,128)S(1)} %get-tuple-element.56.acc, f32[2,32,128]{2,1,0:T(8,128)S(1)} %get-tuple-element.42.gzf, ...), custom_call_target="tpu_custom_call" | custom-call | bytes 9000000 | tf_op jit(solution)/shard_map/last_steps/pallas_call | solution.py:539
  (11 shorter events, 0.4 us)
Async XLA Ops:
  0.0 42.3 %copy-start = (f32[32,32,128]{2,1,0:T(8,128)S(1)}, f32[32,32,128]{2,1,0:T(8,128)}, u32[]{:S(2)}) copy-start(f32[32,32,128]{2,1,0:T(8,128)} %u.3) | copy-start | bytes 1572868
  1.2 10.5 %collective-permute-start = (f32[136,128]{1,0:T(8,128)S(1)}, f32[136,128]{1,0:T(8,128)S(1)}, u32[]{:S(2)}, u32[]{:S(2)}) collective-permute-start(f32[136,128]{1,0:T(8,128)S(1)} %get-tuple-element.45), channel_id=1, source_target_pairs={{0,1},{1,0},{2,3},{3,2},{4,5},{5,4},{6,7},{7,6},{8,9},{9,8},{10,11... | collective-permute-start | bytes 208904 | tf_op jit(solution)/shard_map/ppermute | solution.py:497
  3.6 8.1 %collective-permute-start.1 = (f32[136,128]{1,0:T(8,128)S(1)}, f32[136,128]{1,0:T(8,128)S(1)}, u32[]{:S(2)}, u32[]{:S(2)}) collective-permute-start(f32[136,128]{1,0:T(8,128)S(1)} %get-tuple-element.46), channel_id=1, source_target_pairs={{1,2},{2,1},{5,6},{6,5},{9,10},{10,9},{13,14},{14,13},{17,18},{18,... | collective-permute-start | bytes 208904 | tf_op jit(solution)/shard_map/ppermute | solution.py:497
  11.8 6.2 %collective-permute-start.2 = (f32[40,128]{1,0:T(8,128)S(1)}, f32[40,128]{1,0:T(8,128)S(1)}, u32[]{:S(2)}, u32[]{:S(2)}) collective-permute-start(f32[40,128]{1,0:T(8,128)S(1)} %get-tuple-element.48), channel_id=1, source_target_pairs={{0,4},{4,0},{8,12},{12,8},{16,20},{20,16},{24,28},{28,24},{32,36},... | collective-permute-start | bytes 61448 | tf_op jit(solution)/shard_map/ppermute | solution.py:497
  13.8 6.3 %collective-permute-start.3 = (f32[40,128]{1,0:T(8,128)S(1)}, f32[40,128]{1,0:T(8,128)S(1)}, u32[]{:S(2)}, u32[]{:S(2)}) collective-permute-start(f32[40,128]{1,0:T(8,128)S(1)} %get-tuple-element.49), channel_id=1, source_target_pairs={{4,8},{8,4},{12,16},{16,12},{20,24},{24,20},{28,32},{32,28},{36,40... | collective-permute-start | bytes 61448 | tf_op jit(solution)/shard_map/ppermute | solution.py:497
  20.2 8.8 %collective-permute-start.4 = (f32[104,128]{1,0:T(8,128)S(1)}, f32[104,128]{1,0:T(8,128)S(1)}, u32[]{:S(2)}, u32[]{:S(2)}) collective-permute-start(f32[104,128]{1,0:T(8,128)S(1)} %get-tuple-element.51), channel_id=1, source_target_pairs={{0,64},{64,0},{128,192},{192,128},{256,320},{320,256},{384,448},{4... | collective-permute-start | bytes 159752 | tf_op jit(solution)/shard_map/ppermute | solution.py:497
  23.7 18.6 %collective-permute-start.5 = (f32[104,128]{1,0:T(8,128)S(1)}, f32[104,128]{1,0:T(8,128)S(1)}, u32[]{:S(2)}, u32[]{:S(2)}) collective-permute-start(f32[104,128]{1,0:T(8,128)S(1)} %get-tuple-element.52), channel_id=1, source_target_pairs={{64,128},{128,64},{192,256},{256,192},{320,384},{384,320},{448,512... | collective-permute-start | bytes 159752 | tf_op jit(solution)/shard_map/ppermute | solution.py:497
  44.4 6.1 %collective-permute-start.6 = (f32[80,128]{1,0:T(8,128)S(1)}, f32[80,128]{1,0:T(8,128)S(1)}, u32[]{:S(2)}, u32[]{:S(2)}) collective-permute-start(f32[80,128]{1,0:T(8,128)S(1)} %get-tuple-element.60), channel_id=1, source_target_pairs={{0,1},{1,0},{2,3},{3,2},{4,5},{5,4},{6,7},{7,6},{8,9},{9,8},{10,11... | collective-permute-start | bytes 122888 | tf_op jit(solution)/shard_map/ppermute | solution.py:497
  46.3 5.9 %collective-permute-start.7 = (f32[80,128]{1,0:T(8,128)S(1)}, f32[80,128]{1,0:T(8,128)S(1)}, u32[]{:S(2)}, u32[]{:S(2)}) collective-permute-start(f32[80,128]{1,0:T(8,128)S(1)} %get-tuple-element.61), channel_id=1, source_target_pairs={{1,2},{2,1},{5,6},{6,5},{9,10},{10,9},{13,14},{14,13},{17,18},{18,... | collective-permute-start | bytes 122888 | tf_op jit(solution)/shard_map/ppermute | solution.py:497
  52.3 8.8 %collective-permute-start.8 = (f32[48,128]{1,0:T(8,128)S(1)}, f32[48,128]{1,0:T(8,128)S(1)}, u32[]{:S(2)}, u32[]{:S(2)}) collective-permute-start(f32[48,128]{1,0:T(8,128)S(1)} %get-tuple-element.64), channel_id=1, source_target_pairs={{0,4},{4,0},{8,12},{12,8},{16,20},{20,16},{24,28},{28,24},{32,36},... | collective-permute-start | bytes 73736 | tf_op jit(solution)/shard_map/ppermute | solution.py:497
  54.2 8.3 %collective-permute-start.9 = (f32[48,128]{1,0:T(8,128)S(1)}, f32[48,128]{1,0:T(8,128)S(1)}, u32[]{:S(2)}, u32[]{:S(2)}) collective-permute-start(f32[48,128]{1,0:T(8,128)S(1)} %get-tuple-element.65), channel_id=1, source_target_pairs={{4,8},{8,4},{12,16},{16,12},{20,24},{24,20},{28,32},{32,28},{36,40... | collective-permute-start | bytes 73736 | tf_op jit(solution)/shard_map/ppermute | solution.py:497
  62.7 5.9 %collective-permute-start.10 = (f32[88,128]{1,0:T(8,128)S(1)}, f32[88,128]{1,0:T(8,128)S(1)}, u32[]{:S(2)}, u32[]{:S(2)}) collective-permute-start(f32[88,128]{1,0:T(8,128)S(1)} %get-tuple-element.69), channel_id=1, source_target_pairs={{0,64},{64,0},{128,192},{192,128},{256,320},{320,256},{384,448},{4... | collective-permute-start | bytes 135176 | tf_op jit(solution)/shard_map/ppermute | solution.py:497
  64.7 21.6 %collective-permute-start.11 = (f32[88,128]{1,0:T(8,128)S(1)}, f32[88,128]{1,0:T(8,128)S(1)}, u32[]{:S(2)}, u32[]{:S(2)}) collective-permute-start(f32[88,128]{1,0:T(8,128)S(1)} %get-tuple-element.70), channel_id=1, source_target_pairs={{64,128},{128,64},{192,256},{256,192},{320,384},{384,320},{448,512... | collective-permute-start | bytes 135176 | tf_op jit(solution)/shard_map/ppermute | solution.py:497

commit v3 on v2

--- a/solution.py
+++ b/solution.py
@@ -230,7 +230,7 @@
     return [shift_lanes(yp[side, 0:NX, :], 64) for side in (0, 1)]
 
 
-def first_x_kernel(yeven, yodd, gzf, yp, xp, zh, yh, even, odd, stage):
+def first_x_kernel(yodd, yeven, gzf, yp, xp, zh, yh, even, odd, stage):
     take_in(yh, yeven, yodd, "gy")
     gy = y_couplings(yp)
     for side in (0, 1):
@@ -272,7 +272,7 @@
 
 
 def second_kernel(
-    u, g, diag, s1, perm_sum, gzf, yp, xp, zh, yh, xeven, xodd,
+    u, g, diag, s1, perm_sum, gzf, yp, xp, zh, yh, xodd, xeven,
     xh, s, d, acc, b, even, odd,
     s0, d0, cross, cross2, rsum, rows, stage,
 ):
@@ -363,7 +363,7 @@
     put_out(stage, even, odd, "gy")
 
 
-def second_x_kernel(yeven, yodd, gzf, yp, xp2, b3, zh2, yh2, even, odd, bw, stage):
+def second_x_kernel(yodd, yeven, gzf, yp, xp2, b3, zh2, yh2, even, odd, bw, stage):
     take_in(yh2, yeven, yodd, "gy")
     gy = y_couplings(yp)
     within = lax.rem(iota((16, NY), 1), 32)
@@ -432,7 +432,7 @@
 
 
 def third_kernel(
-    g, s2, d1, acc, gzf, yp, xp, zh, yh, xh, yp2, xp2, zh2, yh2, bw, xeven, xodd,
+    g, s2, d1, acc, gzf, yp, xp, zh, yh, xh, yp2, xp2, zh2, yh2, bw, xodd, xeven,
     out,
     xh2, s, d, cross, cross2, ext, err, spread,
 ):
@@ -517,13 +517,13 @@
     even, odd = swap(even, odd, "gy")
     yh, even, odd = call(
         first_x_kernel, "x_message", 6, [(2, YM1, NY), (XM1, NY), (XM1, NY)], [(2, XM1, NY)]
-    )(even, odd, gzf, yp, xp, zh)
+    )(odd, even, gzf, yp, xp, zh)
     even, odd = swap(even, odd, "gx")
     xh, s, d1, acc, b, even, odd = call(
         second_kernel, "two_steps", 12,
         [(2, XM1, NY), FULL, FULL, FULL, (16, NY), (ZM2, NY), (ZM2, NY)],
         [FULL, FULL, face, face, (4, NX, NY), (2, 16, NY), (2, ZM2, NY)], 3.0,
-    )(u, g, diag, s, perm_sum, gzf, yp, xp, zh, yh, even, odd)
+    )(u, g, diag, s, perm_sum, gzf, yp, xp, zh, yh, odd, even)
     s, yp2, xp2 = call(
         partial_kernel, "block_2", 3, [FULL, (2, NX, NY), (2, 64, NY)], [], 1.5
     )(g, s, d1)
@@ -534,12 +534,12 @@
     even, odd = swap(even, odd, "gy")
     yh2, even, odd, bw = call(
         second_x_kernel, "x_message_2", 7, [(2, YM2, NY), (XM2, NY), (XM2, NY), (16, NY)], [(2, XM2, NY)]
-    )(even, odd, gzf, yp, xp2, b3, zh2)
+    )(odd, even, gzf, yp, xp2, b3, zh2)
     even, odd = swap(even, odd, "gx")
     (out,) = call(
         third_kernel, "last_steps", 17, [FULL],
         [(2, XM2, NY), FULL, FULL, face, face, (10, 16, NY), (16, NY), (4, NX, NY)], 3.0,
-    )(g, s, d1, acc, gzf, yp, xp, zh, yh, xh, yp2, xp2, zh2, yh2, bw, even, odd)
+    )(g, s, d1, acc, gzf, yp, xp, zh, yh, xh, yp2, xp2, zh2, yh2, bw, odd, even)
     return out
 
 

time: 89.4 us -> 84.6 us (0.946)
  the two profiles are of different devices: /device:TPU:642 before, /device:TPU:283 now
where the time goes in v3:
time: 84.6 us; the launch traced here: 84.1 us
  starting transfers between devices  56.7 us (67%)
  waiting for transfers between devices  14.8 us (17%)
  Pallas kernels  12.4 us (15%)
    ppermute x12, starting transfers between devices, swap(): results.append(lax.ppermute(values, axis, pairs))  56.7 us
    ppermute x12, waiting for transfers between devices, swap(): results.append(lax.ppermute(values, axis, pairs))  14.8 us
    pallas_call x1, Pallas kernels, per_device(): call(first_kernel, 'block', 4, [(6,) + FULL, FULL, FULL, (4, NX, NY), (2,...  3.98 us
    pallas_call x1, Pallas kernels, per_device(): call(third_kernel, 'last_steps', 17, [FULL], [(2, XM2, NY), FULL, FULL, f...  2.7 us
    pallas_call x1, Pallas kernels, per_device(): call(second_kernel, 'two_steps', 12, [(2, XM1, NY), FULL, FULL, FULL, (16...  2.01 us
    pallas_call x1, Pallas kernels, per_device(): call(partial_kernel, 'block_2', 3, [FULL, (2, NX, NY), (2, 64, NY)], [],...  1.92 us
  transfers between devices with their start and end apart: 12, of which 5 were waited for; matrix products, arithmetic and copies ran while one was open for 0% of the time, Pallas kernels for 7%

profile of v3, /device:TPU:283, one launch (start us, length us, event | category | flops | bytes accessed | tf_op | source)
XLA Modules:
  0.0 84.1 jit_solution(8033786048422991213)
XLA Ops:
  0.0 1.2 %z_faces.1 = (f32[2,32,128]{2,1,0:T(8,128)S(1)}, f32[136,128]{1,0:T(8,128)S(1)}, f32[136,128]{1,0:T(8,128)S(1)}) custom-call(f32[32,32,128]{2,1,0:T(8,128)} %u.3, f32[32,32,128]{2,1,0:T(8,128)} %f.1, f32[32,32,128]{2,1,0:T(8,128)} %p.1, bf16[3,32,32,128]{3,2,1,0:T(8,128)(2,1)} %w.1), custom_call_target="tpu_custom_call" | custom-call | bytes 3000000 | tf_op jit(solution)/shard_map/z_faces/pallas_call | solution.py:504
  1.2 2.2 %collective-permute-start = (f32[136,128]{1,0:T(8,128)S(1)}, f32[136,128]{1,0:T(8,128)S(1)}, u32[]{:S(2)}, u32[]{:S(2)}) collective-permute-start(f32[136,128]{1,0:T(8,128)S(1)} %get-tuple-element.45), channel_id=1, source_target_pairs={{0,1},{1,0},{2,3},{3,2},{4,5},{5,4},{6,7},{7,6},{8,9},{9,8},{10,11... | collective-permute-start | bytes 208904 | tf_op jit(solution)/shard_map/ppermute | solution.py:497
  3.3 3.8 %collective-permute-start.1 = (f32[136,128]{1,0:T(8,128)S(1)}, f32[136,128]{1,0:T(8,128)S(1)}, u32[]{:S(2)}, u32[]{:S(2)}) collective-permute-start(f32[136,128]{1,0:T(8,128)S(1)} %get-tuple-element.46), channel_id=1, source_target_pairs={{1,2},{2,1},{5,6},{6,5},{9,10},{10,9},{13,14},{14,13},{17,18},{18,... | collective-permute-start | bytes 208904 | tf_op jit(solution)/shard_map/ppermute | solution.py:497
  7.1 4.0 %block.1 = (f32[6,32,32,128]{3,2,1,0:T(8,128)S(1)}, f32[32,32,128]{2,1,0:T(8,128)S(1)}, f32[32,32,128]{2,1,0:T(8,128)S(1)}, f32[4,32,128]{2,1,0:T(8,128)S(1)}, f...) custom-call(f32[32,32,128]{2,1,0:T(8,128)} %u.3, f32[32,32,128]{2,1,0:T(8,128)} %f.1, f32[32,32,128]{2,1,0:T(8,128)} %p.1, ...), custom_call_target="tpu_custom_call" | custom-call | bytes 9000000 | tf_op jit(solution)/shard_map/block/pallas_call | solution.py:508
  11.3 4.7 %collective-permute-start.2 = (f32[40,128]{1,0:T(8,128)S(1)}, f32[40,128]{1,0:T(8,128)S(1)}, u32[]{:S(2)}, u32[]{:S(2)}) collective-permute-start(f32[40,128]{1,0:T(8,128)S(1)} %get-tuple-element.48), channel_id=1, source_target_pairs={{4,8},{8,4},{12,16},{16,12},{20,24},{24,20},{28,32},{32,28},{36,40... | collective-permute-start | bytes 61448 | tf_op jit(solution)/shard_map/ppermute | solution.py:497
  15.9 1.9 %collective-permute-start.3 = (f32[40,128]{1,0:T(8,128)S(1)}, f32[40,128]{1,0:T(8,128)S(1)}, u32[]{:S(2)}, u32[]{:S(2)}) collective-permute-start(f32[40,128]{1,0:T(8,128)S(1)} %get-tuple-element.49), channel_id=1, source_target_pairs={{0,4},{4,0},{8,12},{12,8},{16,20},{20,16},{24,28},{28,24},{32,36},... | collective-permute-start | bytes 61448 | tf_op jit(solution)/shard_map/ppermute | solution.py:497
  17.9 1.1 %collective-permute-done.3.yeven = f32[40,128]{1,0:T(8,128)S(1)} collective-permute-done((f32[40,128]{1,0:T(8,128)S(1)}, f32[40,128]{1,0:T(8,128)S(1)}, u32[]{:S(2)}, u32[]{:S(2)}) %collective-permute-start.3) | collective-permute-done | bytes 20512 | tf_op jit(solution)/shard_map/ppermute | solution.py:497
  19.0 0.2 x_message.1
  19.2 14.2 %collective-permute-start.4 = (f32[104,128]{1,0:T(8,128)S(1)}, f32[104,128]{1,0:T(8,128)S(1)}, u32[]{:S(2)}, u32[]{:S(2)}) collective-permute-start(f32[104,128]{1,0:T(8,128)S(1)} %get-tuple-element.51), channel_id=1, source_target_pairs={{64,128},{128,64},{192,256},{256,192},{320,384},{384,320},{448,512... | collective-permute-start | bytes 159752 | tf_op jit(solution)/shard_map/ppermute | solution.py:497
  33.4 1.9 %collective-permute-start.5 = (f32[104,128]{1,0:T(8,128)S(1)}, f32[104,128]{1,0:T(8,128)S(1)}, u32[]{:S(2)}, u32[]{:S(2)}) collective-permute-start(f32[104,128]{1,0:T(8,128)S(1)} %get-tuple-element.52), channel_id=1, source_target_pairs={{0,64},{64,0},{128,192},{192,128},{256,320},{320,256},{384,448},{4... | collective-permute-start | bytes 159752 | tf_op jit(solution)/shard_map/ppermute | solution.py:497
  35.3 6.1 %collective-permute-done.4.xodd = f32[104,128]{1,0:T(8,128)S(1)} collective-permute-done((f32[104,128]{1,0:T(8,128)S(1)}, f32[104,128]{1,0:T(8,128)S(1)}, u32[]{:S(2)}, u32[]{:S(2)}) %collective-permute-start.4) | collective-permute-done | bytes 53280 | tf_op jit(solution)/shard_map/ppermute | solution.py:497
  41.4 2.0 %two_steps.1 = (f32[2,104,128]{2,1,0:T(8,128)S(1)}, f32[32,32,128]{2,1,0:T(8,128)S(1)}, f32[32,32,128]{2,1,0:T(8,128)S(1)}, f32[32,32,128]{2,1,0:T(8,128)S(1)}, ...) custom-call(f32[32,32,128]{2,1,0:T(8,128)S(1)} %copy-done, ...), custom_call_target="tpu_custom_call" | custom-call | bytes 9000000 | tf_op jit(solution)/shard_map/two_steps/pallas_call | solution.py:522
  43.4 1.9 %collective-permute-start.6 = (f32[80,128]{1,0:T(8,128)S(1)}, f32[80,128]{1,0:T(8,128)S(1)}, u32[]{:S(2)}, u32[]{:S(2)}) collective-permute-start(f32[80,128]{1,0:T(8,128)S(1)} %get-tuple-element.60), channel_id=1, source_target_pairs={{0,1},{1,0},{2,3},{3,2},{4,5},{5,4},{6,7},{7,6},{8,9},{9,8},{10,11... | collective-permute-start | bytes 122888 | tf_op jit(solution)/shard_map/ppermute | solution.py:497
  45.3 1.9 %collective-permute-start.7 = (f32[80,128]{1,0:T(8,128)S(1)}, f32[80,128]{1,0:T(8,128)S(1)}, u32[]{:S(2)}, u32[]{:S(2)}) collective-permute-start(f32[80,128]{1,0:T(8,128)S(1)} %get-tuple-element.61), channel_id=1, source_target_pairs={{1,2},{2,1},{5,6},{6,5},{9,10},{10,9},{13,14},{14,13},{17,18},{18,... | collective-permute-start | bytes 122888 | tf_op jit(solution)/shard_map/ppermute | solution.py:497
  47.3 1.9 %block_2.1 = (f32[32,32,128]{2,1,0:T(8,128)S(1)}, f32[2,32,128]{2,1,0:T(8,128)S(1)}, f32[2,64,128]{2,1,0:T(8,128)S(1)}) custom-call(f32[6,32,32,128]{3,2,1,0:T(8,128)S(1)} %get-tuple-element.38.g, f32[32,32,128]{2,1,0:T(8,128)S(1)} %get-tuple-element.53.s1, f32[32,32,128]{2,1,0:T(8,128)S(1)} %get-tuple-element.54.d.d1), custom_call_target="tpu_custom_call" | custom-call | bytes 4500000 | tf_op jit(solution)/shard_map/block_2/pallas_call | solution.py:527
  49.2 0.9 %collective-permute-done.7.zodd = f32[80,128]{1,0:T(8,128)S(1)} collective-permute-done((f32[80,128]{1,0:T(8,128)S(1)}, f32[80,128]{1,0:T(8,128)S(1)}, u32[]{:S(2)}, u32[]{:S(2)}) %collective-permute-start.7) | collective-permute-done | bytes 40992 | tf_op jit(solution)/shard_map/ppermute | solution.py:497
  50.2 5.5 %collective-permute-start.8 = (f32[48,128]{1,0:T(8,128)S(1)}, f32[48,128]{1,0:T(8,128)S(1)}, u32[]{:S(2)}, u32[]{:S(2)}) collective-permute-start(f32[48,128]{1,0:T(8,128)S(1)} %get-tuple-element.64), channel_id=1, source_target_pairs={{4,8},{8,4},{12,16},{16,12},{20,24},{24,20},{28,32},{32,28},{36,40... | collective-permute-start | bytes 73736 | tf_op jit(solution)/shard_map/ppermute | solution.py:497
  55.7 1.9 %collective-permute-start.9 = (f32[48,128]{1,0:T(8,128)S(1)}, f32[48,128]{1,0:T(8,128)S(1)}, u32[]{:S(2)}, u32[]{:S(2)}) collective-permute-start(f32[48,128]{1,0:T(8,128)S(1)} %get-tuple-element.65), channel_id=1, source_target_pairs={{0,4},{4,0},{8,12},{12,8},{16,20},{20,16},{24,28},{28,24},{32,36},... | collective-permute-start | bytes 73736 | tf_op jit(solution)/shard_map/ppermute | solution.py:497
  57.6 1.2 %collective-permute-done.9.yeven = f32[48,128]{1,0:T(8,128)S(1)} collective-permute-done((f32[48,128]{1,0:T(8,128)S(1)}, f32[48,128]{1,0:T(8,128)S(1)}, u32[]{:S(2)}, u32[]{:S(2)}) %collective-permute-start.9) | collective-permute-done | bytes 24608 | tf_op jit(solution)/shard_map/ppermute | solution.py:497
  58.8 0.2 x_message_2.1
  59.0 14.9 %collective-permute-start.10 = (f32[88,128]{1,0:T(8,128)S(1)}, f32[88,128]{1,0:T(8,128)S(1)}, u32[]{:S(2)}, u32[]{:S(2)}) collective-permute-start(f32[88,128]{1,0:T(8,128)S(1)} %get-tuple-element.69), channel_id=1, source_target_pairs={{64,128},{128,64},{192,256},{256,192},{320,384},{384,320},{448,512... | collective-permute-start | bytes 135176 | tf_op jit(solution)/shard_map/ppermute | solution.py:497
  73.9 1.9 %collective-permute-start.11 = (f32[88,128]{1,0:T(8,128)S(1)}, f32[88,128]{1,0:T(8,128)S(1)}, u32[]{:S(2)}, u32[]{:S(2)}) collective-permute-start(f32[88,128]{1,0:T(8,128)S(1)} %get-tuple-element.70), channel_id=1, source_target_pairs={{0,64},{64,0},{128,192},{192,128},{256,320},{320,256},{384,448},{4... | collective-permute-start | bytes 135176 | tf_op jit(solution)/shard_map/ppermute | solution.py:497
  75.8 5.6 %collective-permute-done.10.xodd = f32[88,128]{1,0:T(8,128)S(1)} collective-permute-done((f32[88,128]{1,0:T(8,128)S(1)}, f32[88,128]{1,0:T(8,128)S(1)}, u32[]{:S(2)}, u32[]{:S(2)}) %collective-permute-start.10) | collective-permute-done | bytes 45088 | tf_op jit(solution)/shard_map/ppermute | solution.py:497
  81.4 2.7 %last_steps.1 = f32[32,32,128]{2,1,0:T(8,128)} custom-call(f32[6,32,32,128]{3,2,1,0:T(8,128)S(1)} %get-tuple-element.38.g, f32[32,32,128]{2,1,0:T(8,128)S(1)} %get-tuple-element.55.s2, f32[32,32,128]{2,1,0:T(8,128)S(1)} %get-tuple-element.54.d.d1, f32[32,32,128]{2,1,0:T(8,128)S(1)} %get-tuple-element.56.acc, f32[2,32,128]{2,1,0:T(8,128)S(1)} %get-tuple-element.42.gzf, ...), custom_call_target="tpu_custom_call" | custom-call | bytes 9000000 | tf_op jit(solution)/shard_map/last_steps/pallas_call | solution.py:539
  (11 shorter events, 0.3 us)
Async XLA Ops:
  0.0 41.4 %copy-start = (f32[32,32,128]{2,1,0:T(8,128)S(1)}, f32[32,32,128]{2,1,0:T(8,128)}, u32[]{:S(2)}) copy-start(f32[32,32,128]{2,1,0:T(8,128)} %u.3) | copy-start | bytes 1572868
  1.2 10.0 %collective-permute-start = (f32[136,128]{1,0:T(8,128)S(1)}, f32[136,128]{1,0:T(8,128)S(1)}, u32[]{:S(2)}, u32[]{:S(2)}) collective-permute-start(f32[136,128]{1,0:T(8,128)S(1)} %get-tuple-element.45), channel_id=1, source_target_pairs={{0,1},{1,0},{2,3},{3,2},{4,5},{5,4},{6,7},{7,6},{8,9},{9,8},{10,11... | collective-permute-start | bytes 208904 | tf_op jit(solution)/shard_map/ppermute | solution.py:497
  3.3 7.8 %collective-permute-start.1 = (f32[136,128]{1,0:T(8,128)S(1)}, f32[136,128]{1,0:T(8,128)S(1)}, u32[]{:S(2)}, u32[]{:S(2)}) collective-permute-start(f32[136,128]{1,0:T(8,128)S(1)} %get-tuple-element.46), channel_id=1, source_target_pairs={{1,2},{2,1},{5,6},{6,5},{9,10},{10,9},{13,14},{14,13},{17,18},{18,... | collective-permute-start | bytes 208904 | tf_op jit(solution)/shard_map/ppermute | solution.py:497
  11.3 6.6 %collective-permute-start.2 = (f32[40,128]{1,0:T(8,128)S(1)}, f32[40,128]{1,0:T(8,128)S(1)}, u32[]{:S(2)}, u32[]{:S(2)}) collective-permute-start(f32[40,128]{1,0:T(8,128)S(1)} %get-tuple-element.48), channel_id=1, source_target_pairs={{4,8},{8,4},{12,16},{16,12},{20,24},{24,20},{28,32},{32,28},{36,40... | collective-permute-start | bytes 61448 | tf_op jit(solution)/shard_map/ppermute | solution.py:497
  15.9 3.1 %collective-permute-start.3 = (f32[40,128]{1,0:T(8,128)S(1)}, f32[40,128]{1,0:T(8,128)S(1)}, u32[]{:S(2)}, u32[]{:S(2)}) collective-permute-start(f32[40,128]{1,0:T(8,128)S(1)} %get-tuple-element.49), channel_id=1, source_target_pairs={{0,4},{4,0},{8,12},{12,8},{16,20},{20,16},{24,28},{28,24},{32,36},... | collective-permute-start | bytes 61448 | tf_op jit(solution)/shard_map/ppermute | solution.py:497
  19.2 22.2 %collective-permute-start.4 = (f32[104,128]{1,0:T(8,128)S(1)}, f32[104,128]{1,0:T(8,128)S(1)}, u32[]{:S(2)}, u32[]{:S(2)}) collective-permute-start(f32[104,128]{1,0:T(8,128)S(1)} %get-tuple-element.51), channel_id=1, source_target_pairs={{64,128},{128,64},{192,256},{256,192},{320,384},{384,320},{448,512... | collective-permute-start | bytes 159752 | tf_op jit(solution)/shard_map/ppermute | solution.py:497
  33.4 8.0 %collective-permute-start.5 = (f32[104,128]{1,0:T(8,128)S(1)}, f32[104,128]{1,0:T(8,128)S(1)}, u32[]{:S(2)}, u32[]{:S(2)}) collective-permute-start(f32[104,128]{1,0:T(8,128)S(1)} %get-tuple-element.52), channel_id=1, source_target_pairs={{0,64},{64,0},{128,192},{192,128},{256,320},{320,256},{384,448},{4... | collective-permute-start | bytes 159752 | tf_op jit(solution)/shard_map/ppermute | solution.py:497
  43.4 5.8 %collective-permute-start.6 = (f32[80,128]{1,0:T(8,128)S(1)}, f32[80,128]{1,0:T(8,128)S(1)}, u32[]{:S(2)}, u32[]{:S(2)}) collective-permute-start(f32[80,128]{1,0:T(8,128)S(1)} %get-tuple-element.60), channel_id=1, source_target_pairs={{0,1},{1,0},{2,3},{3,2},{4,5},{5,4},{6,7},{7,6},{8,9},{9,8},{10,11... | collective-permute-start | bytes 122888 | tf_op jit(solution)/shard_map/ppermute | solution.py:497
  45.3 4.7 %collective-permute-start.7 = (f32[80,128]{1,0:T(8,128)S(1)}, f32[80,128]{1,0:T(8,128)S(1)}, u32[]{:S(2)}, u32[]{:S(2)}) collective-permute-start(f32[80,128]{1,0:T(8,128)S(1)} %get-tuple-element.61), channel_id=1, source_target_pairs={{1,2},{2,1},{5,6},{6,5},{9,10},{10,9},{13,14},{14,13},{17,18},{18,... | collective-permute-start | bytes 122888 | tf_op jit(solution)/shard_map/ppermute | solution.py:497
  50.2 7.4 %collective-permute-start.8 = (f32[48,128]{1,0:T(8,128)S(1)}, f32[48,128]{1,0:T(8,128)S(1)}, u32[]{:S(2)}, u32[]{:S(2)}) collective-permute-start(f32[48,128]{1,0:T(8,128)S(1)} %get-tuple-element.64), channel_id=1, source_target_pairs={{4,8},{8,4},{12,16},{16,12},{20,24},{24,20},{28,32},{32,28},{36,40... | collective-permute-start | bytes 73736 | tf_op jit(solution)/shard_map/ppermute | solution.py:497
  55.7 3.1 %collective-permute-start.9 = (f32[48,128]{1,0:T(8,128)S(1)}, f32[48,128]{1,0:T(8,128)S(1)}, u32[]{:S(2)}, u32[]{:S(2)}) collective-permute-start(f32[48,128]{1,0:T(8,128)S(1)} %get-tuple-element.65), channel_id=1, source_target_pairs={{0,4},{4,0},{8,12},{12,8},{16,20},{20,16},{24,28},{28,24},{32,36},... | collective-permute-start | bytes 73736 | tf_op jit(solution)/shard_map/ppermute | solution.py:497
  59.0 22.4 %collective-permute-start.10 = (f32[88,128]{1,0:T(8,128)S(1)}, f32[88,128]{1,0:T(8,128)S(1)}, u32[]{:S(2)}, u32[]{:S(2)}) collective-permute-start(f32[88,128]{1,0:T(8,128)S(1)} %get-tuple-element.69), channel_id=1, source_target_pairs={{64,128},{128,64},{192,256},{256,192},{320,384},{384,320},{448,512... | collective-permute-start | bytes 135176 | tf_op jit(solution)/shard_map/ppermute | solution.py:497
  73.9 7.5 %collective-permute-start.11 = (f32[88,128]{1,0:T(8,128)S(1)}, f32[88,128]{1,0:T(8,128)S(1)}, u32[]{:S(2)}, u32[]{:S(2)}) collective-permute-start(f32[88,128]{1,0:T(8,128)S(1)} %get-tuple-element.70), channel_id=1, source_target_pairs={{0,64},{64,0},{128,192},{192,128},{256,320},{320,256},{384,448},{4... | collective-permute-start | bytes 135176 | tf_op jit(solution)/shard_map/ppermute | solution.py:497

commit v4 on v3

v4 whole, which is shorter than its diff:
```python
import jax
import jax.numpy as jnp
from jax import lax
from jax.experimental import pallas as pl
from jax.experimental.pallas import tpu as pltpu
from jax.sharding import PartitionSpec as P

THETA = 1.15
DELTA = 0.85
OMEGA = 0.8
F32 = jnp.float32

NZ, NX, NY = 32, 32, 128
FULL = (NZ, NX, NY)

SIGMA = THETA / DELTA
RHO0 = 1.0 / SIGMA
RHO1 = 1.0 / (2.0 * SIGMA - RHO0)
RHO2 = 1.0 / (2.0 * SIGMA - RHO1)
RHO3 = 1.0 / (2.0 * SIGMA - RHO2)
A = (RHO1 * RHO0, RHO2 * RHO1, RHO3 * RHO2)
B = (2.0 * RHO1 / DELTA, 2.0 * RHO2 / DELTA, 2.0 * RHO3 / DELTA)

XM1 = 104
ZM1 = 136
YM1 = 40
XM2 = 80
ZM2 = 88
YM2 = 56


def iota(shape, dim):
    return lax.broadcasted_iota(jnp.int32, shape, dim)


def plane():
    return iota((NX, NY), 0), iota((NX, NY), 1)


def parity(axis):
    return lax.rem(lax.axis_index(axis), 2)


def put_out(stage, even, odd, axis):
    odd_one = parity(axis)
    even[...] = stage[1 - odd_one]
    odd[...] = stage[odd_one]


def take_in(halo, even, odd, axis):
    odd_one = parity(axis)
    halo[1 - odd_one] = even[...]
    halo[odd_one] = odd[...]


def fourths(shape=(NX, NY)):
    return lax.rem(iota(shape, 1), 4)


def layer_lanes(z, shape=(NX, NY)):
    lane = iota(shape, 1)
    return (lane == 4 * z) | (lane == lax.rem(4 * z + NY - 1, NY))


def ends(lane):
    return (lane == 0) | (lane == NY - 1)


def shift_lanes(x, amount):
    return pltpu.roll(x, amount % NY, 1)


def columns(row_values):
    row, lane = plane()
    wide = jnp.broadcast_to(row_values, (NX, NY))
    low = jnp.sum(jnp.where(lane == 4 * row, wide, 0.0), axis=1, keepdims=True)
    high = jnp.sum(jnp.where(lane == lax.rem(4 * row + NY - 1, NY), wide, 0.0), axis=1, keepdims=True)
    return jnp.where(lane == 0, low, 0.0) + jnp.where(lane == NY - 1, high, 0.0)


def combined_row(values):
    row, lane = plane()
    low = jnp.where(lane == 4 * row, jnp.broadcast_to(values[:, 0:1], (NX, NY)), 0.0)
    high = jnp.where(lane == lax.rem(4 * row + NY - 1, NY), jnp.broadcast_to(values[:, NY - 1 :], (NX, NY)), 0.0)
    return jnp.sum(low + high, axis=0, keepdims=True)


def combine(low, high, q):
    return jnp.where(fourths(low.shape) == 0, shift_lanes(low, -q), shift_lanes(high, -q - 1))


def own_neighbours(field, g, z):
    here = field[z]
    total = g[0, z] * field[jnp.maximum(z - 1, 0)] + g[1, z] * field[jnp.minimum(z + 1, NZ - 1)]
    total += g[2, z] * pltpu.roll(here, 1, 0) + g[3, z] * pltpu.roll(here, NX - 1, 0)
    total += g[4, z] * pltpu.roll(here, 1, 1) + g[5, z] * pltpu.roll(here, NY - 1, 1)
    return total


def from_faces(z, zp, xp, yp):
    row, lane = plane()
    total = jnp.where(ends(lane), pltpu.roll(yp, lax.rem(NY - 4 * z, NY), 1), 0.0)
    total += jnp.where(row == 0, xp[0, pl.ds(z, 1), :], 0.0)
    total += jnp.where(row == NX - 1, xp[1, pl.ds(z, 1), :], 0.0)
    total += jnp.where(z == 0, zp[0], 0.0) + jnp.where(z == NZ - 1, zp[1], 0.0)
    return total


def couplings(perm, speeds):
    total = 6.0 * perm + jnp.abs(speeds[0]) + jnp.abs(speeds[1]) + jnp.abs(speeds[2])
    inverse = 1.0 / total
    pairs = []
    for speed in speeds:
        pairs.append((perm + jnp.maximum(speed, 0.0)) * inverse)
        pairs.append((perm - jnp.minimum(speed, 0.0)) * inverse)
    return total, inverse, pairs


def face_rows(side):
    return (slice(0, 8), 0) if side == 0 else (slice(NX - 8, NX), 7)


def inner_neighbours(field, c, z, side):
    rows, _ = face_rows(side)
    lane = iota((8, NY), 1)
    here = field[z, rows, :]
    total = jnp.where(z == 0, 0.0, c[0]) * field[jnp.maximum(z - 1, 0), rows, :]
    total += jnp.where(z == NZ - 1, 0.0, c[1]) * field[jnp.minimum(z + 1, NZ - 1), rows, :]
    total += c[3 - side] * pltpu.roll(here, 7 if side == 0 else 1, 0)
    total += jnp.where(lane == 0, 0.0, c[4]) * pltpu.roll(here, 1, 1)
    total += jnp.where(lane == NY - 1, 0.0, c[5]) * pltpu.roll(here, NY - 1, 1)
    return total


def face_kernel(u_far, f_far, p_far, w_far, u, f, p, w, xp, even, odd, sems):
    lane8 = iota((8, NY), 1)
    copies = []
    for part in range(4):
        rows = pl.ds(8 * part, 8)
        copies.append([
            pltpu.make_async_copy(u_far.at[rows], u.at[rows], sems.at[part, 0]),
            pltpu.make_async_copy(f_far.at[rows], f.at[rows], sems.at[part, 1]),
            pltpu.make_async_copy(p_far.at[rows], p.at[rows], sems.at[part, 2]),
            pltpu.make_async_copy(w_far.at[:, rows], w.at[:, rows], sems.at[part, 3]),
        ])
    for part in range(4):
        copies[part][0].start()
    for part in range(4):
        for copy in copies[part][1:]:
            copy.start()

    def face(z, side):
        rows, _ = face_rows(side)
        half = slice(0, 16) if side == 0 else slice(NX - 16, NX)
        speeds = [w[k, z, half, :].astype(F32)[8 * side : 8 * side + 8] for k in range(3)]
        return couplings(p[z, rows, :], speeds)

    def layer(z, carry):
        edges = []
        for side in (0, 1):
            rows, r = face_rows(side)
            _, inverse, c = face(z, side)
            here = u[z, rows, :]
            res = f[z, rows, :] * inverse - here + inner_neighbours(u, c, z, side)
            for base, values in ((0, here), (NZ, res), (2 * NZ, c[2 + side])):
                xp[side, pl.ds(base + z, 1), :] = values[r : r + 1]
            merged = pltpu.roll(jnp.where(lane8 == 0, c[4], c[5]), 4 * z, 1)
            edges.append(jnp.where(layer_lanes(z, (8, NY)), merged, carry[side]))
        return tuple(edges)

    edges = (jnp.zeros((8, NY), F32),) * 2
    for part in range(4):
        copies[part][0].wait()
    for part in range(4):
        for copy in copies[part][1:]:
            copy.wait()
        edges = lax.fori_loop(8 * part, 8 * part + 8, layer, edges, unroll=4)
    for side in (0, 1):
        _, r = face_rows(side)
        xp[side, 96:104, :] = jnp.zeros((8, NY), F32)
        for end, z in ((0, 0), (1, NZ - 1)):
            _, _, c = face(z, side)
            xp[side, 96 + end : 97 + end, :] = c[end][r : r + 1]
        xp[side, 98:99, :] = edges[side][r : r + 1]
    put_out(xp, even, odd, "gx")


def block_kernel(u, f, p, w, g, diag, s, perm_sum, zp, yp):
    row, lane = plane()
    perm_sum[...] = jnp.zeros_like(perm_sum)

    def layer(z, carry):
        pu, ps, pg = carry
        perm = p[z]
        total, inverse, c = couplings(perm, [w[k, z].astype(F32) for k in range(3)])
        g[0, z] = jnp.where(z == 0, 0.0, c[0])
        g[1, z] = jnp.where(z == NZ - 1, 0.0, c[1])
        g[2, z] = jnp.where(row == 0, 0.0, c[2])
        g[3, z] = jnp.where(row == NX - 1, 0.0, c[3])
        g[4, z] = jnp.where(lane == 0, 0.0, c[4])
        g[5, z] = jnp.where(lane == NY - 1, 0.0, c[5])
        diag[z] = total
        here = u[z]
        res = f[z] * inverse - here + own_neighbours(u, g, z)
        s[z] = res
        perm_sum[z // 8] += perm
        mine = layer_lanes(z)
        pu = jnp.where(mine, pltpu.roll(here, 4 * z, 1), pu)
        ps = jnp.where(mine, pltpu.roll(res, 4 * z, 1), ps)
        pg = jnp.where(mine, pltpu.roll(jnp.where(lane == 0, c[4], c[5]), 4 * z, 1), pg)
        return pu, ps, pg

    zero = jnp.zeros((NX, NY), F32)
    pu, ps, pg = lax.fori_loop(0, NZ, layer, (zero, zero, zero), unroll=4)
    yp[0:32, :] = pu
    yp[32:64, :] = ps
    yp[64:96, :] = pg
    for side, z in ((0, 0), (1, NZ - 1)):
        _, _, c = couplings(p[z], [w[k, z].astype(F32) for k in range(3)])
        zp[side, 0:32, :] = u[z]
        zp[side, 32:64, :] = s[z]
        zp[side, 64:96, :] = c[side]
        zp[side, 96:128, :] = jnp.where(lane == 0, c[4], 0.0) + jnp.where(lane == NY - 1, c[5], 0.0)


def z_part(stage, faces, xp, xh):
    row, _ = plane()
    row8 = iota((8, NY), 0)
    all_lines = []
    for side, z in ((0, 0), (1, NZ - 1)):
        res = faces[side, 32:64, :]
        lines = jnp.zeros((8, NY), F32)
        for end, at in ((0, 0), (1, NX - 1)):
            line = xh[end, z : z + 1, :]
            res += jnp.where(row == at, xp[end, 64 + z : 65 + z, :] * line, 0.0)
            lines = jnp.where(row8 == end, line, lines)
        stage[side, 0:32, :] = faces[side, 0:32, :]
        stage[side, 32:64, :] = res
        all_lines.append(lines)
    return all_lines


def first_z_kernel(xodd, xeven, xp, zp, xh, even, odd, stage):
    take_in(xh, xeven, xodd, "gx")
    lines = z_part(stage, zp, xp, xh)
    for side in (0, 1):
        stage[side, 64:128, :] = zp[side, 64:128, :]
        stage[side, 128:136, :] = lines[side]
    put_out(stage, even, odd, "gz")


def y_part(field, res, coupling, zp, zh, xp, xh):
    row, lane = plane()
    row8 = iota((8, NY), 0)
    z_lines = [zh[end, 0:32, :] for end in (0, 1)]
    res += jnp.where(ends(lane), zp[0, 64:96, :] * z_lines[0], 0.0)
    last = 4 * (NZ - 1)
    res += jnp.where(layer_lanes(NZ - 1), pltpu.roll(zp[1, 64:96, :] * z_lines[1], last, 1), 0.0)
    x_lines = jnp.zeros((8, NY), F32)
    for end, at in ((0, 0), (1, NX - 1)):
        line = xh[end, 0:32, :]
        res += jnp.where(row == at, combined_row(xp[end, 64:96, :] * line), 0.0)
        x_lines = jnp.where(row8 == end, combined_row(line), x_lines)
    messages = []
    q = fourths()
    for side in (0, 1):
        body = jnp.where(q == 0, shift_lanes(field, side), shift_lanes(res, 1 + side))
        if coupling is not None:
            body = jnp.where(q == 2, shift_lanes(coupling, 2 + side), body)
        for end in (0, 1):
            at = 3 + 4 * end
            body = jnp.where(lane == at, shift_lanes(z_lines[end], at + side), body)
        messages.append((body, shift_lanes(x_lines, side)))
    return messages


def first_y_kernel(zeven, zodd, xp, zp, yp, xh, zh, even, odd, stage):
    take_in(zh, zeven, zodd, "gz")
    messages = y_part(yp[0:32, :], yp[32:64, :], yp[64:96, :], zp, zh, xp, xh)
    for side in (0, 1):
        stage[side, 0:32, :], stage[side, 32:40, :] = messages[side]
    put_out(stage, even, odd, "gy")


def z_halo_residual(side, res, zh1, yh, mine):
    _, lane = plane()
    at = 3 + 4 * side
    low, high = yh[0, 0:32, at : at + 1], yh[1, 0:32, at : at + 1]
    corner = jnp.where(lane == 0, low, 0.0) + jnp.where(lane == NY - 1, high, 0.0)
    return res + zh1[side, 64:96, :] * mine + zh1[side, 96:128, :] * corner


def x_halo_residual(side, res, xh1, zh, lines, yh, mine):
    row, _ = plane()
    total = res + xh1[side, 64:96, :] * mine
    for end, at in ((0, 0), (1, NZ - 1)):
        total += jnp.where(row == at, xh1[side, 96 + end : 97 + end, :] * zh[end, lines + side : lines + side + 1, :], 0.0)
    corner = combine(yh[0, 32 + side : 33 + side, :], yh[1, 32 + side : 33 + side, :], 0)
    return total + columns(xh1[side, 98:99, :] * corner)


def group_sums(x):
    return jnp.sum(x.reshape(4, 8, NY), axis=1)


def exact_dot(a, b):
    return jnp.dot(a, b, precision=lax.Precision.HIGHEST, preferred_element_type=F32)


def second_kernel(
    u, g, diag, s1, perm_sum, zp, yp, xp, xh, zh, yodd, yeven,
    yh, s, d, acc, b, xp2, even, odd,
    s0, d0, cross, cross2, rsum, rows, stage,
):
    take_in(yh, yeven, yodd, "gy")
    scale = 1.0 / THETA
    low, high = yh[0, 0:32, :], yh[1, 0:32, :]
    own_y = yp[64:96, :]
    yq = own_y * combine(low, high, 0)
    yq2 = own_y * (scale * (combine(low, high, 1) + combine(low, high, 2) * yp[0:32, :]))
    zq, zq2 = [], []
    for side, z in ((0, 0), (1, NZ - 1)):
        zq.append(zp[side, 64:96, :] * zh[side, 0:32, :])
        zq2.append(zp[side, 64:96, :] * (scale * z_halo_residual(side, zh[side, 32:64, :], zh, yh, u[z])))
        gx = xp[side, 64:96, :]
        cross[side] = gx * xh[side, 0:32, :]
        cross2[side] = gx * (scale * x_halo_residual(side, xh[side, 32:64, :], xh, zh, 128, yh, xp[side, 0:32, :]))
    rsum[...] = jnp.zeros_like(rsum)

    def start(z, carry):
        res = s1[z] + from_faces(z, zq, cross, yq)
        s0[z] = res
        d0[z] = res * scale
        rsum[z // 8] += res * diag[z]
        return carry

    lax.fori_loop(0, NZ, start, 0, unroll=8)
    for block in range(4):
        rows[0, 4 * block : 4 * block + 4, :] = group_sums(rsum[block])
        rows[1, 4 * block : 4 * block + 4, :] = group_sums(perm_sum[block])
    select = jnp.where(iota((NY, NY), 0) // 8 == iota((NY, NY), 1), 1.0, 0.0)
    lane16 = iota((16, NY), 1)
    weights = jnp.where(lane16 < 16, exact_dot(rows[1], select), 1.0)
    rhs = jnp.where(lane16 < 16, (OMEGA * 8.0 / 6.0) * exact_dot(rows[0], select) / weights, 0.0)
    b[...] = rhs

    def step(z, carry):
        before = d0[z]
        res = s0[z] - before + own_neighbours(d0, g, z) + from_faces(z, zq2, cross2, yq2)
        after = A[0] * before + B[0] * res
        s[z] = res
        d[z] = after
        acc[z] = u[z] + before + after
        return carry

    lax.fori_loop(0, NZ, step, 0, unroll=8)

    def face(z, carry):
        for side in (0, 1):
            at, r = face_rows(side)
            here = d[z, at, :]
            res = s[z, at, :] - here + inner_neighbours(d, [g[k, z, at, :] for k in range(6)], z, side)
            xp2[side, pl.ds(z, 1), :] = here[r : r + 1]
            xp2[side, pl.ds(NZ + z, 1), :] = res[r : r + 1]
        return carry

    lax.fori_loop(0, NZ, face, 0, unroll=8)
    for side in (0, 1):
        stage[side, 0:64, :] = xp2[side]
        for z in range(4):
            stage[side, 64 + 3 * z : 67 + 3 * z, :] = rhs[4 * z + side : 4 * z + side + 3]
        stage[side, 76:80, :] = jnp.zeros((4, NY), F32)
    put_out(stage, even, odd, "gx")


def second_block_kernel(g, s1, d, s, zp2, yp2):
    def partial(z, carry):
        pu, ps = carry
        here = d[z]
        res = s1[z] - here + own_neighbours(d, g, z)
        s[z] = res
        mine = layer_lanes(z)
        return jnp.where(mine, pltpu.roll(here, 4 * z, 1), pu), jnp.where(mine, pltpu.roll(res, 4 * z, 1), ps)

    zero = jnp.zeros((NX, NY), F32)
    pu, ps = lax.fori_loop(0, NZ, partial, (zero, zero), unroll=8)
    yp2[0:32, :] = pu
    yp2[32:64, :] = ps
    for side, z in ((0, 0), (1, NZ - 1)):
        zp2[side, 0:32, :] = d[z]
        zp2[side, 32:64, :] = s[z]


def second_z_kernel(xodd, xeven, xp, zp2, b, xh2, even, odd, b3, stage, rows):
    take_in(xh2, xeven, xodd, "gx")
    lines = z_part(stage, zp2, xp, xh2)
    lane16 = iota((16, NY), 1)
    wide = b[...]
    for end in (0, 1):
        first = 1 - end
        rows[...] = jnp.zeros_like(rows)
        for z in range(4):
            rows[4 * z + first : 4 * z + first + 3, :] = xh2[end, 64 + 3 * z : 67 + 3 * z, :]
        base = 32 * (end + 1)
        wide = jnp.where((lane16 >= base) & (lane16 < base + 16), pltpu.roll(rows[...], base, 1), wide)
    b3[...] = wide
    for side in (0, 1):
        stage[side, 64:72, :] = lines[side]
        stage[side, 72:88, :] = wide
    put_out(stage, even, odd, "gz")


def second_y_kernel(zeven, zodd, xp, zp, yp2, xh2, b3, zh2, even, odd, stage):
    take_in(zh2, zeven, zodd, "gz")
    messages = y_part(yp2[0:32, :], yp2[32:64, :], None, zp, zh2, xp, xh2)
    within = lax.rem(iota((16, NY), 1), 32)
    parts = (b3[...], zh2[0, 72:88, :], zh2[1, 72:88, :])
    for side in (0, 1):
        stage[side, 0:32, :], stage[side, 32:40, :] = messages[side]
        coarse = jnp.zeros((16, NY), F32)
        for k in range(3):
            at = 4 * k
            moved = shift_lanes(parts[k], at - 13 * side)
            coarse = jnp.where((within >= at) & (within < at + 3), moved, coarse)
        stage[side, 40:56, :] = coarse
    put_out(stage, even, odd, "gy")


def coarse_solve(b3, zh2, yh2, ext, err, spread):
    ext[...] = jnp.zeros_like(ext)
    lane4 = iota((4, NY), 1)
    within = lax.rem(iota((16, NY), 1), 32)
    wide = []
    for k, part in enumerate((b3[...], zh2[0, 72:88, :], zh2[1, 72:88, :])):
        full = jnp.where((within >= 3) & (within < 19), shift_lanes(part, 3), 0.0)
        full = jnp.where(within < 3, shift_lanes(yh2[0, 40:56, :], -4 * k), full)
        wide.append(jnp.where((within >= 19) & (within < 22), shift_lanes(yh2[1, 40:56, :], 19 - 4 * k), full))

    for z in range(10):
        values, at = (wide[1], 4 * (z + 1)) if z < 3 else (wide[0], 4 * (z - 3)) if z < 7 else (wide[2], 4 * (z - 7))
        four = values[at : at + 4]
        own, low, high = [jnp.where(lane4 < 22, shift_lanes(four, -32 * k), 0.0) for k in range(3)]
        ext[z, 0:3, :] = low[1:4]
        ext[z, 3:7, :] = own
        ext[z, 7:10, :] = high[0:3]
    x, y = iota((16, NY), 0), iota((16, NY), 1)
    at_z, at_x, at_y = lax.axis_index("gz"), lax.axis_index("gx"), lax.axis_index("gy")
    last_z, last_x, last_y = lax.axis_size("gz") - 1, lax.axis_size("gx") - 1, lax.axis_size("gy") - 1
    inside = (x < 10) & (y < 22)
    inside &= ((x >= 3) | (at_x > 0)) & ((x < 7) | (at_x < last_x))
    inside &= ((y >= 3) | (at_y > 0)) & ((y < 19) | (at_y < last_y))
    keep = jnp.where(inside, 1.0, 0.0)
    keep_low = jnp.where(at_z > 0, keep, 0.0)
    keep_high = jnp.where(at_z < last_z, keep, 0.0)
    rhs = [ext[z] for z in range(10)]
    e = rhs
    for sweep in range(3):
        lo, hi = sweep + 1, 9 - sweep
        new = []
        for z in range(10):
            if z < lo or z >= hi:
                new.append(e[z])
                continue
            c = e[z]
            beside = e[z - 1] + e[z + 1] + pltpu.roll(c, 1, 0) + pltpu.roll(c, 15, 0) + pltpu.roll(c, 1, 1) + pltpu.roll(c, NY - 1, 1)
            v = (1.0 - OMEGA) * c + (OMEGA / 6.0) * beside + rhs[z]
            new.append(v * (keep_low if z < 3 else keep_high if z >= 7 else keep))
        e = new
    for z in range(4):
        err[4 * z : 4 * z + 4, :] = e[z + 3][3:7]
    select = jnp.where(iota((NY, NY), 0) == iota((NY, NY), 1) // 8 + 3, 1.0, 0.0)
    fine = exact_dot(err[...], select)
    for z in range(4):
        spread[z] = jnp.broadcast_to(fine[4 * z : 4 * z + 4][:, None, :], (4, 8, NY)).reshape(NX, NY)


def third_kernel(
    g, s2, d1, acc, zp, yp, xp, xh, zh, yh, xp2, zp2, yp2, xh2, zh2, b3, yodd, yeven,
    out,
    yh2, s, d, cross, cross2, ext, err, spread,
):
    take_in(yh2, yeven, yodd, "gy")
    low, high = yh2[0, 0:32, :], yh2[1, 0:32, :]
    own_y = yp[64:96, :]
    yu = combine(low, high, 0)
    yq = own_y * yu
    yq2 = own_y * (A[1] * yu + B[1] * (combine(low, high, 1) + combine(yh[0, 0:32, :], yh[1, 0:32, :], 2) * yp2[0:32, :]))
    zq, zq2 = [], []
    for side, z in ((0, 0), (1, NZ - 1)):
        zu, xu = zh2[side, 0:32, :], xh2[side, 0:32, :]
        zq.append(zp[side, 64:96, :] * zu)
        dz = A[1] * zu + B[1] * z_halo_residual(side, zh2[side, 32:64, :], zh, yh2, zp2[side, 0:32, :])
        zq2.append(zp[side, 64:96, :] * dz)
        gx = xp[side, 64:96, :]
        cross[side] = gx * xu
        dx = A[1] * xu + B[1] * x_halo_residual(side, xh2[side, 32:64, :], xh, zh2, 64, yh2, xp2[side, 0:32, :])
        cross2[side] = gx * dx
    coarse_solve(b3, zh2, yh2, ext, err, spread)

    def step(z, carry):
        res = s2[z] + from_faces(z, zq, cross, yq)
        s[z] = res
        d[z] = A[1] * d1[z] + B[1] * res
        return carry

    lax.fori_loop(0, NZ, step, 0, unroll=8)

    def finish(z, carry):
        before = d[z]
        res = s[z] - before + own_neighbours(d, g, z) + from_faces(z, zq2, cross2, yq2)
        out[z] = acc[z] + before + (A[2] * before + B[2] * res) + spread[z // 8]
        return carry

    lax.fori_loop(0, NZ, finish, 0, unroll=8)


VM = pl.BlockSpec(memory_space=pltpu.VMEM)
HBM = pl.BlockSpec(memory_space=pltpu.HBM)
BF16_FIELD = jax.ShapeDtypeStruct((3,) + FULL, jnp.bfloat16)


def call(kernel, name, n_in, outs, scratch=(), us=0.2, place=VM, more=()):
    return pl.pallas_call(
        kernel,
        out_shape=[x if isinstance(x, jax.ShapeDtypeStruct) else jax.ShapeDtypeStruct(x, F32) for x in outs],
        in_specs=[place] * n_in,
        out_specs=[VM] * len(outs),
        scratch_shapes=[pltpu.VMEM(shape, F32) for shape in scratch] + list(more),
        compiler_params=pltpu.CompilerParams(vmem_limit_bytes=32 * 2**20),
        cost_estimate=pl.CostEstimate(flops=0, transcendentals=0, bytes_accessed=int(us * 3e6)),
        name=name,
    )


def swap(even, odd, axis):
    count = lax.axis_size(axis)
    results = []
    for first, values in ((1, odd), (0, even)):
        pairs = []
        for i in range(first, count - 1, 2):
            pairs += [(i, i + 1), (i + 1, i)]
        results.append(lax.ppermute(values, axis, pairs))
    return results[::-1]


def per_device(u, f, p, w):
    face = (2, 32, NY)
    far = [pltpu.with_memory_space_constraint(x, pltpu.HBM) for x in (u, f, p, w)]
    u, f, p, w, xp, even, odd = call(
        face_kernel, "x_faces", 4, [FULL, FULL, FULL, BF16_FIELD, (2, XM1, NY), (XM1, NY), (XM1, NY)], (), 2.0, HBM,
        [pltpu.SemaphoreType.DMA((4, 4))],
    )(*far)
    g, diag, s, perm_sum, zp, yp = call(
        block_kernel, "block", 4, [(6,) + FULL, FULL, FULL, (4, NX, NY), (2, 128, NY), (96, NY)], (), 2.5
    )(u, f, p, w)
    even, odd = swap(even, odd, "gx")
    xh, even, odd = call(first_z_kernel, "z_message", 4, [(2, XM1, NY), (ZM1, NY), (ZM1, NY)], [(2, ZM1, NY)])(odd, even, xp, zp)
    even, odd = swap(even, odd, "gz")
    zh, even, odd = call(
        first_y_kernel, "y_message", 6, [(2, ZM1, NY), (YM1, NY), (YM1, NY)], [(2, YM1, NY)]
    )(even, odd, xp, zp, yp, xh)
    even, odd = swap(even, odd, "gy")
    yh, s, d1, acc, b, xp2, even, odd = call(
        second_kernel, "two_steps", 12,
        [(2, YM1, NY), FULL, FULL, FULL, (16, NY), (2, 64, NY), (XM2, NY), (XM2, NY)],
        [FULL, FULL, face, face, (4, NX, NY), (2, 16, NY), (2, XM2, NY)], 2.0,
    )(u, g, diag, s, perm_sum, zp, yp, xp, xh, zh, odd, even)
    s, zp2, yp2 = call(
        second_block_kernel, "block_2", 3, [FULL, (2, 64, NY), (64, NY)], (), 1.5
    )(g, s, d1)
    even, odd = swap(even, odd, "gx")
    xh2, even, odd, b3 = call(
        second_z_kernel, "z_message_2", 5, [(2, XM2, NY), (ZM2, NY), (ZM2, NY), (16, NY)], [(2, ZM2, NY), (16, NY)]
    )(odd, even, xp, zp2, b)
    even, odd = swap(even, odd, "gz")
    zh2, even, odd = call(
        second_y_kernel, "y_message_2", 7, [(2, ZM2, NY), (YM2, NY), (YM2, NY)], [(2, YM2, NY)]
    )(even, odd, xp, zp, yp2, xh2, b3)
    even, odd = swap(even, odd, "gy")
    (out,) = call(
        third_kernel, "last_steps", 18, [FULL],
        [(2, YM2, NY), FULL, FULL, face, face, (10, 16, NY), (16, NY), (4, NX, NY)], 2.5,
    )(g, s, d1, acc, zp, yp, xp, xh, zh, yh, xp2, zp2, yp2, xh2, zh2, b3, odd, even)
    return out


def solution(mesh):
    placed = (
        P("gz", "gx", "gy"),
        P("gz", "gx", "gy"),
        P("gz", "gx", "gy"),
        P(None, "gz", "gx", "gy"),
    )
    return jax.shard_map(
        per_device, mesh=mesh, in_specs=placed, out_specs=P("gz", "gx", "gy"), check_vma=False
    )
```

time: 84.6 us -> 83 us (0.981)
  the two profiles are of different devices: /device:TPU:283 before, /device:TPU:285 now
where the time goes in v4:
time: 83 us; the launch traced here: 82.6 us
  starting transfers between devices  55.5 us (67%)
  waiting for transfers between devices  16.4 us (20%)
  Pallas kernels  10.5 us (13%)
    ppermute x12, starting transfers between devices, swap(): results.append(lax.ppermute(values, axis, pairs))  55.5 us
    ppermute x12, waiting for transfers between devices, swap(): results.append(lax.ppermute(values, axis, pairs))  16.4 us
    pallas_call x1, Pallas kernels, per_device(): call(third_kernel, 'last_steps', 18, [FULL], [(2, YM2, NY), FULL, FULL, f...  2.66 us
    pallas_call x1, Pallas kernels, per_device(): call(face_kernel, 'x_faces', 4, [FULL, FULL, FULL, BF16_FIELD, (2, XM1, N...  2.26 us
    pallas_call x1, Pallas kernels, per_device(): call(second_kernel, 'two_steps', 12, [(2, YM1, NY), FULL, FULL, FULL, (16...  2.22 us
    pallas_call x1, Pallas kernels, per_device(): call(block_kernel, 'block', 4, [(6,) + FULL, FULL, FULL, (4, NX, NY), (2,...  1.67 us
  transfers between devices with their start and end apart: 12, of which 8 were waited for; matrix products, arithmetic and copies ran while one was open for 0% of the time, Pallas kernels for 3%

profile of v4, /device:TPU:285, one launch (start us, length us, event | category | flops | bytes accessed | tf_op | source)
XLA Modules:
  0.0 82.6 jit_solution(16867200464697171621)
XLA Ops:
  0.0 2.3 %x_faces.1 = (f32[32,32,128]{2,1,0:T(8,128)S(1)}, f32[32,32,128]{2,1,0:T(8,128)S(1)}, f32[32,32,128]{2,1,0:T(8,128)S(1)}, bf16[3,32,32,128]{3,2,1,0:T(8,128)(2,1...) custom-call(f32[32,32,128]{2,1,0:T(8,128)} %u_far.1, f32[32,32,128]{2,1,0:T(8,128)} %f_far.1, ...), custom_call_target="tpu_custom_call" | custom-call | bytes 6000000 | tf_op jit(solution)/shard_map/x_faces/pallas_call | solution.py:549
  2.3 15.1 %collective-permute-start = (f32[104,128]{1,0:T(8,128)S(1)}, f32[104,128]{1,0:T(8,128)S(1)}, u32[]{:S(2)}, u32[]{:S(2)}) collective-permute-start(f32[104,128]{1,0:T(8,128)S(1)} %get-tuple-element.53), channel_id=1, source_target_pairs={{64,128},{128,64},{192,256},{256,192},{320,384},{384,320},{448,512... | collective-permute-start | bytes 159752 | tf_op jit(solution)/shard_map/ppermute | solution.py:542
  17.4 1.9 %collective-permute-start.1 = (f32[104,128]{1,0:T(8,128)S(1)}, f32[104,128]{1,0:T(8,128)S(1)}, u32[]{:S(2)}, u32[]{:S(2)}) collective-permute-start(f32[104,128]{1,0:T(8,128)S(1)} %get-tuple-element.54), channel_id=1, source_target_pairs={{0,64},{64,0},{128,192},{192,128},{256,320},{320,256},{384,448},{4... | collective-permute-start | bytes 159752 | tf_op jit(solution)/shard_map/ppermute | solution.py:542
  19.3 1.7 %block.1 = (f32[6,32,32,128]{3,2,1,0:T(8,128)S(1)}, f32[32,32,128]{2,1,0:T(8,128)S(1)}, f32[32,32,128]{2,1,0:T(8,128)S(1)}, f32[4,32,128]{2,1,0:T(8,128)S(1)}, f...) custom-call(f32[32,32,128]{2,1,0:T(8,128)S(1)} %get-tuple-element.42.u, f32[32,32,128]{2,1,0:T(8,128)S(1)} %get-tuple-element.43.f, ...), custom_call_target="tpu_custom_call" | custom-call | bytes 7500000 | tf_op jit(solution)/shard_map/block/pallas_call | solution.py:553
  21.0 3.5 %collective-permute-done.xodd = f32[104,128]{1,0:T(8,128)S(1)} collective-permute-done((f32[104,128]{1,0:T(8,128)S(1)}, f32[104,128]{1,0:T(8,128)S(1)}, u32[]{:S(2)}, u32[]{:S(2)}) %collective-permute-start) | collective-permute-done | bytes 53280 | tf_op jit(solution)/shard_map/ppermute | solution.py:542
  24.5 2.8 %collective-permute-start.2 = (f32[136,128]{1,0:T(8,128)S(1)}, f32[136,128]{1,0:T(8,128)S(1)}, u32[]{:S(2)}, u32[]{:S(2)}) collective-permute-start(f32[136,128]{1,0:T(8,128)S(1)} %get-tuple-element.56), channel_id=1, source_target_pairs={{0,1},{1,0},{2,3},{3,2},{4,5},{5,4},{6,7},{7,6},{8,9},{9,8},{10,11... | collective-permute-start | bytes 208904 | tf_op jit(solution)/shard_map/ppermute | solution.py:542
  27.3 1.9 %collective-permute-start.3 = (f32[136,128]{1,0:T(8,128)S(1)}, f32[136,128]{1,0:T(8,128)S(1)}, u32[]{:S(2)}, u32[]{:S(2)}) collective-permute-start(f32[136,128]{1,0:T(8,128)S(1)} %get-tuple-element.57), channel_id=1, source_target_pairs={{1,2},{2,1},{5,6},{6,5},{9,10},{10,9},{13,14},{14,13},{17,18},{18,... | collective-permute-start | bytes 208904 | tf_op jit(solution)/shard_map/ppermute | solution.py:542
  29.5 2.8 %collective-permute-done.3.zodd = f32[136,128]{1,0:T(8,128)S(1)} collective-permute-done((f32[136,128]{1,0:T(8,128)S(1)}, f32[136,128]{1,0:T(8,128)S(1)}, u32[]{:S(2)}, u32[]{:S(2)}) %collective-permute-start.3) | collective-permute-done | bytes 69664 | tf_op jit(solution)/shard_map/ppermute | solution.py:542
  32.6 6.0 %collective-permute-start.4 = (f32[40,128]{1,0:T(8,128)S(1)}, f32[40,128]{1,0:T(8,128)S(1)}, u32[]{:S(2)}, u32[]{:S(2)}) collective-permute-start(f32[40,128]{1,0:T(8,128)S(1)} %get-tuple-element.59), channel_id=1, source_target_pairs={{4,8},{8,4},{12,16},{16,12},{20,24},{24,20},{28,32},{32,28},{36,40... | collective-permute-start | bytes 61448 | tf_op jit(solution)/shard_map/ppermute | solution.py:542
  38.6 1.9 %collective-permute-start.5 = (f32[40,128]{1,0:T(8,128)S(1)}, f32[40,128]{1,0:T(8,128)S(1)}, u32[]{:S(2)}, u32[]{:S(2)}) collective-permute-start(f32[40,128]{1,0:T(8,128)S(1)} %get-tuple-element.60), channel_id=1, source_target_pairs={{0,4},{4,0},{8,12},{12,8},{16,20},{20,16},{24,28},{28,24},{32,36},... | collective-permute-start | bytes 61448 | tf_op jit(solution)/shard_map/ppermute | solution.py:542
  40.5 1.1 %collective-permute-done.5.yeven = f32[40,128]{1,0:T(8,128)S(1)} collective-permute-done((f32[40,128]{1,0:T(8,128)S(1)}, f32[40,128]{1,0:T(8,128)S(1)}, u32[]{:S(2)}, u32[]{:S(2)}) %collective-permute-start.5) | collective-permute-done | bytes 20512 | tf_op jit(solution)/shard_map/ppermute | solution.py:542
  41.7 2.2 %two_steps.1 = (f32[2,40,128]{2,1,0:T(8,128)S(1)}, f32[32,32,128]{2,1,0:T(8,128)S(1)}, f32[32,32,128]{2,1,0:T(8,128)S(1)}, f32[32,32,128]{2,1,0:T(8,128)S(1)}, f...) custom-call(f32[32,32,128]{2,1,0:T(8,128)S(1)} %get-tuple-element.42.u, ...), custom_call_target="tpu_custom_call" | custom-call | bytes 6000000 | tf_op jit(solution)/shard_map/two_steps/pallas_call | solution.py:563
  43.9 14.9 %collective-permute-start.6 = (f32[80,128]{1,0:T(8,128)S(1)}, f32[80,128]{1,0:T(8,128)S(1)}, u32[]{:S(2)}, u32[]{:S(2)}) collective-permute-start(f32[80,128]{1,0:T(8,128)S(1)} %get-tuple-element.69), channel_id=1, source_target_pairs={{64,128},{128,64},{192,256},{256,192},{320,384},{384,320},{448,512... | collective-permute-start | bytes 122888 | tf_op jit(solution)/shard_map/ppermute | solution.py:542
  58.8 1.9 %collective-permute-start.7 = (f32[80,128]{1,0:T(8,128)S(1)}, f32[80,128]{1,0:T(8,128)S(1)}, u32[]{:S(2)}, u32[]{:S(2)}) collective-permute-start(f32[80,128]{1,0:T(8,128)S(1)} %get-tuple-element.70), channel_id=1, source_target_pairs={{0,64},{64,0},{128,192},{192,128},{256,320},{320,256},{384,448},{4... | collective-permute-start | bytes 122888 | tf_op jit(solution)/shard_map/ppermute | solution.py:542
  60.8 1.1 %block_2.1 = (f32[32,32,128]{2,1,0:T(8,128)S(1)}, f32[2,64,128]{2,1,0:T(8,128)S(1)}, f32[64,128]{1,0:T(8,128)S(1)}) custom-call(f32[6,32,32,128]{3,2,1,0:T(8,128)S(1)} %get-tuple-element.46.g, f32[32,32,128]{2,1,0:T(8,128)S(1)} %get-tuple-element.61.s1, f32[32,32,128]{2,1,0:T(8,128)S(1)} %get-tuple-element.62.d.d1), custom_call_target="tpu_custom_call" | custom-call | bytes 4500000 | tf_op jit(solution)/shard_map/block_2/pallas_call | solution.py:568
  61.9 4.7 %collective-permute-done.6.xodd = f32[80,128]{1,0:T(8,128)S(1)} collective-permute-done((f32[80,128]{1,0:T(8,128)S(1)}, f32[80,128]{1,0:T(8,128)S(1)}, u32[]{:S(2)}, u32[]{:S(2)}) %collective-permute-start.6) | collective-permute-done | bytes 40992 | tf_op jit(solution)/shard_map/ppermute | solution.py:542
  66.7 1.9 %collective-permute-start.8 = (f32[88,128]{1,0:T(8,128)S(1)}, f32[88,128]{1,0:T(8,128)S(1)}, u32[]{:S(2)}, u32[]{:S(2)}) collective-permute-start(f32[88,128]{1,0:T(8,128)S(1)} %get-tuple-element.73), channel_id=1, source_target_pairs={{0,1},{1,0},{2,3},{3,2},{4,5},{5,4},{6,7},{7,6},{8,9},{9,8},{10,11... | collective-permute-start | bytes 135176 | tf_op jit(solution)/shard_map/ppermute | solution.py:542
  68.6 1.9 %collective-permute-start.9 = (f32[88,128]{1,0:T(8,128)S(1)}, f32[88,128]{1,0:T(8,128)S(1)}, u32[]{:S(2)}, u32[]{:S(2)}) collective-permute-start(f32[88,128]{1,0:T(8,128)S(1)} %get-tuple-element.74), channel_id=1, source_target_pairs={{1,2},{2,1},{5,6},{6,5},{9,10},{10,9},{13,14},{14,13},{17,18},{18,... | collective-permute-start | bytes 135176 | tf_op jit(solution)/shard_map/ppermute | solution.py:542
  70.5 0.9 %collective-permute-done.8.zeven = f32[88,128]{1,0:T(8,128)S(1)} collective-permute-done((f32[88,128]{1,0:T(8,128)S(1)}, f32[88,128]{1,0:T(8,128)S(1)}, u32[]{:S(2)}, u32[]{:S(2)}) %collective-permute-start.8) | collective-permute-done | bytes 45088 | tf_op jit(solution)/shard_map/ppermute | solution.py:542
  71.4 1.9 %collective-permute-done.9.zodd = f32[88,128]{1,0:T(8,128)S(1)} collective-permute-done((f32[88,128]{1,0:T(8,128)S(1)}, f32[88,128]{1,0:T(8,128)S(1)}, u32[]{:S(2)}, u32[]{:S(2)}) %collective-permute-start.9) | collective-permute-done | bytes 45088 | tf_op jit(solution)/shard_map/ppermute | solution.py:542
  73.6 3.2 %collective-permute-start.10 = (f32[56,128]{1,0:T(8,128)S(1)}, f32[56,128]{1,0:T(8,128)S(1)}, u32[]{:S(2)}, u32[]{:S(2)}) collective-permute-start(f32[56,128]{1,0:T(8,128)S(1)} %get-tuple-element.77), channel_id=1, source_target_pairs={{4,8},{8,4},{12,16},{16,12},{20,24},{24,20},{28,32},{32,28},{36,40... | collective-permute-start | bytes 86024 | tf_op jit(solution)/shard_map/ppermute | solution.py:542
  76.8 1.9 %collective-permute-start.11 = (f32[56,128]{1,0:T(8,128)S(1)}, f32[56,128]{1,0:T(8,128)S(1)}, u32[]{:S(2)}, u32[]{:S(2)}) collective-permute-start(f32[56,128]{1,0:T(8,128)S(1)} %get-tuple-element.78), channel_id=1, source_target_pairs={{0,4},{4,0},{8,12},{12,8},{16,20},{20,16},{24,28},{28,24},{32,36},... | collective-permute-start | bytes 86024 | tf_op jit(solution)/shard_map/ppermute | solution.py:542
  78.8 1.1 %collective-permute-done.11.yeven = f32[56,128]{1,0:T(8,128)S(1)} collective-permute-done((f32[56,128]{1,0:T(8,128)S(1)}, f32[56,128]{1,0:T(8,128)S(1)}, u32[]{:S(2)}, u32[]{:S(2)}) %collective-permute-start.11) | collective-permute-done | bytes 28704 | tf_op jit(solution)/shard_map/ppermute | solution.py:542
  79.9 2.7 %last_steps.1 = f32[32,32,128]{2,1,0:T(8,128)} custom-call(f32[6,32,32,128]{3,2,1,0:T(8,128)S(1)} %get-tuple-element.46.g, f32[32,32,128]{2,1,0:T(8,128)S(1)} %get-tuple-element.63.s2, f32[32,32,128]{2,1,0:T(8,128)S(1)} %get-tuple-element.62.d.d1, f32[32,32,128]{2,1,0:T(8,128)S(1)} %get-tuple-element.64.acc, f32[2,128,128]{2,1,0:T(8,128)S(1)} %get-tuple-element.50.zp, ...), custom_call_target="tpu_custom_call" | custom-call | bytes 7500000 | tf_op jit(solution)/shard_map/last_steps/pallas_call | solution.py:580
  (9 shorter events, 0.9 us)
Async XLA Ops:
  2.3 22.2 %collective-permute-start = (f32[104,128]{1,0:T(8,128)S(1)}, f32[104,128]{1,0:T(8,128)S(1)}, u32[]{:S(2)}, u32[]{:S(2)}) collective-permute-start(f32[104,128]{1,0:T(8,128)S(1)} %get-tuple-element.53), channel_id=1, source_target_pairs={{64,128},{128,64},{192,256},{256,192},{320,384},{384,320},{448,512... | collective-permute-start | bytes 159752 | tf_op jit(solution)/shard_map/ppermute | solution.py:542
  17.4 7.1 %collective-permute-start.1 = (f32[104,128]{1,0:T(8,128)S(1)}, f32[104,128]{1,0:T(8,128)S(1)}, u32[]{:S(2)}, u32[]{:S(2)}) collective-permute-start(f32[104,128]{1,0:T(8,128)S(1)} %get-tuple-element.54), channel_id=1, source_target_pairs={{0,64},{64,0},{128,192},{192,128},{256,320},{320,256},{384,448},{4... | collective-permute-start | bytes 159752 | tf_op jit(solution)/shard_map/ppermute | solution.py:542
  24.5 5.1 %collective-permute-start.2 = (f32[136,128]{1,0:T(8,128)S(1)}, f32[136,128]{1,0:T(8,128)S(1)}, u32[]{:S(2)}, u32[]{:S(2)}) collective-permute-start(f32[136,128]{1,0:T(8,128)S(1)} %get-tuple-element.56), channel_id=1, source_target_pairs={{0,1},{1,0},{2,3},{3,2},{4,5},{5,4},{6,7},{7,6},{8,9},{9,8},{10,11... | collective-permute-start | bytes 208904 | tf_op jit(solution)/shard_map/ppermute | solution.py:542
  27.3 5.1 %collective-permute-start.3 = (f32[136,128]{1,0:T(8,128)S(1)}, f32[136,128]{1,0:T(8,128)S(1)}, u32[]{:S(2)}, u32[]{:S(2)}) collective-permute-start(f32[136,128]{1,0:T(8,128)S(1)} %get-tuple-element.57), channel_id=1, source_target_pairs={{1,2},{2,1},{5,6},{6,5},{9,10},{10,9},{13,14},{14,13},{17,18},{18,... | collective-permute-start | bytes 208904 | tf_op jit(solution)/shard_map/ppermute | solution.py:542
  32.6 7.9 %collective-permute-start.4 = (f32[40,128]{1,0:T(8,128)S(1)}, f32[40,128]{1,0:T(8,128)S(1)}, u32[]{:S(2)}, u32[]{:S(2)}) collective-permute-start(f32[40,128]{1,0:T(8,128)S(1)} %get-tuple-element.59), channel_id=1, source_target_pairs={{4,8},{8,4},{12,16},{16,12},{20,24},{24,20},{28,32},{32,28},{36,40... | collective-permute-start | bytes 61448 | tf_op jit(solution)/shard_map/ppermute | solution.py:542
  38.6 3.1 %collective-permute-start.5 = (f32[40,128]{1,0:T(8,128)S(1)}, f32[40,128]{1,0:T(8,128)S(1)}, u32[]{:S(2)}, u32[]{:S(2)}) collective-permute-start(f32[40,128]{1,0:T(8,128)S(1)} %get-tuple-element.60), channel_id=1, source_target_pairs={{0,4},{4,0},{8,12},{12,8},{16,20},{20,16},{24,28},{28,24},{32,36},... | collective-permute-start | bytes 61448 | tf_op jit(solution)/shard_map/ppermute | solution.py:542
  43.9 22.7 %collective-permute-start.6 = (f32[80,128]{1,0:T(8,128)S(1)}, f32[80,128]{1,0:T(8,128)S(1)}, u32[]{:S(2)}, u32[]{:S(2)}) collective-permute-start(f32[80,128]{1,0:T(8,128)S(1)} %get-tuple-element.69), channel_id=1, source_target_pairs={{64,128},{128,64},{192,256},{256,192},{320,384},{384,320},{448,512... | collective-permute-start | bytes 122888 | tf_op jit(solution)/shard_map/ppermute | solution.py:542
  58.8 7.7 %collective-permute-start.7 = (f32[80,128]{1,0:T(8,128)S(1)}, f32[80,128]{1,0:T(8,128)S(1)}, u32[]{:S(2)}, u32[]{:S(2)}) collective-permute-start(f32[80,128]{1,0:T(8,128)S(1)} %get-tuple-element.70), channel_id=1, source_target_pairs={{0,64},{64,0},{128,192},{192,128},{256,320},{320,256},{384,448},{4... | collective-permute-start | bytes 122888 | tf_op jit(solution)/shard_map/ppermute | solution.py:542
  66.7 4.8 %collective-permute-start.8 = (f32[88,128]{1,0:T(8,128)S(1)}, f32[88,128]{1,0:T(8,128)S(1)}, u32[]{:S(2)}, u32[]{:S(2)}) collective-permute-start(f32[88,128]{1,0:T(8,128)S(1)} %get-tuple-element.73), channel_id=1, source_target_pairs={{0,1},{1,0},{2,3},{3,2},{4,5},{5,4},{6,7},{7,6},{8,9},{9,8},{10,11... | collective-permute-start | bytes 135176 | tf_op jit(solution)/shard_map/ppermute | solution.py:542
  68.6 4.8 %collective-permute-start.9 = (f32[88,128]{1,0:T(8,128)S(1)}, f32[88,128]{1,0:T(8,128)S(1)}, u32[]{:S(2)}, u32[]{:S(2)}) collective-permute-start(f32[88,128]{1,0:T(8,128)S(1)} %get-tuple-element.74), channel_id=1, source_target_pairs={{1,2},{2,1},{5,6},{6,5},{9,10},{10,9},{13,14},{14,13},{17,18},{18,... | collective-permute-start | bytes 135176 | tf_op jit(solution)/shard_map/ppermute | solution.py:542
  73.6 5.2 %collective-permute-start.10 = (f32[56,128]{1,0:T(8,128)S(1)}, f32[56,128]{1,0:T(8,128)S(1)}, u32[]{:S(2)}, u32[]{:S(2)}) collective-permute-start(f32[56,128]{1,0:T(8,128)S(1)} %get-tuple-element.77), channel_id=1, source_target_pairs={{4,8},{8,4},{12,16},{16,12},{20,24},{24,20},{28,32},{32,28},{36,40... | collective-permute-start | bytes 86024 | tf_op jit(solution)/shard_map/ppermute | solution.py:542
  76.8 3.1 %collective-permute-start.11 = (f32[56,128]{1,0:T(8,128)S(1)}, f32[56,128]{1,0:T(8,128)S(1)}, u32[]{:S(2)}, u32[]{:S(2)}) collective-permute-start(f32[56,128]{1,0:T(8,128)S(1)} %get-tuple-element.78), channel_id=1, source_target_pairs={{0,4},{4,0},{8,12},{12,8},{16,20},{20,16},{24,28},{28,24},{32,36},... | collective-permute-start | bytes 86024 | tf_op jit(solution)/shard_map/ppermute | solution.py:542

commit v5 on v4

--- a/solution.py
+++ b/solution.py
@@ -22,7 +22,8 @@
 B = (2.0 * RHO1 / DELTA, 2.0 * RHO2 / DELTA, 2.0 * RHO3 / DELTA)
 
 XM1 = 104
-ZM1 = 136
+ZM1 = 104
+ZH1 = 136
 YM1 = 40
 XM2 = 80
 ZM2 = 88
@@ -132,7 +133,7 @@
     return total
 
 
-def face_kernel(u_far, f_far, p_far, w_far, u, f, p, w, xp, even, odd, sems):
+def face_kernel(u_far, f_far, p_far, w_far, u, f, p, w, xp, even, odd, zeven, zodd, sems):
     lane8 = iota((8, NY), 1)
     copies = []
     for part in range(4):
@@ -183,6 +184,9 @@
             xp[side, 96 + end : 97 + end, :] = c[end][r : r + 1]
         xp[side, 98:99, :] = edges[side][r : r + 1]
     put_out(xp, even, odd, "gx")
+    odd_one = parity("gz")
+    zeven[...] = u[(1 - odd_one) * (NZ - 1)]
+    zodd[...] = u[odd_one * (NZ - 1)]
 
 
 def block_kernel(u, f, p, w, g, diag, s, perm_sum, zp, yp):
@@ -240,15 +244,6 @@
     return all_lines
 
 
-def first_z_kernel(xodd, xeven, xp, zp, xh, even, odd, stage):
-    take_in(xh, xeven, xodd, "gx")
-    lines = z_part(stage, zp, xp, xh)
-    for side in (0, 1):
-        stage[side, 64:128, :] = zp[side, 64:128, :]
-        stage[side, 128:136, :] = lines[side]
-    put_out(stage, even, odd, "gz")
-
-
 def y_part(field, res, coupling, zp, zh, xp, xh):
     row, lane = plane()
     row8 = iota((8, NY), 0)
@@ -274,12 +269,23 @@
     return messages
 
 
-def first_y_kernel(zeven, zodd, xp, zp, yp, xh, zh, even, odd, stage):
-    take_in(zh, zeven, zodd, "gz")
-    messages = y_part(yp[0:32, :], yp[32:64, :], yp[64:96, :], zp, zh, xp, xh)
-    for side in (0, 1):
-        stage[side, 0:32, :], stage[side, 32:40, :] = messages[side]
-    put_out(stage, even, odd, "gy")
+def first_message_kernel(
+    xodd, xeven, zeven, zodd, xp, zp, yp,
+    xh, zu, z_to_even, z_to_odd, y_to_even, y_to_odd,
+    z_stage, z_rows, y_stage,
+):
+    take_in(xh, xeven, xodd, "gx")
+    take_in(zu, zeven, zodd, "gz")
+    lines = z_part(z_stage, zp, xp, xh)
+    for side in (0, 1):
+        z_rows[side, 0:32, :] = z_stage[side, 32:64, :]
+        z_rows[side, 32:96, :] = zp[side, 64:128, :]
+        z_rows[side, 96:104, :] = lines[side]
+    put_out(z_rows, z_to_even, z_to_odd, "gz")
+    messages = y_part(yp[0:32, :], yp[32:64, :], yp[64:96, :], zp, zu, xp, xh)
+    for side in (0, 1):
+        y_stage[side, 0:32, :], y_stage[side, 32:40, :] = messages[side]
+    put_out(y_stage, y_to_even, y_to_odd, "gy")
 
 
 def z_halo_residual(side, res, zh1, yh, mine):
@@ -308,11 +314,15 @@
 
 
 def second_kernel(
-    u, g, diag, s1, perm_sum, zp, yp, xp, xh, zh, yodd, yeven,
-    yh, s, d, acc, b, xp2, even, odd,
-    s0, d0, cross, cross2, rsum, rows, stage,
+    u, g, diag, s1, perm_sum, zp, yp, xp, xh, zu, yodd, zeven, zodd, yeven,
+    zh, yh, s, d, acc, b, xp2, even, odd,
+    zin, s0, d0, cross, cross2, rsum, rows, stage,
 ):
     take_in(yh, yeven, yodd, "gy")
+    take_in(zin, zeven, zodd, "gz")
+    for side in (0, 1):
+        zh[side, 0:32, :] = zu[side]
+        zh[side, 32:ZH1, :] = zin[side]
     scale = 1.0 / THETA
     low, high = yh[0, 0:32, :], yh[1, 0:32, :]
     own_y = yp[64:96, :]
@@ -546,25 +556,28 @@
 def per_device(u, f, p, w):
     face = (2, 32, NY)
     far = [pltpu.with_memory_space_constraint(x, pltpu.HBM) for x in (u, f, p, w)]
-    u, f, p, w, xp, even, odd = call(
-        face_kernel, "x_faces", 4, [FULL, FULL, FULL, BF16_FIELD, (2, XM1, NY), (XM1, NY), (XM1, NY)], (), 2.0, HBM,
+    u, f, p, w, xp, even, odd, zeven, zodd = call(
+        face_kernel, "x_faces", 4,
+        [FULL, FULL, FULL, BF16_FIELD, (2, XM1, NY), (XM1, NY), (XM1, NY), (NX, NY), (NX, NY)], (), 2.0, HBM,
         [pltpu.SemaphoreType.DMA((4, 4))],
     )(*far)
     g, diag, s, perm_sum, zp, yp = call(
         block_kernel, "block", 4, [(6,) + FULL, FULL, FULL, (4, NX, NY), (2, 128, NY), (96, NY)], (), 2.5
     )(u, f, p, w)
     even, odd = swap(even, odd, "gx")
-    xh, even, odd = call(first_z_kernel, "z_message", 4, [(2, XM1, NY), (ZM1, NY), (ZM1, NY)], [(2, ZM1, NY)])(odd, even, xp, zp)
-    even, odd = swap(even, odd, "gz")
-    zh, even, odd = call(
-        first_y_kernel, "y_message", 6, [(2, ZM1, NY), (YM1, NY), (YM1, NY)], [(2, YM1, NY)]
-    )(even, odd, xp, zp, yp, xh)
-    even, odd = swap(even, odd, "gy")
-    yh, s, d1, acc, b, xp2, even, odd = call(
-        second_kernel, "two_steps", 12,
-        [(2, YM1, NY), FULL, FULL, FULL, (16, NY), (2, 64, NY), (XM2, NY), (XM2, NY)],
-        [FULL, FULL, face, face, (4, NX, NY), (2, 16, NY), (2, XM2, NY)], 2.0,
-    )(u, g, diag, s, perm_sum, zp, yp, xp, xh, zh, odd, even)
+    zeven, zodd = swap(zeven, zodd, "gz")
+    xh, zu, zeven, zodd, yeven, yodd = call(
+        first_message_kernel, "zy_message", 7,
+        [(2, XM1, NY), (2, NX, NY), (ZM1, NY), (ZM1, NY), (YM1, NY), (YM1, NY)],
+        [(2, 64, NY), (2, ZM1, NY), (2, YM1, NY)],
+    )(odd, even, zeven, zodd, xp, zp, yp)
+    zeven, zodd = swap(zeven, zodd, "gz")
+    yeven, yodd = swap(yeven, yodd, "gy")
+    zh, yh, s, d1, acc, b, xp2, even, odd = call(
+        second_kernel, "two_steps", 14,
+        [(2, ZH1, NY), (2, YM1, NY), FULL, FULL, FULL, (16, NY), (2, 64, NY), (XM2, NY), (XM2, NY)],
+        [(2, ZM1, NY), FULL, FULL, face, face, (4, NX, NY), (2, 16, NY), (2, XM2, NY)], 2.0,
+    )(u, g, diag, s, perm_sum, zp, yp, xp, xh, zu, yodd, zeven, zodd, yeven)
     s, zp2, yp2 = call(
         second_block_kernel, "block_2", 3, [FULL, (2, 64, NY), (64, NY)], (), 1.5
     )(g, s, d1)

time: 83 us -> 81.8 us (0.986)
  the two profiles are of different devices: /device:TPU:285 before, /device:TPU:283 now
where the time goes in v5:
time: 81.8 us; the launch traced here: 81.4 us
  starting transfers between devices  63.5 us (78%)
  Pallas kernels  10.5 us (13%)
  waiting for transfers between devices  7.18 us (9%)
    ppermute x14, starting transfers between devices, swap(): results.append(lax.ppermute(values, axis, pairs))  63.5 us
    ppermute x14, waiting for transfers between devices, swap(): results.append(lax.ppermute(values, axis, pairs))  7.18 us
    pallas_call x1, Pallas kernels, per_device(): call(third_kernel, 'last_steps', 18, [FULL], [(2, YM2, NY), FULL, FULL, f...  2.66 us
    pallas_call x1, Pallas kernels, per_device(): call(second_kernel, 'two_steps', 14, [(2, ZH1, NY), (2, YM1, NY), FULL, F...  2.31 us
    pallas_call x1, Pallas kernels, per_device(): call(face_kernel, 'x_faces', 4, [FULL, FULL, FULL, BF16_FIELD, (2, XM1, N...  2.25 us
    pallas_call x1, Pallas kernels, per_device(): call(block_kernel, 'block', 4, [(6,) + FULL, FULL, FULL, (4, NX, NY), (2,...  1.66 us
  transfers between devices with their start and end apart: 14, of which 5 were waited for; matrix products, arithmetic and copies ran while one was open for 0% of the time, Pallas kernels for 3%

profile of v5, /device:TPU:283, one launch (start us, length us, event | category | flops | bytes accessed | tf_op | source)
XLA Modules:
  0.0 81.4 jit_solution(14191042453385748374)
XLA Ops:
  0.0 2.3 %x_faces.1 = (f32[32,32,128]{2,1,0:T(8,128)S(1)}, f32[32,32,128]{2,1,0:T(8,128)S(1)}, f32[32,32,128]{2,1,0:T(8,128)S(1)}, bf16[3,32,32,128]{3,2,1,0:T(8,128)(2,1...) custom-call(f32[32,32,128]{2,1,0:T(8,128)} %u_far.1, ...), custom_call_target="tpu_custom_call" | custom-call | bytes 6000000 | tf_op jit(solution)/shard_map/x_faces/pallas_call | solution.py:559
  2.3 15.1 %collective-permute-start = (f32[104,128]{1,0:T(8,128)S(1)}, f32[104,128]{1,0:T(8,128)S(1)}, u32[]{:S(2)}, u32[]{:S(2)}) collective-permute-start(f32[104,128]{1,0:T(8,128)S(1)} %get-tuple-element.56), channel_id=1, source_target_pairs={{64,128},{128,64},{192,256},{256,192},{320,384},{384,320},{448,512... | collective-permute-start | bytes 159752 | tf_op jit(solution)/shard_map/ppermute | solution.py:552
  17.4 1.9 %collective-permute-start.1 = (f32[104,128]{1,0:T(8,128)S(1)}, f32[104,128]{1,0:T(8,128)S(1)}, u32[]{:S(2)}, u32[]{:S(2)}) collective-permute-start(f32[104,128]{1,0:T(8,128)S(1)} %get-tuple-element.57), channel_id=1, source_target_pairs={{0,64},{64,0},{128,192},{192,128},{256,320},{320,256},{384,448},{4... | collective-permute-start | bytes 159752 | tf_op jit(solution)/shard_map/ppermute | solution.py:552
  19.3 2.2 %collective-permute-start.2 = (f32[32,128]{1,0:T(8,128)S(1)}, f32[32,128]{1,0:T(8,128)S(1)}, u32[]{:S(2)}, u32[]{:S(2)}) collective-permute-start(f32[32,128]{1,0:T(8,128)S(1)} %get-tuple-element.58), channel_id=1, source_target_pairs={{0,1},{1,0},{2,3},{3,2},{4,5},{5,4},{6,7},{7,6},{8,9},{9,8},{10,11... | collective-permute-start | bytes 49160 | tf_op jit(solution)/shard_map/ppermute | solution.py:552
  21.5 3.8 %collective-permute-start.3 = (f32[32,128]{1,0:T(8,128)S(1)}, f32[32,128]{1,0:T(8,128)S(1)}, u32[]{:S(2)}, u32[]{:S(2)}) collective-permute-start(f32[32,128]{1,0:T(8,128)S(1)} %get-tuple-element.59), channel_id=1, source_target_pairs={{1,2},{2,1},{5,6},{6,5},{9,10},{10,9},{13,14},{14,13},{17,18},{18,... | collective-permute-start | bytes 49160 | tf_op jit(solution)/shard_map/ppermute | solution.py:552
  25.3 1.7 %block.1 = (f32[6,32,32,128]{3,2,1,0:T(8,128)S(1)}, f32[32,32,128]{2,1,0:T(8,128)S(1)}, f32[32,32,128]{2,1,0:T(8,128)S(1)}, f32[4,32,128]{2,1,0:T(8,128)S(1)}, f...) custom-call(f32[32,32,128]{2,1,0:T(8,128)S(1)} %get-tuple-element.45.u, f32[32,32,128]{2,1,0:T(8,128)S(1)} %get-tuple-element.46.f, ...), custom_call_target="tpu_custom_call" | custom-call | bytes 7500000 | tf_op jit(solution)/shard_map/block/pallas_call | solution.py:564
  27.2 1.9 %collective-permute-start.5 = (f32[104,128]{1,0:T(8,128)S(1)}, f32[104,128]{1,0:T(8,128)S(1)}, u32[]{:S(2)}, u32[]{:S(2)}) collective-permute-start(f32[104,128]{1,0:T(8,128)S(1)} %get-tuple-element.63), channel_id=1, source_target_pairs={{0,1},{1,0},{2,3},{3,2},{4,5},{5,4},{6,7},{7,6},{8,9},{9,8},{10,11... | collective-permute-start | bytes 159752 | tf_op jit(solution)/shard_map/ppermute | solution.py:552
  29.1 2.8 %collective-permute-start.6 = (f32[104,128]{1,0:T(8,128)S(1)}, f32[104,128]{1,0:T(8,128)S(1)}, u32[]{:S(2)}, u32[]{:S(2)}) collective-permute-start(f32[104,128]{1,0:T(8,128)S(1)} %get-tuple-element.64), channel_id=1, source_target_pairs={{1,2},{2,1},{5,6},{6,5},{9,10},{10,9},{13,14},{14,13},{17,18},{18,... | collective-permute-start | bytes 159752 | tf_op jit(solution)/shard_map/ppermute | solution.py:552
  31.9 5.2 %collective-permute-start.4 = (f32[40,128]{1,0:T(8,128)S(1)}, f32[40,128]{1,0:T(8,128)S(1)}, u32[]{:S(2)}, u32[]{:S(2)}) collective-permute-start(f32[40,128]{1,0:T(8,128)S(1)} %get-tuple-element.62), channel_id=1, source_target_pairs={{4,8},{8,4},{12,16},{16,12},{20,24},{24,20},{28,32},{32,28},{36,40... | collective-permute-start | bytes 61448 | tf_op jit(solution)/shard_map/ppermute | solution.py:552
  37.1 1.9 %collective-permute-start.7 = (f32[40,128]{1,0:T(8,128)S(1)}, f32[40,128]{1,0:T(8,128)S(1)}, u32[]{:S(2)}, u32[]{:S(2)}) collective-permute-start(f32[40,128]{1,0:T(8,128)S(1)} %get-tuple-element.65), channel_id=1, source_target_pairs={{0,4},{4,0},{8,12},{12,8},{16,20},{20,16},{24,28},{28,24},{32,36},... | collective-permute-start | bytes 61448 | tf_op jit(solution)/shard_map/ppermute | solution.py:552
  39.0 1.1 %collective-permute-done.7.yeven = f32[40,128]{1,0:T(8,128)S(1)} collective-permute-done((f32[40,128]{1,0:T(8,128)S(1)}, f32[40,128]{1,0:T(8,128)S(1)}, u32[]{:S(2)}, u32[]{:S(2)}) %collective-permute-start.7) | collective-permute-done | bytes 20512 | tf_op jit(solution)/shard_map/ppermute | solution.py:552
  40.2 2.3 %two_steps.1 = (f32[2,136,128]{2,1,0:T(8,128)S(1)}, f32[2,40,128]{2,1,0:T(8,128)S(1)}, f32[32,32,128]{2,1,0:T(8,128)S(1)}, f32[32,32,128]{2,1,0:T(8,128)S(1)}, f...) custom-call(f32[32,32,128]{2,1,0:T(8,128)S(1)} %get-tuple-element.45, ...), custom_call_target="tpu_custom_call" | custom-call | bytes 6000000 | tf_op jit(solution)/shard_map/two_steps/pallas_call | solution.py:576
  42.5 13.6 %collective-permute-start.8 = (f32[80,128]{1,0:T(8,128)S(1)}, f32[80,128]{1,0:T(8,128)S(1)}, u32[]{:S(2)}, u32[]{:S(2)}) collective-permute-start(f32[80,128]{1,0:T(8,128)S(1)} %get-tuple-element.75), channel_id=1, source_target_pairs={{64,128},{128,64},{192,256},{256,192},{320,384},{384,320},{448,512... | collective-permute-start | bytes 122888 | tf_op jit(solution)/shard_map/ppermute | solution.py:552
  56.1 1.9 %collective-permute-start.9 = (f32[80,128]{1,0:T(8,128)S(1)}, f32[80,128]{1,0:T(8,128)S(1)}, u32[]{:S(2)}, u32[]{:S(2)}) collective-permute-start(f32[80,128]{1,0:T(8,128)S(1)} %get-tuple-element.76), channel_id=1, source_target_pairs={{0,64},{64,0},{128,192},{192,128},{256,320},{320,256},{384,448},{4... | collective-permute-start | bytes 122888 | tf_op jit(solution)/shard_map/ppermute | solution.py:552
  58.0 1.1 %block_2.1 = (f32[32,32,128]{2,1,0:T(8,128)S(1)}, f32[2,64,128]{2,1,0:T(8,128)S(1)}, f32[64,128]{1,0:T(8,128)S(1)}) custom-call(f32[6,32,32,128]{3,2,1,0:T(8,128)S(1)} %get-tuple-element.49.g, f32[32,32,128]{2,1,0:T(8,128)S(1)} %get-tuple-element.66.s1, f32[32,32,128]{2,1,0:T(8,128)S(1)} %get-tuple-element.67.d.d1), custom_call_target="tpu_custom_call" | custom-call | bytes 4500000 | tf_op jit(solution)/shard_map/block_2/pallas_call | solution.py:581
  59.1 2.0 %collective-permute-done.9.xeven = f32[80,128]{1,0:T(8,128)S(1)} collective-permute-done((f32[80,128]{1,0:T(8,128)S(1)}, f32[80,128]{1,0:T(8,128)S(1)}, u32[]{:S(2)}, u32[]{:S(2)}) %collective-permute-start.9) | collective-permute-done | bytes 40992 | tf_op jit(solution)/shard_map/ppermute | solution.py:552
  61.2 1.9 %collective-permute-start.10 = (f32[88,128]{1,0:T(8,128)S(1)}, f32[88,128]{1,0:T(8,128)S(1)}, u32[]{:S(2)}, u32[]{:S(2)}) collective-permute-start(f32[88,128]{1,0:T(8,128)S(1)} %get-tuple-element.79), channel_id=1, source_target_pairs={{0,1},{1,0},{2,3},{3,2},{4,5},{5,4},{6,7},{7,6},{8,9},{9,8},{10,11... | collective-permute-start | bytes 135176 | tf_op jit(solution)/shard_map/ppermute | solution.py:552
  63.2 1.9 %collective-permute-start.11 = (f32[88,128]{1,0:T(8,128)S(1)}, f32[88,128]{1,0:T(8,128)S(1)}, u32[]{:S(2)}, u32[]{:S(2)}) collective-permute-start(f32[88,128]{1,0:T(8,128)S(1)} %get-tuple-element.80), channel_id=1, source_target_pairs={{1,2},{2,1},{5,6},{6,5},{9,10},{10,9},{13,14},{14,13},{17,18},{18,... | collective-permute-start | bytes 135176 | tf_op jit(solution)/shard_map/ppermute | solution.py:552
  65.1 0.9 %collective-permute-done.10.zeven = f32[88,128]{1,0:T(8,128)S(1)} collective-permute-done((f32[88,128]{1,0:T(8,128)S(1)}, f32[88,128]{1,0:T(8,128)S(1)}, u32[]{:S(2)}, u32[]{:S(2)}) %collective-permute-start.10) | collective-permute-done | bytes 45088 | tf_op jit(solution)/shard_map/ppermute | solution.py:552
  66.0 1.9 %collective-permute-done.11.zodd = f32[88,128]{1,0:T(8,128)S(1)} collective-permute-done((f32[88,128]{1,0:T(8,128)S(1)}, f32[88,128]{1,0:T(8,128)S(1)}, u32[]{:S(2)}, u32[]{:S(2)}) %collective-permute-start.11) | collective-permute-done | bytes 45088 | tf_op jit(solution)/shard_map/ppermute | solution.py:552
  68.2 7.5 %collective-permute-start.12 = (f32[56,128]{1,0:T(8,128)S(1)}, f32[56,128]{1,0:T(8,128)S(1)}, u32[]{:S(2)}, u32[]{:S(2)}) collective-permute-start(f32[56,128]{1,0:T(8,128)S(1)} %get-tuple-element.83), channel_id=1, source_target_pairs={{4,8},{8,4},{12,16},{16,12},{20,24},{24,20},{28,32},{32,28},{36,40... | collective-permute-start | bytes 86024 | tf_op jit(solution)/shard_map/ppermute | solution.py:552
  75.6 1.9 %collective-permute-start.13 = (f32[56,128]{1,0:T(8,128)S(1)}, f32[56,128]{1,0:T(8,128)S(1)}, u32[]{:S(2)}, u32[]{:S(2)}) collective-permute-start(f32[56,128]{1,0:T(8,128)S(1)} %get-tuple-element.84), channel_id=1, source_target_pairs={{0,4},{4,0},{8,12},{12,8},{16,20},{20,16},{24,28},{28,24},{32,36},... | collective-permute-start | bytes 86024 | tf_op jit(solution)/shard_map/ppermute | solution.py:552
  77.6 1.2 %collective-permute-done.13.yeven = f32[56,128]{1,0:T(8,128)S(1)} collective-permute-done((f32[56,128]{1,0:T(8,128)S(1)}, f32[56,128]{1,0:T(8,128)S(1)}, u32[]{:S(2)}, u32[]{:S(2)}) %collective-permute-start.13) | collective-permute-done | bytes 28704 | tf_op jit(solution)/shard_map/ppermute | solution.py:552
  78.7 2.7 %last_steps.1 = f32[32,32,128]{2,1,0:T(8,128)} custom-call(f32[6,32,32,128]{3,2,1,0:T(8,128)S(1)} %get-tuple-element.49.g, f32[32,32,128]{2,1,0:T(8,128)S(1)} %get-tuple-element.68.s2, f32[32,32,128]{2,1,0:T(8,128)S(1)} %get-tuple-element.67.d.d1, f32[32,32,128]{2,1,0:T(8,128)S(1)} %get-tuple-element.69.acc, f32[2,128,128]{2,1,0:T(8,128)S(1)} %get-tuple-element.53.zp, ...), custom_call_target="tpu_custom_call" | custom-call | bytes 7500000 | tf_op jit(solution)/shard_map/last_steps/pallas_call | solution.py:593
  (12 shorter events, 0.6 us)
Async XLA Ops:
  2.3 24.7 %collective-permute-start = (f32[104,128]{1,0:T(8,128)S(1)}, f32[104,128]{1,0:T(8,128)S(1)}, u32[]{:S(2)}, u32[]{:S(2)}) collective-permute-start(f32[104,128]{1,0:T(8,128)S(1)} %get-tuple-element.56), channel_id=1, source_target_pairs={{64,128},{128,64},{192,256},{256,192},{320,384},{384,320},{448,512... | collective-permute-start | bytes 159752 | tf_op jit(solution)/shard_map/ppermute | solution.py:552
  17.4 9.6 %collective-permute-start.1 = (f32[104,128]{1,0:T(8,128)S(1)}, f32[104,128]{1,0:T(8,128)S(1)}, u32[]{:S(2)}, u32[]{:S(2)}) collective-permute-start(f32[104,128]{1,0:T(8,128)S(1)} %get-tuple-element.57), channel_id=1, source_target_pairs={{0,64},{64,0},{128,192},{192,128},{256,320},{320,256},{384,448},{4... | collective-permute-start | bytes 159752 | tf_op jit(solution)/shard_map/ppermute | solution.py:552
  19.3 7.6 %collective-permute-start.2 = (f32[32,128]{1,0:T(8,128)S(1)}, f32[32,128]{1,0:T(8,128)S(1)}, u32[]{:S(2)}, u32[]{:S(2)}) collective-permute-start(f32[32,128]{1,0:T(8,128)S(1)} %get-tuple-element.58), channel_id=1, source_target_pairs={{0,1},{1,0},{2,3},{3,2},{4,5},{5,4},{6,7},{7,6},{8,9},{9,8},{10,11... | collective-permute-start | bytes 49160 | tf_op jit(solution)/shard_map/ppermute | solution.py:552
  21.5 5.5 %collective-permute-start.3 = (f32[32,128]{1,0:T(8,128)S(1)}, f32[32,128]{1,0:T(8,128)S(1)}, u32[]{:S(2)}, u32[]{:S(2)}) collective-permute-start(f32[32,128]{1,0:T(8,128)S(1)} %get-tuple-element.59), channel_id=1, source_target_pairs={{1,2},{2,1},{5,6},{6,5},{9,10},{10,9},{13,14},{14,13},{17,18},{18,... | collective-permute-start | bytes 49160 | tf_op jit(solution)/shard_map/ppermute | solution.py:552
  27.2 13.0 %collective-permute-start.5 = (f32[104,128]{1,0:T(8,128)S(1)}, f32[104,128]{1,0:T(8,128)S(1)}, u32[]{:S(2)}, u32[]{:S(2)}) collective-permute-start(f32[104,128]{1,0:T(8,128)S(1)} %get-tuple-element.63), channel_id=1, source_target_pairs={{0,1},{1,0},{2,3},{3,2},{4,5},{5,4},{6,7},{7,6},{8,9},{9,8},{10,11... | collective-permute-start | bytes 159752 | tf_op jit(solution)/shard_map/ppermute | solution.py:552
  29.1 11.1 %collective-permute-start.6 = (f32[104,128]{1,0:T(8,128)S(1)}, f32[104,128]{1,0:T(8,128)S(1)}, u32[]{:S(2)}, u32[]{:S(2)}) collective-permute-start(f32[104,128]{1,0:T(8,128)S(1)} %get-tuple-element.64), channel_id=1, source_target_pairs={{1,2},{2,1},{5,6},{6,5},{9,10},{10,9},{13,14},{14,13},{17,18},{18,... | collective-permute-start | bytes 159752 | tf_op jit(solution)/shard_map/ppermute | solution.py:552
  31.9 7.1 %collective-permute-start.4 = (f32[40,128]{1,0:T(8,128)S(1)}, f32[40,128]{1,0:T(8,128)S(1)}, u32[]{:S(2)}, u32[]{:S(2)}) collective-permute-start(f32[40,128]{1,0:T(8,128)S(1)} %get-tuple-element.62), channel_id=1, source_target_pairs={{4,8},{8,4},{12,16},{16,12},{20,24},{24,20},{28,32},{32,28},{36,40... | collective-permute-start | bytes 61448 | tf_op jit(solution)/shard_map/ppermute | solution.py:552
  37.1 3.1 %collective-permute-start.7 = (f32[40,128]{1,0:T(8,128)S(1)}, f32[40,128]{1,0:T(8,128)S(1)}, u32[]{:S(2)}, u32[]{:S(2)}) collective-permute-start(f32[40,128]{1,0:T(8,128)S(1)} %get-tuple-element.65), channel_id=1, source_target_pairs={{0,4},{4,0},{8,12},{12,8},{16,20},{20,16},{24,28},{28,24},{32,36},... | collective-permute-start | bytes 61448 | tf_op jit(solution)/shard_map/ppermute | solution.py:552
  42.5 16.6 %collective-permute-start.8 = (f32[80,128]{1,0:T(8,128)S(1)}, f32[80,128]{1,0:T(8,128)S(1)}, u32[]{:S(2)}, u32[]{:S(2)}) collective-permute-start(f32[80,128]{1,0:T(8,128)S(1)} %get-tuple-element.75), channel_id=1, source_target_pairs={{64,128},{128,64},{192,256},{256,192},{320,384},{384,320},{448,512... | collective-permute-start | bytes 122888 | tf_op jit(solution)/shard_map/ppermute | solution.py:552
  56.1 5.0 %collective-permute-start.9 = (f32[80,128]{1,0:T(8,128)S(1)}, f32[80,128]{1,0:T(8,128)S(1)}, u32[]{:S(2)}, u32[]{:S(2)}) collective-permute-start(f32[80,128]{1,0:T(8,128)S(1)} %get-tuple-element.76), channel_id=1, source_target_pairs={{0,64},{64,0},{128,192},{192,128},{256,320},{320,256},{384,448},{4... | collective-permute-start | bytes 122888 | tf_op jit(solution)/shard_map/ppermute | solution.py:552
  61.2 4.8 %collective-permute-start.10 = (f32[88,128]{1,0:T(8,128)S(1)}, f32[88,128]{1,0:T(8,128)S(1)}, u32[]{:S(2)}, u32[]{:S(2)}) collective-permute-start(f32[88,128]{1,0:T(8,128)S(1)} %get-tuple-element.79), channel_id=1, source_target_pairs={{0,1},{1,0},{2,3},{3,2},{4,5},{5,4},{6,7},{7,6},{8,9},{9,8},{10,11... | collective-permute-start | bytes 135176 | tf_op jit(solution)/shard_map/ppermute | solution.py:552
  63.2 4.8 %collective-permute-start.11 = (f32[88,128]{1,0:T(8,128)S(1)}, f32[88,128]{1,0:T(8,128)S(1)}, u32[]{:S(2)}, u32[]{:S(2)}) collective-permute-start(f32[88,128]{1,0:T(8,128)S(1)} %get-tuple-element.80), channel_id=1, source_target_pairs={{1,2},{2,1},{5,6},{6,5},{9,10},{10,9},{13,14},{14,13},{17,18},{18,... | collective-permute-start | bytes 135176 | tf_op jit(solution)/shard_map/ppermute | solution.py:552
  68.2 9.4 %collective-permute-start.12 = (f32[56,128]{1,0:T(8,128)S(1)}, f32[56,128]{1,0:T(8,128)S(1)}, u32[]{:S(2)}, u32[]{:S(2)}) collective-permute-start(f32[56,128]{1,0:T(8,128)S(1)} %get-tuple-element.83), channel_id=1, source_target_pairs={{4,8},{8,4},{12,16},{16,12},{20,24},{24,20},{28,32},{32,28},{36,40... | collective-permute-start | bytes 86024 | tf_op jit(solution)/shard_map/ppermute | solution.py:552
  75.6 3.1 %collective-permute-start.13 = (f32[56,128]{1,0:T(8,128)S(1)}, f32[56,128]{1,0:T(8,128)S(1)}, u32[]{:S(2)}, u32[]{:S(2)}) collective-permute-start(f32[56,128]{1,0:T(8,128)S(1)} %get-tuple-element.84), channel_id=1, source_target_pairs={{0,4},{4,0},{8,12},{12,8},{16,20},{20,16},{24,28},{28,24},{32,36},... | collective-permute-start | bytes 86024 | tf_op jit(solution)/shard_map/ppermute | solution.py:552

commit v6 on v5

--- a/solution.py
+++ b/solution.py
@@ -98,13 +98,18 @@
     return total
 
 
-def from_faces(z, zp, xp, yp):
-    row, lane = plane()
-    total = jnp.where(ends(lane), pltpu.roll(yp, lax.rem(NY - 4 * z, NY), 1), 0.0)
-    total += jnp.where(row == 0, xp[0, pl.ds(z, 1), :], 0.0)
-    total += jnp.where(row == NX - 1, xp[1, pl.ds(z, 1), :], 0.0)
-    total += jnp.where(z == 0, zp[0], 0.0) + jnp.where(z == NZ - 1, zp[1], 0.0)
-    return total
+def from_faces(z, xp, yp):
+    row8 = iota((8, NY), 0)
+    total = jnp.where(ends(iota((NX, NY), 1)), pltpu.roll(yp, lax.rem(NY - 4 * z, NY), 1), 0.0)
+    first = total[0:8] + jnp.where(row8 == 0, xp[0, pl.ds(z, 1), :], 0.0)
+    last = total[NX - 8 :] + jnp.where(row8 == 7, xp[1, pl.ds(z, 1), :], 0.0)
+    return jnp.concatenate([first, total[8 : NX - 8], last], axis=0)
+
+
+def from_faces_rows(z, xp, yp, side):
+    rows, r = face_rows(side)
+    total = jnp.where(ends(iota((8, NY), 1)), pltpu.roll(yp[rows], lax.rem(NY - 4 * z, NY), 1), 0.0)
+    return total + jnp.where(iota((8, NY), 0) == r, xp[side, pl.ds(z, 1), :], 0.0)
 
 
 def couplings(perm, speeds):
@@ -175,7 +180,7 @@
     for part in range(4):
         for copy in copies[part][1:]:
             copy.wait()
-        edges = lax.fori_loop(8 * part, 8 * part + 8, layer, edges, unroll=4)
+        edges = lax.fori_loop(8 * part, 8 * part + 8, layer, edges, unroll=8)
     for side in (0, 1):
         _, r = face_rows(side)
         xp[side, 96:104, :] = jnp.zeros((8, NY), F32)
@@ -215,7 +220,7 @@
         return pu, ps, pg
 
     zero = jnp.zeros((NX, NY), F32)
-    pu, ps, pg = lax.fori_loop(0, NZ, layer, (zero, zero, zero), unroll=4)
+    pu, ps, pg = lax.fori_loop(0, NZ, layer, (zero, zero, zero), unroll=8)
     yp[0:32, :] = pu
     yp[32:64, :] = ps
     yp[64:96, :] = pg
@@ -315,8 +320,8 @@
 
 def second_kernel(
     u, g, diag, s1, perm_sum, zp, yp, xp, xh, zu, yodd, zeven, zodd, yeven,
-    zh, yh, s, d, acc, b, xp2, even, odd,
-    zin, s0, d0, cross, cross2, rsum, rows, stage,
+    zh, yh, s0, d0, b, xp2, cross2, zy2, even, odd,
+    zin, cross, rsum, rows, edge_s, edge_d, stage,
 ):
     take_in(yh, yeven, yodd, "gy")
     take_in(zin, zeven, zodd, "gz")
@@ -328,23 +333,28 @@
     own_y = yp[64:96, :]
     yq = own_y * combine(low, high, 0)
     yq2 = own_y * (scale * (combine(low, high, 1) + combine(low, high, 2) * yp[0:32, :]))
-    zq, zq2 = [], []
+    zy2[2] = yq2
+    zq = []
     for side, z in ((0, 0), (1, NZ - 1)):
         zq.append(zp[side, 64:96, :] * zh[side, 0:32, :])
-        zq2.append(zp[side, 64:96, :] * (scale * z_halo_residual(side, zh[side, 32:64, :], zh, yh, u[z])))
+        zy2[side] = zp[side, 64:96, :] * (scale * z_halo_residual(side, zh[side, 32:64, :], zh, yh, u[z]))
         gx = xp[side, 64:96, :]
         cross[side] = gx * xh[side, 0:32, :]
         cross2[side] = gx * (scale * x_halo_residual(side, xh[side, 32:64, :], xh, zh, 128, yh, xp[side, 0:32, :]))
     rsum[...] = jnp.zeros_like(rsum)
 
     def start(z, carry):
-        res = s1[z] + from_faces(z, zq, cross, yq)
+        res = s1[z] + from_faces(z, cross, yq)
         s0[z] = res
         d0[z] = res * scale
         rsum[z // 8] += res * diag[z]
         return carry
 
-    lax.fori_loop(0, NZ, start, 0, unroll=8)
+    lax.fori_loop(0, NZ, start, 0, unroll=32)
+    for side, z in ((0, 0), (1, NZ - 1)):
+        s0[z] += zq[side]
+        d0[z] += zq[side] * scale
+        rsum[z // 8] += zq[side] * diag[z]
     for block in range(4):
         rows[0, 4 * block : 4 * block + 4, :] = group_sums(rsum[block])
         rows[1, 4 * block : 4 * block + 4, :] = group_sums(perm_sum[block])
@@ -354,27 +364,34 @@
     rhs = jnp.where(lane16 < 16, (OMEGA * 8.0 / 6.0) * exact_dot(rows[0], select) / weights, 0.0)
     b[...] = rhs
 
-    def step(z, carry):
-        before = d0[z]
-        res = s0[z] - before + own_neighbours(d0, g, z) + from_faces(z, zq2, cross2, yq2)
-        after = A[0] * before + B[0] * res
-        s[z] = res
-        d[z] = after
-        acc[z] = u[z] + before + after
+    def edge(z, carry):
+        for side in (0, 1):
+            at, _ = face_rows(side)
+            before = d0[z, at, :]
+            near = edge_neighbours(lambda k: d0[k, at, :], [g[k, z, at, :] for k in range(6)], z)
+            res = s0[z, at, :] - before + near + from_faces_rows(z, cross2, yq2, side)
+            edge_s[side, z] = res
+            edge_d[side, z] = A[0] * before + B[0] * res
         return carry
 
-    lax.fori_loop(0, NZ, step, 0, unroll=8)
+    lax.fori_loop(0, NZ, edge, 0, unroll=32)
+    for side in (0, 1):
+        at, _ = face_rows(side)
+        for end, z in ((0, 0), (1, NZ - 1)):
+            edge_s[side, z] += zy2[end, at, :]
+            edge_d[side, z] += B[0] * zy2[end, at, :]
 
     def face(z, carry):
         for side in (0, 1):
             at, r = face_rows(side)
-            here = d[z, at, :]
-            res = s[z, at, :] - here + inner_neighbours(d, [g[k, z, at, :] for k in range(6)], z, side)
+            here = edge_d[side, z]
+            near = edge_neighbours(lambda k: edge_d[side, k], [g[k, z, at, :] for k in range(6)], z)
+            res = edge_s[side, z] - here + near
             xp2[side, pl.ds(z, 1), :] = here[r : r + 1]
             xp2[side, pl.ds(NZ + z, 1), :] = res[r : r + 1]
         return carry
 
-    lax.fori_loop(0, NZ, face, 0, unroll=8)
+    lax.fori_loop(0, NZ, face, 0, unroll=32)
     for side in (0, 1):
         stage[side, 0:64, :] = xp2[side]
         for z in range(4):
@@ -383,7 +400,31 @@
     put_out(stage, even, odd, "gx")
 
 
-def second_block_kernel(g, s1, d, s, zp2, yp2):
+def edge_neighbours(rows_of, g, z):
+    here = rows_of(z)
+    total = g[0] * rows_of(jnp.maximum(z - 1, 0)) + g[1] * rows_of(jnp.minimum(z + 1, NZ - 1))
+    total += g[2] * pltpu.roll(here, 1, 0) + g[3] * pltpu.roll(here, 7, 0)
+    return total + g[4] * pltpu.roll(here, 1, 1) + g[5] * pltpu.roll(here, NY - 1, 1)
+
+
+def second_block_kernel(u, g, s0, d0, cross2, zy2, s, d, acc, zp2, yp2, s1):
+    yq2 = zy2[2]
+
+    def step(z, carry):
+        before = d0[z]
+        res = s0[z] - before + own_neighbours(d0, g, z) + from_faces(z, cross2, yq2)
+        after = A[0] * before + B[0] * res
+        s1[z] = res
+        d[z] = after
+        acc[z] = u[z] + before + after
+        return carry
+
+    lax.fori_loop(0, NZ, step, 0, unroll=32)
+    for side, z in ((0, 0), (1, NZ - 1)):
+        s1[z] += zy2[side]
+        d[z] += B[0] * zy2[side]
+        acc[z] += B[0] * zy2[side]
+
     def partial(z, carry):
         pu, ps = carry
         here = d[z]
@@ -486,8 +527,8 @@
 
 def third_kernel(
     g, s2, d1, acc, zp, yp, xp, xh, zh, yh, xp2, zp2, yp2, xh2, zh2, b3, yodd, yeven,
-    out,
-    yh2, s, d, cross, cross2, ext, err, spread,
+    far_out,
+    yh2, s, d, cross, cross2, ext, err, spread, out, sems,
 ):
     take_in(yh2, yeven, yodd, "gy")
     low, high = yh2[0, 0:32, :], yh2[1, 0:32, :]
@@ -508,20 +549,34 @@
     coarse_solve(b3, zh2, yh2, ext, err, spread)
 
     def step(z, carry):
-        res = s2[z] + from_faces(z, zq, cross, yq)
+        res = s2[z] + from_faces(z, cross, yq)
         s[z] = res
         d[z] = A[1] * d1[z] + B[1] * res
         return carry
 
-    lax.fori_loop(0, NZ, step, 0, unroll=8)
+    lax.fori_loop(0, NZ, step, 0, unroll=32)
+    for side, z in ((0, 0), (1, NZ - 1)):
+        s[z] += zq[side]
+        d[z] += B[1] * zq[side]
 
     def finish(z, carry):
         before = d[z]
-        res = s[z] - before + own_neighbours(d, g, z) + from_faces(z, zq2, cross2, yq2)
+        res = s[z] - before + own_neighbours(d, g, z) + from_faces(z, cross2, yq2)
         out[z] = acc[z] + before + (A[2] * before + B[2] * res) + spread[z // 8]
         return carry
 
-    lax.fori_loop(0, NZ, finish, 0, unroll=8)
+    copies = []
+    for part in range(4):
+        lax.fori_loop(8 * part, 8 * part + 8, finish, 0, unroll=8)
+        if part == 0:
+            out[0] += B[2] * zq2[0]
+        if part == 3:
+            out[NZ - 1] += B[2] * zq2[1]
+        rows = pl.ds(8 * part, 8)
+        copies.append(pltpu.make_async_copy(out.at[rows], far_out.at[rows], sems.at[part]))
+        copies[part].start()
+    for copy in copies:
+        copy.wait()
 
 
 VM = pl.BlockSpec(memory_space=pltpu.VMEM)
@@ -529,12 +584,12 @@
 BF16_FIELD = jax.ShapeDtypeStruct((3,) + FULL, jnp.bfloat16)
 
 
-def call(kernel, name, n_in, outs, scratch=(), us=0.2, place=VM, more=()):
+def call(kernel, name, n_in, outs, scratch=(), us=0.2, place=VM, more=(), results=VM):
     return pl.pallas_call(
         kernel,
         out_shape=[x if isinstance(x, jax.ShapeDtypeStruct) else jax.ShapeDtypeStruct(x, F32) for x in outs],
         in_specs=[place] * n_in,
-        out_specs=[VM] * len(outs),
+        out_specs=[results] * len(outs),
         scratch_shapes=[pltpu.VMEM(shape, F32) for shape in scratch] + list(more),
         compiler_params=pltpu.CompilerParams(vmem_limit_bytes=32 * 2**20),
         cost_estimate=pl.CostEstimate(flops=0, transcendentals=0, bytes_accessed=int(us * 3e6)),
@@ -573,14 +628,14 @@
     )(odd, even, zeven, zodd, xp, zp, yp)
     zeven, zodd = swap(zeven, zodd, "gz")
     yeven, yodd = swap(yeven, yodd, "gy")
-    zh, yh, s, d1, acc, b, xp2, even, odd = call(
+    zh, yh, s, d, b, xp2, cross2, zy2, even, odd = call(
         second_kernel, "two_steps", 14,
-        [(2, ZH1, NY), (2, YM1, NY), FULL, FULL, FULL, (16, NY), (2, 64, NY), (XM2, NY), (XM2, NY)],
-        [(2, ZM1, NY), FULL, FULL, face, face, (4, NX, NY), (2, 16, NY), (2, XM2, NY)], 2.0,
+        [(2, ZH1, NY), (2, YM1, NY), FULL, FULL, (16, NY), (2, 64, NY), face, (3, NX, NY), (XM2, NY), (XM2, NY)],
+        [(2, ZM1, NY), face, (4, NX, NY), (2, 16, NY), (2, NZ, 8, NY), (2, NZ, 8, NY), (2, XM2, NY)], 1.5,
     )(u, g, diag, s, perm_sum, zp, yp, xp, xh, zu, yodd, zeven, zodd, yeven)
-    s, zp2, yp2 = call(
-        second_block_kernel, "block_2", 3, [FULL, (2, 64, NY), (64, NY)], (), 1.5
-    )(g, s, d1)
+    s, d1, acc, zp2, yp2 = call(
+        second_block_kernel, "block_2", 6, [FULL, FULL, FULL, (2, 64, NY), (64, NY)], [FULL], 2.0
+    )(u, g, s, d, cross2, zy2)
     even, odd = swap(even, odd, "gx")
     xh2, even, odd, b3 = call(
         second_z_kernel, "z_message_2", 5, [(2, XM2, NY), (ZM2, NY), (ZM2, NY), (16, NY)], [(2, ZM2, NY), (16, NY)]
@@ -592,7 +647,8 @@
     even, odd = swap(even, odd, "gy")
     (out,) = call(
         third_kernel, "last_steps", 18, [FULL],
-        [(2, YM2, NY), FULL, FULL, face, face, (10, 16, NY), (16, NY), (4, NX, NY)], 2.5,
+        [(2, YM2, NY), FULL, FULL, face, face, (10, 16, NY), (16, NY), (4, NX, NY), FULL], 2.5, VM,
+        [pltpu.SemaphoreType.DMA((4,))], HBM,
     )(g, s, d1, acc, zp, yp, xp, xh, zh, yh, xp2, zp2, yp2, xh2, zh2, b3, odd, even)
     return out
 

time: 81.8 us -> 79.3 us (0.969)
  Pallas kernels: 10.5 us -> 8.33 us
    pallas_call x1, Pallas kernels: 2.31 us -> 0.81 us  [per_device(): call(second_kernel, 'two_steps', 14, [(2, ZH1, NY), (2, YM1, NY), FULL, F...]
  transfers between devices with their start and end apart: 14 -> 14, of which waited for: 5 -> 5; matrix products, arithmetic and copies ran while one was open for 0% -> 0% of each run, Pallas kernels for 3% -> 4%
where the time goes in v6:
time: 79.3 us; the launch traced here: 78.8 us
  starting transfers between devices  63.7 us (80%)
  Pallas kernels  8.33 us (11%)
  waiting for transfers between devices  6.6 us (8%)
    ppermute x14, starting transfers between devices, swap(): results.append(lax.ppermute(values, axis, pairs))  63.7 us
    ppermute x14, waiting for transfers between devices, swap(): results.append(lax.ppermute(values, axis, pairs))  6.6 us
    pallas_call x1, Pallas kernels, per_device(): call(face_kernel, 'x_faces', 4, [FULL, FULL, FULL, BF16_FIELD, (2, XM1, N...  1.95 us
    pallas_call x1, Pallas kernels, per_device(): call(third_kernel, 'last_steps', 18, [FULL], [(2, YM2, NY), FULL, FULL, f...  1.87 us
    pallas_call x1, Pallas kernels, per_device(): call(second_block_kernel, 'block_2', 6, [FULL, FULL, FULL, (2, 64, NY), (...  1.68 us
  transfers between devices with their start and end apart: 14, of which 5 were waited for; matrix products, arithmetic and copies ran while one was open for 0% of the time, Pallas kernels for 4%

profile of v6, /device:TPU:283, one launch (start us, length us, event | category | flops | bytes accessed | tf_op | source)
XLA Modules:
  0.0 78.8 jit_solution(593850379472337539)
XLA Ops:
  0.0 2.0 %x_faces.1 = (f32[32,32,128]{2,1,0:T(8,128)S(1)}, f32[32,32,128]{2,1,0:T(8,128)S(1)}, f32[32,32,128]{2,1,0:T(8,128)S(1)}, bf16[3,32,32,128]{3,2,1,0:T(8,128)(2,1...) custom-call(f32[32,32,128]{2,1,0:T(8,128)} %u_far.1, ...), custom_call_target="tpu_custom_call" | custom-call | bytes 6000000 | tf_op jit(solution)/shard_map/x_faces/pallas_call | solution.py:614
  2.0 15.1 %collective-permute-start = (f32[104,128]{1,0:T(8,128)S(1)}, f32[104,128]{1,0:T(8,128)S(1)}, u32[]{:S(2)}, u32[]{:S(2)}) collective-permute-start(f32[104,128]{1,0:T(8,128)S(1)} %get-tuple-element.59), channel_id=1, source_target_pairs={{64,128},{128,64},{192,256},{256,192},{320,384},{384,320},{448,512... | collective-permute-start | bytes 159752 | tf_op jit(solution)/shard_map/ppermute | solution.py:607
  17.1 1.9 %collective-permute-start.1 = (f32[104,128]{1,0:T(8,128)S(1)}, f32[104,128]{1,0:T(8,128)S(1)}, u32[]{:S(2)}, u32[]{:S(2)}) collective-permute-start(f32[104,128]{1,0:T(8,128)S(1)} %get-tuple-element.60), channel_id=1, source_target_pairs={{0,64},{64,0},{128,192},{192,128},{256,320},{320,256},{384,448},{4... | collective-permute-start | bytes 159752 | tf_op jit(solution)/shard_map/ppermute | solution.py:607
  19.0 2.2 %collective-permute-start.2 = (f32[32,128]{1,0:T(8,128)S(1)}, f32[32,128]{1,0:T(8,128)S(1)}, u32[]{:S(2)}, u32[]{:S(2)}) collective-permute-start(f32[32,128]{1,0:T(8,128)S(1)} %get-tuple-element.61), channel_id=1, source_target_pairs={{0,1},{1,0},{2,3},{3,2},{4,5},{5,4},{6,7},{7,6},{8,9},{9,8},{10,11... | collective-permute-start | bytes 49160 | tf_op jit(solution)/shard_map/ppermute | solution.py:607
  21.2 3.8 %collective-permute-start.3 = (f32[32,128]{1,0:T(8,128)S(1)}, f32[32,128]{1,0:T(8,128)S(1)}, u32[]{:S(2)}, u32[]{:S(2)}) collective-permute-start(f32[32,128]{1,0:T(8,128)S(1)} %get-tuple-element.62), channel_id=1, source_target_pairs={{1,2},{2,1},{5,6},{6,5},{9,10},{10,9},{13,14},{14,13},{17,18},{18,... | collective-permute-start | bytes 49160 | tf_op jit(solution)/shard_map/ppermute | solution.py:607
  25.0 1.5 %block.1 = (f32[6,32,32,128]{3,2,1,0:T(8,128)S(1)}, f32[32,32,128]{2,1,0:T(8,128)S(1)}, f32[32,32,128]{2,1,0:T(8,128)S(1)}, f32[4,32,128]{2,1,0:T(8,128)S(1)}, f...) custom-call(f32[32,32,128]{2,1,0:T(8,128)S(1)} %get-tuple-element.48.u, f32[32,32,128]{2,1,0:T(8,128)S(1)} %get-tuple-element.49.f, ...), custom_call_target="tpu_custom_call" | custom-call | bytes 7500000 | tf_op jit(solution)/shard_map/block/pallas_call | solution.py:619
  26.7 1.9 %collective-permute-start.5 = (f32[104,128]{1,0:T(8,128)S(1)}, f32[104,128]{1,0:T(8,128)S(1)}, u32[]{:S(2)}, u32[]{:S(2)}) collective-permute-start(f32[104,128]{1,0:T(8,128)S(1)} %get-tuple-element.66), channel_id=1, source_target_pairs={{0,1},{1,0},{2,3},{3,2},{4,5},{5,4},{6,7},{7,6},{8,9},{9,8},{10,11... | collective-permute-start | bytes 159752 | tf_op jit(solution)/shard_map/ppermute | solution.py:607
  28.6 3.0 %collective-permute-start.6 = (f32[104,128]{1,0:T(8,128)S(1)}, f32[104,128]{1,0:T(8,128)S(1)}, u32[]{:S(2)}, u32[]{:S(2)}) collective-permute-start(f32[104,128]{1,0:T(8,128)S(1)} %get-tuple-element.67), channel_id=1, source_target_pairs={{1,2},{2,1},{5,6},{6,5},{9,10},{10,9},{13,14},{14,13},{17,18},{18,... | collective-permute-start | bytes 159752 | tf_op jit(solution)/shard_map/ppermute | solution.py:607
  31.6 5.2 %collective-permute-start.4 = (f32[40,128]{1,0:T(8,128)S(1)}, f32[40,128]{1,0:T(8,128)S(1)}, u32[]{:S(2)}, u32[]{:S(2)}) collective-permute-start(f32[40,128]{1,0:T(8,128)S(1)} %get-tuple-element.65), channel_id=1, source_target_pairs={{4,8},{8,4},{12,16},{16,12},{20,24},{24,20},{28,32},{32,28},{36,40... | collective-permute-start | bytes 61448 | tf_op jit(solution)/shard_map/ppermute | solution.py:607
  36.8 1.9 %collective-permute-start.7 = (f32[40,128]{1,0:T(8,128)S(1)}, f32[40,128]{1,0:T(8,128)S(1)}, u32[]{:S(2)}, u32[]{:S(2)}) collective-permute-start(f32[40,128]{1,0:T(8,128)S(1)} %get-tuple-element.68), channel_id=1, source_target_pairs={{0,4},{4,0},{8,12},{12,8},{16,20},{20,16},{24,28},{28,24},{32,36},... | collective-permute-start | bytes 61448 | tf_op jit(solution)/shard_map/ppermute | solution.py:607
  38.7 1.1 %collective-permute-done.7.yeven = f32[40,128]{1,0:T(8,128)S(1)} collective-permute-done((f32[40,128]{1,0:T(8,128)S(1)}, f32[40,128]{1,0:T(8,128)S(1)}, u32[]{:S(2)}, u32[]{:S(2)}) %collective-permute-start.7) | collective-permute-done | bytes 20512 | tf_op jit(solution)/shard_map/ppermute | solution.py:607
  39.9 0.8 %two_steps.1 = (f32[2,136,128]{2,1,0:T(8,128)S(1)}, f32[2,40,128]{2,1,0:T(8,128)S(1)}, f32[32,32,128]{2,1,0:T(8,128)S(1)}, f32[32,32,128]{2,1,0:T(8,128)S(1)}, f...) custom-call(f32[32,32,128]{2,1,0:T(8,128)S(1)} %get-tuple-element.48, ...), custom_call_target="tpu_custom_call" | custom-call | bytes 4500000 | tf_op jit(solution)/shard_map/two_steps/pallas_call | solution.py:631
  40.7 13.6 %collective-permute-start.8 = (f32[80,128]{1,0:T(8,128)S(1)}, f32[80,128]{1,0:T(8,128)S(1)}, u32[]{:S(2)}, u32[]{:S(2)}) collective-permute-start(f32[80,128]{1,0:T(8,128)S(1)} %get-tuple-element.81), channel_id=1, source_target_pairs={{64,128},{128,64},{192,256},{256,192},{320,384},{384,320},{448,512... | collective-permute-start | bytes 122888 | tf_op jit(solution)/shard_map/ppermute | solution.py:607
  54.3 1.9 %collective-permute-start.9 = (f32[80,128]{1,0:T(8,128)S(1)}, f32[80,128]{1,0:T(8,128)S(1)}, u32[]{:S(2)}, u32[]{:S(2)}) collective-permute-start(f32[80,128]{1,0:T(8,128)S(1)} %get-tuple-element.82), channel_id=1, source_target_pairs={{0,64},{64,0},{128,192},{192,128},{256,320},{320,256},{384,448},{4... | collective-permute-start | bytes 122888 | tf_op jit(solution)/shard_map/ppermute | solution.py:607
  56.2 1.7 %block_2.1 = (f32[32,32,128]{2,1,0:T(8,128)S(1)}, f32[32,32,128]{2,1,0:T(8,128)S(1)}, f32[32,32,128]{2,1,0:T(8,128)S(1)}, f32[2,64,128]{2,1,0:T(8,128)S(1)}, f32[64,128]{1,0:T(8,128)S(1)}) custom-call(f32[32,32,128]{2,1,0:T(8,128)S(1)} %get-tuple-element.48.u, f32[6,32,32,128]{3,2,1,0:T(8,128)S(1)} %get-tuple-element.52.g, ...), custom_call_target="tpu_custom_call" | custom-call | bytes 6000000 | tf_op jit(solution)/shard_map/block_2/pallas_call | solution.py:636
  57.9 1.4 %collective-permute-done.9.xeven = f32[80,128]{1,0:T(8,128)S(1)} collective-permute-done((f32[80,128]{1,0:T(8,128)S(1)}, f32[80,128]{1,0:T(8,128)S(1)}, u32[]{:S(2)}, u32[]{:S(2)}) %collective-permute-start.9) | collective-permute-done | bytes 40992 | tf_op jit(solution)/shard_map/ppermute | solution.py:607
  59.4 1.9 %collective-permute-start.10 = (f32[88,128]{1,0:T(8,128)S(1)}, f32[88,128]{1,0:T(8,128)S(1)}, u32[]{:S(2)}, u32[]{:S(2)}) collective-permute-start(f32[88,128]{1,0:T(8,128)S(1)} %get-tuple-element.85), channel_id=1, source_target_pairs={{0,1},{1,0},{2,3},{3,2},{4,5},{5,4},{6,7},{7,6},{8,9},{9,8},{10,11... | collective-permute-start | bytes 135176 | tf_op jit(solution)/shard_map/ppermute | solution.py:607
  61.4 1.9 %collective-permute-start.11 = (f32[88,128]{1,0:T(8,128)S(1)}, f32[88,128]{1,0:T(8,128)S(1)}, u32[]{:S(2)}, u32[]{:S(2)}) collective-permute-start(f32[88,128]{1,0:T(8,128)S(1)} %get-tuple-element.86), channel_id=1, source_target_pairs={{1,2},{2,1},{5,6},{6,5},{9,10},{10,9},{13,14},{14,13},{17,18},{18,... | collective-permute-start | bytes 135176 | tf_op jit(solution)/shard_map/ppermute | solution.py:607
  63.3 0.9 %collective-permute-done.10.zeven = f32[88,128]{1,0:T(8,128)S(1)} collective-permute-done((f32[88,128]{1,0:T(8,128)S(1)}, f32[88,128]{1,0:T(8,128)S(1)}, u32[]{:S(2)}, u32[]{:S(2)}) %collective-permute-start.10) | collective-permute-done | bytes 45088 | tf_op jit(solution)/shard_map/ppermute | solution.py:607
  64.2 1.9 %collective-permute-done.11.zodd = f32[88,128]{1,0:T(8,128)S(1)} collective-permute-done((f32[88,128]{1,0:T(8,128)S(1)}, f32[88,128]{1,0:T(8,128)S(1)}, u32[]{:S(2)}, u32[]{:S(2)}) %collective-permute-start.11) | collective-permute-done | bytes 45088 | tf_op jit(solution)/shard_map/ppermute | solution.py:607
  66.4 7.5 %collective-permute-start.12 = (f32[56,128]{1,0:T(8,128)S(1)}, f32[56,128]{1,0:T(8,128)S(1)}, u32[]{:S(2)}, u32[]{:S(2)}) collective-permute-start(f32[56,128]{1,0:T(8,128)S(1)} %get-tuple-element.89), channel_id=1, source_target_pairs={{4,8},{8,4},{12,16},{16,12},{20,24},{24,20},{28,32},{32,28},{36,40... | collective-permute-start | bytes 86024 | tf_op jit(solution)/shard_map/ppermute | solution.py:607
  73.8 1.9 %collective-permute-start.13 = (f32[56,128]{1,0:T(8,128)S(1)}, f32[56,128]{1,0:T(8,128)S(1)}, u32[]{:S(2)}, u32[]{:S(2)}) collective-permute-start(f32[56,128]{1,0:T(8,128)S(1)} %get-tuple-element.90), channel_id=1, source_target_pairs={{0,4},{4,0},{8,12},{12,8},{16,20},{20,16},{24,28},{28,24},{32,36},... | collective-permute-start | bytes 86024 | tf_op jit(solution)/shard_map/ppermute | solution.py:607
  75.8 1.2 %collective-permute-done.13.yeven = f32[56,128]{1,0:T(8,128)S(1)} collective-permute-done((f32[56,128]{1,0:T(8,128)S(1)}, f32[56,128]{1,0:T(8,128)S(1)}, u32[]{:S(2)}, u32[]{:S(2)}) %collective-permute-start.13) | collective-permute-done | bytes 28704 | tf_op jit(solution)/shard_map/ppermute | solution.py:607
  76.9 1.9 %last_steps.1 = f32[32,32,128]{2,1,0:T(8,128)} custom-call(f32[6,32,32,128]{3,2,1,0:T(8,128)S(1)} %get-tuple-element.52.g, f32[32,32,128]{2,1,0:T(8,128)S(1)} %get-tuple-element.73.s2, f32[32,32,128]{2,1,0:T(8,128)S(1)} %get-tuple-element.74.d1, f32[32,32,128]{2,1,0:T(8,128)S(1)} %get-tuple-element.75.acc, f32[2,128,128]{2,1,0:T(8,128)S(1)} %get-tuple-element.56.zp, ...), custom_call_target="tpu_custom_call" | custom-call | bytes 7500000 | tf_op jit(solution)/shard_map/last_steps/pallas_call | solution.py:648
  (12 shorter events, 0.6 us)
Async XLA Ops:
  2.0 24.5 %collective-permute-start = (f32[104,128]{1,0:T(8,128)S(1)}, f32[104,128]{1,0:T(8,128)S(1)}, u32[]{:S(2)}, u32[]{:S(2)}) collective-permute-start(f32[104,128]{1,0:T(8,128)S(1)} %get-tuple-element.59), channel_id=1, source_target_pairs={{64,128},{128,64},{192,256},{256,192},{320,384},{384,320},{448,512... | collective-permute-start | bytes 159752 | tf_op jit(solution)/shard_map/ppermute | solution.py:607
  17.1 9.4 %collective-permute-start.1 = (f32[104,128]{1,0:T(8,128)S(1)}, f32[104,128]{1,0:T(8,128)S(1)}, u32[]{:S(2)}, u32[]{:S(2)}) collective-permute-start(f32[104,128]{1,0:T(8,128)S(1)} %get-tuple-element.60), channel_id=1, source_target_pairs={{0,64},{64,0},{128,192},{192,128},{256,320},{320,256},{384,448},{4... | collective-permute-start | bytes 159752 | tf_op jit(solution)/shard_map/ppermute | solution.py:607
  19.0 7.4 %collective-permute-start.2 = (f32[32,128]{1,0:T(8,128)S(1)}, f32[32,128]{1,0:T(8,128)S(1)}, u32[]{:S(2)}, u32[]{:S(2)}) collective-permute-start(f32[32,128]{1,0:T(8,128)S(1)} %get-tuple-element.61), channel_id=1, source_target_pairs={{0,1},{1,0},{2,3},{3,2},{4,5},{5,4},{6,7},{7,6},{8,9},{9,8},{10,11... | collective-permute-start | bytes 49160 | tf_op jit(solution)/shard_map/ppermute | solution.py:607
  21.2 5.3 %collective-permute-start.3 = (f32[32,128]{1,0:T(8,128)S(1)}, f32[32,128]{1,0:T(8,128)S(1)}, u32[]{:S(2)}, u32[]{:S(2)}) collective-permute-start(f32[32,128]{1,0:T(8,128)S(1)} %get-tuple-element.62), channel_id=1, source_target_pairs={{1,2},{2,1},{5,6},{6,5},{9,10},{10,9},{13,14},{14,13},{17,18},{18,... | collective-permute-start | bytes 49160 | tf_op jit(solution)/shard_map/ppermute | solution.py:607
  26.7 13.2 %collective-permute-start.5 = (f32[104,128]{1,0:T(8,128)S(1)}, f32[104,128]{1,0:T(8,128)S(1)}, u32[]{:S(2)}, u32[]{:S(2)}) collective-permute-start(f32[104,128]{1,0:T(8,128)S(1)} %get-tuple-element.66), channel_id=1, source_target_pairs={{0,1},{1,0},{2,3},{3,2},{4,5},{5,4},{6,7},{7,6},{8,9},{9,8},{10,11... | collective-permute-start | bytes 159752 | tf_op jit(solution)/shard_map/ppermute | solution.py:607
  28.6 11.3 %collective-permute-start.6 = (f32[104,128]{1,0:T(8,128)S(1)}, f32[104,128]{1,0:T(8,128)S(1)}, u32[]{:S(2)}, u32[]{:S(2)}) collective-permute-start(f32[104,128]{1,0:T(8,128)S(1)} %get-tuple-element.67), channel_id=1, source_target_pairs={{1,2},{2,1},{5,6},{6,5},{9,10},{10,9},{13,14},{14,13},{17,18},{18,... | collective-permute-start | bytes 159752 | tf_op jit(solution)/shard_map/ppermute | solution.py:607
  31.6 7.1 %collective-permute-start.4 = (f32[40,128]{1,0:T(8,128)S(1)}, f32[40,128]{1,0:T(8,128)S(1)}, u32[]{:S(2)}, u32[]{:S(2)}) collective-permute-start(f32[40,128]{1,0:T(8,128)S(1)} %get-tuple-element.65), channel_id=1, source_target_pairs={{4,8},{8,4},{12,16},{16,12},{20,24},{24,20},{28,32},{32,28},{36,40... | collective-permute-start | bytes 61448 | tf_op jit(solution)/shard_map/ppermute | solution.py:607
  36.8 3.1 %collective-permute-start.7 = (f32[40,128]{1,0:T(8,128)S(1)}, f32[40,128]{1,0:T(8,128)S(1)}, u32[]{:S(2)}, u32[]{:S(2)}) collective-permute-start(f32[40,128]{1,0:T(8,128)S(1)} %get-tuple-element.68), channel_id=1, source_target_pairs={{0,4},{4,0},{8,12},{12,8},{16,20},{20,16},{24,28},{28,24},{32,36},... | collective-permute-start | bytes 61448 | tf_op jit(solution)/shard_map/ppermute | solution.py:607
  40.7 17.2 %collective-permute-start.8 = (f32[80,128]{1,0:T(8,128)S(1)}, f32[80,128]{1,0:T(8,128)S(1)}, u32[]{:S(2)}, u32[]{:S(2)}) collective-permute-start(f32[80,128]{1,0:T(8,128)S(1)} %get-tuple-element.81), channel_id=1, source_target_pairs={{64,128},{128,64},{192,256},{256,192},{320,384},{384,320},{448,512... | collective-permute-start | bytes 122888 | tf_op jit(solution)/shard_map/ppermute | solution.py:607
  54.3 5.0 %collective-permute-start.9 = (f32[80,128]{1,0:T(8,128)S(1)}, f32[80,128]{1,0:T(8,128)S(1)}, u32[]{:S(2)}, u32[]{:S(2)}) collective-permute-start(f32[80,128]{1,0:T(8,128)S(1)} %get-tuple-element.82), channel_id=1, source_target_pairs={{0,64},{64,0},{128,192},{192,128},{256,320},{320,256},{384,448},{4... | collective-permute-start | bytes 122888 | tf_op jit(solution)/shard_map/ppermute | solution.py:607
  59.4 4.8 %collective-permute-start.10 = (f32[88,128]{1,0:T(8,128)S(1)}, f32[88,128]{1,0:T(8,128)S(1)}, u32[]{:S(2)}, u32[]{:S(2)}) collective-permute-start(f32[88,128]{1,0:T(8,128)S(1)} %get-tuple-element.85), channel_id=1, source_target_pairs={{0,1},{1,0},{2,3},{3,2},{4,5},{5,4},{6,7},{7,6},{8,9},{9,8},{10,11... | collective-permute-start | bytes 135176 | tf_op jit(solution)/shard_map/ppermute | solution.py:607
  61.4 4.8 %collective-permute-start.11 = (f32[88,128]{1,0:T(8,128)S(1)}, f32[88,128]{1,0:T(8,128)S(1)}, u32[]{:S(2)}, u32[]{:S(2)}) collective-permute-start(f32[88,128]{1,0:T(8,128)S(1)} %get-tuple-element.86), channel_id=1, source_target_pairs={{1,2},{2,1},{5,6},{6,5},{9,10},{10,9},{13,14},{14,13},{17,18},{18,... | collective-permute-start | bytes 135176 | tf_op jit(solution)/shard_map/ppermute | solution.py:607
  66.4 9.4 %collective-permute-start.12 = (f32[56,128]{1,0:T(8,128)S(1)}, f32[56,128]{1,0:T(8,128)S(1)}, u32[]{:S(2)}, u32[]{:S(2)}) collective-permute-start(f32[56,128]{1,0:T(8,128)S(1)} %get-tuple-element.89), channel_id=1, source_target_pairs={{4,8},{8,4},{12,16},{16,12},{20,24},{24,20},{28,32},{32,28},{36,40... | collective-permute-start | bytes 86024 | tf_op jit(solution)/shard_map/ppermute | solution.py:607
  73.8 3.1 %collective-permute-start.13 = (f32[56,128]{1,0:T(8,128)S(1)}, f32[56,128]{1,0:T(8,128)S(1)}, u32[]{:S(2)}, u32[]{:S(2)}) collective-permute-start(f32[56,128]{1,0:T(8,128)S(1)} %get-tuple-element.90), channel_id=1, source_target_pairs={{0,4},{4,0},{8,12},{12,8},{16,20},{20,16},{24,28},{28,24},{32,36},... | collective-permute-start | bytes 86024 | tf_op jit(solution)/shard_map/ppermute | solution.py:607

commit v7 on v6

--- a/solution.py
+++ b/solution.py
@@ -22,8 +22,7 @@
 B = (2.0 * RHO1 / DELTA, 2.0 * RHO2 / DELTA, 2.0 * RHO3 / DELTA)
 
 XM1 = 104
-ZM1 = 104
-ZH1 = 136
+ZM1 = 99
 YM1 = 40
 XM2 = 80
 ZM2 = 88
@@ -138,7 +137,7 @@
     return total
 
 
-def face_kernel(u_far, f_far, p_far, w_far, u, f, p, w, xp, even, odd, zeven, zodd, sems):
+def face_kernel(u_far, f_far, p_far, w_far, u, f, p, w, xp, zp, last_coupling, even, odd, z_even, z_odd, sems):
     lane8 = iota((8, NY), 1)
     copies = []
     for part in range(4):
@@ -183,18 +182,36 @@
         edges = lax.fori_loop(8 * part, 8 * part + 8, layer, edges, unroll=8)
     for side in (0, 1):
         _, r = face_rows(side)
-        xp[side, 96:104, :] = jnp.zeros((8, NY), F32)
         for end, z in ((0, 0), (1, NZ - 1)):
             _, _, c = face(z, side)
             xp[side, 96 + end : 97 + end, :] = c[end][r : r + 1]
+            xp[side, 99 + 2 * end : 100 + 2 * end, :] = jnp.where(lane8 == 0, 0.0, c[4])[r : r + 1]
+            xp[side, 100 + 2 * end : 101 + 2 * end, :] = jnp.where(lane8 == NY - 1, 0.0, c[5])[r : r + 1]
         xp[side, 98:99, :] = edges[side][r : r + 1]
+        _, _, c = face(1, side)
+        xp[side, 103:104, :] = c[0][r : r + 1]
+        _, _, c = face(NZ - 2, side)
+        last_coupling[side] = jnp.broadcast_to(c[1][r : r + 1], (8, NY))
     put_out(xp, even, odd, "gx")
-    odd_one = parity("gz")
-    zeven[...] = u[(1 - odd_one) * (NZ - 1)]
-    zodd[...] = u[odd_one * (NZ - 1)]
-
-
-def block_kernel(u, f, p, w, g, diag, s, perm_sum, zp, yp):
+    row, lane = plane()
+    for side, z, inner in ((0, 0, 1), (1, NZ - 1, NZ - 2)):
+        here = u[z]
+        _, inverse, c = couplings(p[z], [w[k, z].astype(F32) for k in range(3)])
+        res = f[z] * inverse - here + c[1 - side] * u[inner]
+        res += jnp.where(row == 0, 0.0, c[2]) * pltpu.roll(here, 1, 0)
+        res += jnp.where(row == NX - 1, 0.0, c[3]) * pltpu.roll(here, NX - 1, 0)
+        res += jnp.where(lane == 0, 0.0, c[4]) * pltpu.roll(here, 1, 1)
+        res += jnp.where(lane == NY - 1, 0.0, c[5]) * pltpu.roll(here, NY - 1, 1)
+        zp[side, 0:32, :] = here
+        zp[side, 32:64, :] = res
+        zp[side, 64:96, :] = c[side]
+        zp[side, 96:97, :] = combined_row(jnp.where(lane == 0, c[4], c[5]))
+        zp[side, 97:98, :] = c[2][0:1]
+        zp[side, 98:99, :] = c[3][NX - 1 :]
+    put_out(zp, z_even, z_odd, "gz")
+
+
+def block_kernel(u, f, p, w, g, diag, s, perm_sum, yp):
     row, lane = plane()
     perm_sum[...] = jnp.zeros_like(perm_sum)
 
@@ -224,12 +241,6 @@
     yp[0:32, :] = pu
     yp[32:64, :] = ps
     yp[64:96, :] = pg
-    for side, z in ((0, 0), (1, NZ - 1)):
-        _, _, c = couplings(p[z], [w[k, z].astype(F32) for k in range(3)])
-        zp[side, 0:32, :] = u[z]
-        zp[side, 32:64, :] = s[z]
-        zp[side, 64:96, :] = c[side]
-        zp[side, 96:128, :] = jnp.where(lane == 0, c[4], 0.0) + jnp.where(lane == NY - 1, c[5], 0.0)
 
 
 def z_part(stage, faces, xp, xh):
@@ -274,23 +285,23 @@
     return messages
 
 
-def first_message_kernel(
+def first_y_kernel(
     xodd, xeven, zeven, zodd, xp, zp, yp,
-    xh, zu, z_to_even, z_to_odd, y_to_even, y_to_odd,
-    z_stage, z_rows, y_stage,
+    xh, zh, even, odd, line_even, line_odd,
+    stage, lines,
 ):
     take_in(xh, xeven, xodd, "gx")
-    take_in(zu, zeven, zodd, "gz")
-    lines = z_part(z_stage, zp, xp, xh)
+    take_in(zh, zeven, zodd, "gz")
+    messages = y_part(yp[0:32, :], yp[32:64, :], yp[64:96, :], zp, zh, xp, xh)
     for side in (0, 1):
-        z_rows[side, 0:32, :] = z_stage[side, 32:64, :]
-        z_rows[side, 32:96, :] = zp[side, 64:128, :]
-        z_rows[side, 96:104, :] = lines[side]
-    put_out(z_rows, z_to_even, z_to_odd, "gz")
-    messages = y_part(yp[0:32, :], yp[32:64, :], yp[64:96, :], zp, zu, xp, xh)
-    for side in (0, 1):
-        y_stage[side, 0:32, :], y_stage[side, 32:40, :] = messages[side]
-    put_out(y_stage, y_to_even, y_to_odd, "gy")
+        stage[side, 0:32, :], stage[side, 32:40, :] = messages[side]
+    put_out(stage, even, odd, "gy")
+    for side, z in ((0, 0), (1, NZ - 1)):
+        for end in (0, 1):
+            lines[side, end : end + 1, :] = xh[end, z : z + 1, :]
+            lines[side, 2 + end : 3 + end, :] = xh[end, 64 + z : 65 + z, :]
+        lines[side, 4:8, :] = jnp.zeros((4, NY), F32)
+    put_out(lines, line_even, line_odd, "gz")
 
 
 def z_halo_residual(side, res, zh1, yh, mine):
@@ -298,14 +309,15 @@
     at = 3 + 4 * side
     low, high = yh[0, 0:32, at : at + 1], yh[1, 0:32, at : at + 1]
     corner = jnp.where(lane == 0, low, 0.0) + jnp.where(lane == NY - 1, high, 0.0)
-    return res + zh1[side, 64:96, :] * mine + zh1[side, 96:128, :] * corner
+    return res + zh1[side, 64:96, :] * mine + columns(zh1[side, 96:97, :]) * corner
 
 
 def x_halo_residual(side, res, xh1, zh, lines, yh, mine):
     row, _ = plane()
     total = res + xh1[side, 64:96, :] * mine
-    for end, at in ((0, 0), (1, NZ - 1)):
-        total += jnp.where(row == at, xh1[side, 96 + end : 97 + end, :] * zh[end, lines + side : lines + side + 1, :], 0.0)
+    if zh is not None:
+        for end, at in ((0, 0), (1, NZ - 1)):
+            total += jnp.where(row == at, xh1[side, 96 + end : 97 + end, :] * zh[end, lines + side : lines + side + 1, :], 0.0)
     corner = combine(yh[0, 32 + side : 33 + side, :], yh[1, 32 + side : 33 + side, :], 0)
     return total + columns(xh1[side, 98:99, :] * corner)
 
@@ -319,15 +331,11 @@
 
 
 def second_kernel(
-    u, g, diag, s1, perm_sum, zp, yp, xp, xh, zu, yodd, zeven, zodd, yeven,
-    zh, yh, s0, d0, b, xp2, cross2, zy2, even, odd,
-    zin, cross, rsum, rows, edge_s, edge_d, stage,
+    u, g, diag, s1, perm_sum, zp, yp, xp, last_coupling, xh, zh, yodd, yeven,
+    yh, s0, d0, b, xp2, cross2, zy2, even, odd,
+    cross, rsum, rows, edge_s, edge_d, stage,
 ):
     take_in(yh, yeven, yodd, "gy")
-    take_in(zin, zeven, zodd, "gz")
-    for side in (0, 1):
-        zh[side, 0:32, :] = zu[side]
-        zh[side, 32:ZH1, :] = zin[side]
     scale = 1.0 / THETA
     low, high = yh[0, 0:32, :], yh[1, 0:32, :]
     own_y = yp[64:96, :]
@@ -340,7 +348,7 @@
         zy2[side] = zp[side, 64:96, :] * (scale * z_halo_residual(side, zh[side, 32:64, :], zh, yh, u[z]))
         gx = xp[side, 64:96, :]
         cross[side] = gx * xh[side, 0:32, :]
-        cross2[side] = gx * (scale * x_halo_residual(side, xh[side, 32:64, :], xh, zh, 128, yh, xp[side, 0:32, :]))
+        cross2[side] = gx * (scale * x_halo_residual(side, xh[side, 32:64, :], xh, None, 0, yh, xp[side, 0:32, :]))
     rsum[...] = jnp.zeros_like(rsum)
 
     def start(z, carry):
@@ -396,7 +404,7 @@
         stage[side, 0:64, :] = xp2[side]
         for z in range(4):
             stage[side, 64 + 3 * z : 67 + 3 * z, :] = rhs[4 * z + side : 4 * z + side + 3]
-        stage[side, 76:80, :] = jnp.zeros((4, NY), F32)
+        stage[side, 76:80, :] = last_coupling[side, 0:4, :]
     put_out(stage, even, odd, "gx")
 
 
@@ -407,7 +415,15 @@
     return total + g[4] * pltpu.roll(here, 1, 1) + g[5] * pltpu.roll(here, NY - 1, 1)
 
 
-def second_block_kernel(u, g, s0, d0, cross2, zy2, s, d, acc, zp2, yp2, s1):
+def edge_change(coupling_x, edge_z, coupling_z, edge_x, corner):
+    return (coupling_x * edge_z + coupling_z * edge_x) * corner * (1.0 / THETA)
+
+
+def second_block_kernel(
+    u, g, s0, d0, cross2, zy2, xp, xp2, zp, xh, zh, line_even, line_odd,
+    s, d, acc, zp2, yp2, xm, lh,
+    s1,
+):
     yq2 = zy2[2]
 
     def step(z, carry):
@@ -424,6 +440,19 @@
         s1[z] += zy2[side]
         d[z] += B[0] * zy2[side]
         acc[z] += B[0] * zy2[side]
+    take_in(lh, line_even, line_odd, "gz")
+    xm[...] = xp2[:, 0:32, :]
+    for end, z in ((0, 0), (1, NZ - 1)):
+        for side, x in ((0, 0), (1, NX - 1)):
+            change = edge_change(
+                xp[side, 64 + z : 65 + z, :], xh[side, 96 + end : 97 + end, :],
+                zp[end, 64 + x : 65 + x, :], zh[end, 97 + side : 98 + side, :],
+                lh[end, side : side + 1, :],
+            )
+            s1[z, x : x + 1, :] += change
+            d[z, x : x + 1, :] += B[0] * change
+            acc[z, x : x + 1, :] += B[0] * change
+            xm[side, z : z + 1, :] += B[0] * change
 
     def partial(z, carry):
         pu, ps = carry
@@ -442,8 +471,22 @@
         zp2[side, 32:64, :] = s[z]
 
 
-def second_z_kernel(xodd, xeven, xp, zp2, b, xh2, even, odd, b3, stage, rows):
+def second_z_kernel(xodd, xeven, xp, zp, zp2, b, xh, zh, lh, xh2, even, odd, b3, stage, rows):
     take_in(xh2, xeven, xodd, "gx")
+    for side, x in ((0, 0), (1, NX - 1)):
+        for end, z, inner in ((0, 0, 1), (1, NZ - 1, NZ - 2)):
+            change = edge_change(
+                xh[side, 64 + z : 65 + z, :], zp[end, 64 + x : 65 + x, :],
+                xh[side, 96 + end : 97 + end, :], lh[end, 2 + side : 3 + side, :],
+                zh[end, x : x + 1, :],
+            )
+            turn = B[0] * change
+            at = 99 + 2 * end
+            beside = xh[side, at : at + 1, :] * pltpu.roll(turn, 1, 1) + xh[side, at + 1 : at + 2, :] * pltpu.roll(turn, NY - 1, 1)
+            inward = xh[side, 103:104, :] if end == 0 else xh2[side, 76:77, :]
+            xh2[side, z : z + 1, :] += turn
+            xh2[side, 32 + z : 33 + z, :] += change - turn + beside
+            xh2[side, 32 + inner : 33 + inner, :] += inward * turn
     lines = z_part(stage, zp2, xp, xh2)
     lane16 = iota((16, NY), 1)
     wide = b[...]
@@ -526,7 +569,7 @@
 
 
 def third_kernel(
-    g, s2, d1, acc, zp, yp, xp, xh, zh, yh, xp2, zp2, yp2, xh2, zh2, b3, yodd, yeven,
+    g, s2, d1, acc, zp, yp, xp, xh, zh, yh, xm, zp2, yp2, xh2, zh2, b3, yodd, yeven,
     far_out,
     yh2, s, d, cross, cross2, ext, err, spread, out, sems,
 ):
@@ -544,7 +587,7 @@
         zq2.append(zp[side, 64:96, :] * dz)
         gx = xp[side, 64:96, :]
         cross[side] = gx * xu
-        dx = A[1] * xu + B[1] * x_halo_residual(side, xh2[side, 32:64, :], xh, zh2, 64, yh2, xp2[side, 0:32, :])
+        dx = A[1] * xu + B[1] * x_halo_residual(side, xh2[side, 32:64, :], xh, zh2, 64, yh2, xm[side])
         cross2[side] = gx * dx
     coarse_solve(b3, zh2, yh2, ext, err, spread)
 
@@ -611,35 +654,35 @@
 def per_device(u, f, p, w):
     face = (2, 32, NY)
     far = [pltpu.with_memory_space_constraint(x, pltpu.HBM) for x in (u, f, p, w)]
-    u, f, p, w, xp, even, odd, zeven, zodd = call(
-        face_kernel, "x_faces", 4,
-        [FULL, FULL, FULL, BF16_FIELD, (2, XM1, NY), (XM1, NY), (XM1, NY), (NX, NY), (NX, NY)], (), 2.0, HBM,
-        [pltpu.SemaphoreType.DMA((4, 4))],
+    u, f, p, w, xp, zp, last_coupling, even, odd, zeven, zodd = call(
+        face_kernel, "faces", 4,
+        [FULL, FULL, FULL, BF16_FIELD, (2, XM1, NY), (2, ZM1, NY), (2, 8, NY), (XM1, NY), (XM1, NY), (ZM1, NY), (ZM1, NY)],
+        (), 2.0, HBM, [pltpu.SemaphoreType.DMA((4, 4))],
     )(*far)
-    g, diag, s, perm_sum, zp, yp = call(
-        block_kernel, "block", 4, [(6,) + FULL, FULL, FULL, (4, NX, NY), (2, 128, NY), (96, NY)], (), 2.5
+    g, diag, s, perm_sum, yp = call(
+        block_kernel, "block", 4, [(6,) + FULL, FULL, FULL, (4, NX, NY), (96, NY)], (), 2.5
     )(u, f, p, w)
     even, odd = swap(even, odd, "gx")
     zeven, zodd = swap(zeven, zodd, "gz")
-    xh, zu, zeven, zodd, yeven, yodd = call(
-        first_message_kernel, "zy_message", 7,
-        [(2, XM1, NY), (2, NX, NY), (ZM1, NY), (ZM1, NY), (YM1, NY), (YM1, NY)],
-        [(2, 64, NY), (2, ZM1, NY), (2, YM1, NY)],
+    xh, zh, yeven, yodd, line_even, line_odd = call(
+        first_y_kernel, "y_message", 7,
+        [(2, XM1, NY), (2, ZM1, NY), (YM1, NY), (YM1, NY), (8, NY), (8, NY)],
+        [(2, YM1, NY), (2, 8, NY)],
     )(odd, even, zeven, zodd, xp, zp, yp)
-    zeven, zodd = swap(zeven, zodd, "gz")
     yeven, yodd = swap(yeven, yodd, "gy")
-    zh, yh, s, d, b, xp2, cross2, zy2, even, odd = call(
-        second_kernel, "two_steps", 14,
-        [(2, ZH1, NY), (2, YM1, NY), FULL, FULL, (16, NY), (2, 64, NY), face, (3, NX, NY), (XM2, NY), (XM2, NY)],
-        [(2, ZM1, NY), face, (4, NX, NY), (2, 16, NY), (2, NZ, 8, NY), (2, NZ, 8, NY), (2, XM2, NY)], 1.5,
-    )(u, g, diag, s, perm_sum, zp, yp, xp, xh, zu, yodd, zeven, zodd, yeven)
-    s, d1, acc, zp2, yp2 = call(
-        second_block_kernel, "block_2", 6, [FULL, FULL, FULL, (2, 64, NY), (64, NY)], [FULL], 2.0
-    )(u, g, s, d, cross2, zy2)
+    yh, s, d, b, xp2, cross2, zy2, even, odd = call(
+        second_kernel, "two_steps", 13,
+        [(2, YM1, NY), FULL, FULL, (16, NY), (2, 64, NY), face, (3, NX, NY), (XM2, NY), (XM2, NY)],
+        [face, (4, NX, NY), (2, 16, NY), (2, NZ, 8, NY), (2, NZ, 8, NY), (2, XM2, NY)], 1.5,
+    )(u, g, diag, s, perm_sum, zp, yp, xp, last_coupling, xh, zh, yodd, yeven)
     even, odd = swap(even, odd, "gx")
+    line_even, line_odd = swap(line_even, line_odd, "gz")
+    s, d1, acc, zp2, yp2, xm, lh = call(
+        second_block_kernel, "block_2", 13, [FULL, FULL, FULL, (2, 64, NY), (64, NY), face, (2, 8, NY)], [FULL], 2.0
+    )(u, g, s, d, cross2, zy2, xp, xp2, zp, xh, zh, line_even, line_odd)
     xh2, even, odd, b3 = call(
-        second_z_kernel, "z_message_2", 5, [(2, XM2, NY), (ZM2, NY), (ZM2, NY), (16, NY)], [(2, ZM2, NY), (16, NY)]
-    )(odd, even, xp, zp2, b)
+        second_z_kernel, "z_message_2", 9, [(2, XM2, NY), (ZM2, NY), (ZM2, NY), (16, NY)], [(2, ZM2, NY), (16, NY)]
+    )(odd, even, xp, zp, zp2, b, xh, zh, lh)
     even, odd = swap(even, odd, "gz")
     zh2, even, odd = call(
         second_y_kernel, "y_message_2", 7, [(2, ZM2, NY), (YM2, NY), (YM2, NY)], [(2, YM2, NY)]
@@ -649,7 +692,7 @@
         third_kernel, "last_steps", 18, [FULL],
         [(2, YM2, NY), FULL, FULL, face, face, (10, 16, NY), (16, NY), (4, NX, NY), FULL], 2.5, VM,
         [pltpu.SemaphoreType.DMA((4,))], HBM,
-    )(g, s, d1, acc, zp, yp, xp, xh, zh, yh, xp2, zp2, yp2, xh2, zh2, b3, odd, even)
+    )(g, s, d1, acc, zp, yp, xp, xh, zh, yh, xm, zp2, yp2, xh2, zh2, b3, odd, even)
     return out
 
 

time: 79.3 us -> 79.1 us (level)
  the two profiles are of different devices: /device:TPU:283 before, /device:TPU:277 now
where the time goes in v7:
time: 79.1 us; the launch traced here: 78.6 us
  starting transfers between devices  60.8 us (77%)
  waiting for transfers between devices  9.05 us (11%)
  Pallas kernels  8.58 us (11%)
    ppermute x14, starting transfers between devices, swap(): results.append(lax.ppermute(values, axis, pairs))  60.8 us
    ppermute x14, waiting for transfers between devices, swap(): results.append(lax.ppermute(values, axis, pairs))  9.05 us
    pallas_call x1, Pallas kernels, per_device(): call(face_kernel, 'faces', 4, [FULL, FULL, FULL, BF16_FIELD, (2, XM1, NY)...  2.04 us
    pallas_call x1, Pallas kernels, per_device(): call(third_kernel, 'last_steps', 18, [FULL], [(2, YM2, NY), FULL, FULL, f...  1.92 us
    pallas_call x1, Pallas kernels, per_device(): call(second_block_kernel, 'block_2', 13, [FULL, FULL, FULL, (2, 64, NY),...  1.63 us
  transfers between devices with their start and end apart: 14, of which 6 were waited for; matrix products, arithmetic and copies ran while one was open for 0% of the time, Pallas kernels for 4%

profile of v7, /device:TPU:277, one launch (start us, length us, event | category | flops | bytes accessed | tf_op | source)
XLA Modules:
  0.0 78.6 jit_solution(992052814216000479)
XLA Ops:
  0.0 2.0 %faces.1 = (f32[32,32,128]{2,1,0:T(8,128)S(1)}, f32[32,32,128]{2,1,0:T(8,128)S(1)}, f32[32,32,128]{2,1,0:T(8,128)S(1)}, bf16[3,32,32,128]{3,2,1,0:T(8,128)(2,1)S...) custom-call(f32[32,32,128]{2,1,0:T(8,128)} %u_far.1, ...), custom_call_target="tpu_custom_call" | custom-call | bytes 6000000 | tf_op jit(solution)/shard_map/faces/pallas_call | solution.py:657
  2.0 2.1 %collective-permute-start = (f32[104,128]{1,0:T(8,128)S(1)}, f32[104,128]{1,0:T(8,128)S(1)}, u32[]{:S(2)}, u32[]{:S(2)}) collective-permute-start(f32[104,128]{1,0:T(8,128)S(1)} %get-tuple-element.62), channel_id=1, source_target_pairs={{64,128},{128,64},{192,256},{256,192},{320,384},{384,320},{448,512... | collective-permute-start | bytes 159752 | tf_op jit(solution)/shard_map/ppermute | solution.py:650
  4.1 15.9 %collective-permute-start.1 = (f32[104,128]{1,0:T(8,128)S(1)}, f32[104,128]{1,0:T(8,128)S(1)}, u32[]{:S(2)}, u32[]{:S(2)}) collective-permute-start(f32[104,128]{1,0:T(8,128)S(1)} %get-tuple-element.63), channel_id=1, source_target_pairs={{0,64},{64,0},{128,192},{192,128},{256,320},{320,256},{384,448},{4... | collective-permute-start | bytes 159752 | tf_op jit(solution)/shard_map/ppermute | solution.py:650
  20.1 2.8 %collective-permute-start.2 = (f32[99,128]{1,0:T(8,128)S(1)}, f32[99,128]{1,0:T(8,128)S(1)}, u32[]{:S(2)}, u32[]{:S(2)}) collective-permute-start(f32[99,128]{1,0:T(8,128)S(1)} %get-tuple-element.64), channel_id=1, source_target_pairs={{0,1},{1,0},{2,3},{3,2},{4,5},{5,4},{6,7},{7,6},{8,9},{9,8},{10,11... | collective-permute-start | bytes 152072 | tf_op jit(solution)/shard_map/ppermute | solution.py:650
  22.9 1.9 %collective-permute-start.3 = (f32[99,128]{1,0:T(8,128)S(1)}, f32[99,128]{1,0:T(8,128)S(1)}, u32[]{:S(2)}, u32[]{:S(2)}) collective-permute-start(f32[99,128]{1,0:T(8,128)S(1)} %get-tuple-element.65), channel_id=1, source_target_pairs={{1,2},{2,1},{5,6},{6,5},{9,10},{10,9},{13,14},{14,13},{17,18},{18,... | collective-permute-start | bytes 152072 | tf_op jit(solution)/shard_map/ppermute | solution.py:650
  24.8 1.5 %block.1 = (f32[6,32,32,128]{3,2,1,0:T(8,128)S(1)}, f32[32,32,128]{2,1,0:T(8,128)S(1)}, f32[32,32,128]{2,1,0:T(8,128)S(1)}, f32[4,32,128]{2,1,0:T(8,128)S(1)}, f32[96,128]{1,0:T(8,128)S(1)}) custom-call(f32[32,32,128]{2,1,0:T(8,128)S(1)} %get-tuple-element.50.u, f32[32,32,128]{2,1,0:T(8,128)S(1)} %get-tuple-element.51.f, ...), custom_call_target="tpu_custom_call" | custom-call | bytes 7500000 | tf_op jit(solution)/shard_map/block/pallas_call | solution.py:662
  26.3 1.4 %collective-permute-done.3.zodd = f32[99,128]{1,0:T(8,128)S(1)} collective-permute-done((f32[99,128]{1,0:T(8,128)S(1)}, f32[99,128]{1,0:T(8,128)S(1)}, u32[]{:S(2)}, u32[]{:S(2)}) %collective-permute-start.3) | collective-permute-done | bytes 50720 | tf_op jit(solution)/shard_map/ppermute | solution.py:650
  28.0 5.2 %collective-permute-start.4 = (f32[40,128]{1,0:T(8,128)S(1)}, f32[40,128]{1,0:T(8,128)S(1)}, u32[]{:S(2)}, u32[]{:S(2)}) collective-permute-start(f32[40,128]{1,0:T(8,128)S(1)} %get-tuple-element.68), channel_id=1, source_target_pairs={{4,8},{8,4},{12,16},{16,12},{20,24},{24,20},{28,32},{32,28},{36,40... | collective-permute-start | bytes 61448 | tf_op jit(solution)/shard_map/ppermute | solution.py:650
  33.2 1.9 %collective-permute-start.5 = (f32[40,128]{1,0:T(8,128)S(1)}, f32[40,128]{1,0:T(8,128)S(1)}, u32[]{:S(2)}, u32[]{:S(2)}) collective-permute-start(f32[40,128]{1,0:T(8,128)S(1)} %get-tuple-element.69), channel_id=1, source_target_pairs={{0,4},{4,0},{8,12},{12,8},{16,20},{20,16},{24,28},{28,24},{32,36},... | collective-permute-start | bytes 61448 | tf_op jit(solution)/shard_map/ppermute | solution.py:650
  35.2 1.1 %collective-permute-done.5.yeven = f32[40,128]{1,0:T(8,128)S(1)} collective-permute-done((f32[40,128]{1,0:T(8,128)S(1)}, f32[40,128]{1,0:T(8,128)S(1)}, u32[]{:S(2)}, u32[]{:S(2)}) %collective-permute-start.5) | collective-permute-done | bytes 20512 | tf_op jit(solution)/shard_map/ppermute | solution.py:650
  36.3 1.0 %two_steps.1 = (f32[2,40,128]{2,1,0:T(8,128)S(1)}, f32[32,32,128]{2,1,0:T(8,128)S(1)}, f32[32,32,128]{2,1,0:T(8,128)S(1)}, f32[16,128]{1,0:T(8,128)S(1)}, f32[2,...) custom-call(f32[32,32,128]{2,1,0:T(8,128)S(1)} %get-tuple-element.50, ...), custom_call_target="tpu_custom_call" | custom-call | bytes 4500000 | tf_op jit(solution)/shard_map/two_steps/pallas_call | solution.py:673
  37.3 1.9 %collective-permute-start.8 = (f32[80,128]{1,0:T(8,128)S(1)}, f32[80,128]{1,0:T(8,128)S(1)}, u32[]{:S(2)}, u32[]{:S(2)}) collective-permute-start(f32[80,128]{1,0:T(8,128)S(1)} %get-tuple-element.84), channel_id=1, source_target_pairs={{64,128},{128,64},{192,256},{256,192},{320,384},{384,320},{448,512... | collective-permute-start | bytes 122888 | tf_op jit(solution)/shard_map/ppermute | solution.py:650
  39.2 11.7 %collective-permute-start.9 = (f32[80,128]{1,0:T(8,128)S(1)}, f32[80,128]{1,0:T(8,128)S(1)}, u32[]{:S(2)}, u32[]{:S(2)}) collective-permute-start(f32[80,128]{1,0:T(8,128)S(1)} %get-tuple-element.85), channel_id=1, source_target_pairs={{0,64},{64,0},{128,192},{192,128},{256,320},{320,256},{384,448},{4... | collective-permute-start | bytes 122888 | tf_op jit(solution)/shard_map/ppermute | solution.py:650
  50.9 2.8 %collective-permute-start.6 = (f32[8,128]{1,0:T(8,128)S(1)}, f32[8,128]{1,0:T(8,128)S(1)}, u32[]{:S(2)}, u32[]{:S(2)}) collective-permute-start(f32[8,128]{1,0:T(8,128)S(1)} %get-tuple-element.75), channel_id=1, source_target_pairs={{0,1},{1,0},{2,3},{3,2},{4,5},{5,4},{6,7},{7,6},{8,9},{9,8},{10,11... | collective-permute-start | bytes 12296 | tf_op jit(solution)/shard_map/ppermute | solution.py:650
  53.8 1.9 %collective-permute-start.7 = (f32[8,128]{1,0:T(8,128)S(1)}, f32[8,128]{1,0:T(8,128)S(1)}, u32[]{:S(2)}, u32[]{:S(2)}) collective-permute-start(f32[8,128]{1,0:T(8,128)S(1)} %get-tuple-element.76), channel_id=1, source_target_pairs={{1,2},{2,1},{5,6},{6,5},{9,10},{10,9},{13,14},{14,13},{17,18},{18,... | collective-permute-start | bytes 12296 | tf_op jit(solution)/shard_map/ppermute | solution.py:650
  55.7 2.4 %collective-permute-done.7.line_odd = f32[8,128]{1,0:T(8,128)S(1)} collective-permute-done((f32[8,128]{1,0:T(8,128)S(1)}, f32[8,128]{1,0:T(8,128)S(1)}, u32[]{:S(2)}, u32[]{:S(2)}) %collective-permute-start.7) | collective-permute-done | bytes 4128 | tf_op jit(solution)/shard_map/ppermute | solution.py:650
  58.1 1.6 %block_2.1 = (f32[32,32,128]{2,1,0:T(8,128)S(1)}, f32[32,32,128]{2,1,0:T(8,128)S(1)}, f32[32,32,128]{2,1,0:T(8,128)S(1)}, f32[2,64,128]{2,1,0:T(8,128)S(1)}, f32...) custom-call(f32[32,32,128]{2,1,0:T(8,128)S(1)} %get-tuple-element.50.u, ...), custom_call_target="tpu_custom_call" | custom-call | bytes 6000000 | tf_op jit(solution)/shard_map/block_2/pallas_call | solution.py:680
  59.9 1.9 %collective-permute-start.10 = (f32[88,128]{1,0:T(8,128)S(1)}, f32[88,128]{1,0:T(8,128)S(1)}, u32[]{:S(2)}, u32[]{:S(2)}) collective-permute-start(f32[88,128]{1,0:T(8,128)S(1)} %get-tuple-element.89), channel_id=1, source_target_pairs={{0,1},{1,0},{2,3},{3,2},{4,5},{5,4},{6,7},{7,6},{8,9},{9,8},{10,11... | collective-permute-start | bytes 135176 | tf_op jit(solution)/shard_map/ppermute | solution.py:650
  61.8 1.9 %collective-permute-start.11 = (f32[88,128]{1,0:T(8,128)S(1)}, f32[88,128]{1,0:T(8,128)S(1)}, u32[]{:S(2)}, u32[]{:S(2)}) collective-permute-start(f32[88,128]{1,0:T(8,128)S(1)} %get-tuple-element.90), channel_id=1, source_target_pairs={{1,2},{2,1},{5,6},{6,5},{9,10},{10,9},{13,14},{14,13},{17,18},{18,... | collective-permute-start | bytes 135176 | tf_op jit(solution)/shard_map/ppermute | solution.py:650
  64.7 1.9 %collective-permute-done.11.zodd = f32[88,128]{1,0:T(8,128)S(1)} collective-permute-done((f32[88,128]{1,0:T(8,128)S(1)}, f32[88,128]{1,0:T(8,128)S(1)}, u32[]{:S(2)}, u32[]{:S(2)}) %collective-permute-start.11) | collective-permute-done | bytes 45088 | tf_op jit(solution)/shard_map/ppermute | solution.py:650
  66.8 6.8 %collective-permute-start.12 = (f32[56,128]{1,0:T(8,128)S(1)}, f32[56,128]{1,0:T(8,128)S(1)}, u32[]{:S(2)}, u32[]{:S(2)}) collective-permute-start(f32[56,128]{1,0:T(8,128)S(1)} %get-tuple-element.93), channel_id=1, source_target_pairs={{4,8},{8,4},{12,16},{16,12},{20,24},{24,20},{28,32},{32,28},{36,40... | collective-permute-start | bytes 86024 | tf_op jit(solution)/shard_map/ppermute | solution.py:650
  73.6 1.9 %collective-permute-start.13 = (f32[56,128]{1,0:T(8,128)S(1)}, f32[56,128]{1,0:T(8,128)S(1)}, u32[]{:S(2)}, u32[]{:S(2)}) collective-permute-start(f32[56,128]{1,0:T(8,128)S(1)} %get-tuple-element.94), channel_id=1, source_target_pairs={{0,4},{4,0},{8,12},{12,8},{16,20},{20,16},{24,28},{28,24},{32,36},... | collective-permute-start | bytes 86024 | tf_op jit(solution)/shard_map/ppermute | solution.py:650
  75.5 1.2 %collective-permute-done.13.yeven = f32[56,128]{1,0:T(8,128)S(1)} collective-permute-done((f32[56,128]{1,0:T(8,128)S(1)}, f32[56,128]{1,0:T(8,128)S(1)}, u32[]{:S(2)}, u32[]{:S(2)}) %collective-permute-start.13) | collective-permute-done | bytes 28704 | tf_op jit(solution)/shard_map/ppermute | solution.py:650
  76.7 1.9 %last_steps.1 = f32[32,32,128]{2,1,0:T(8,128)} custom-call(f32[6,32,32,128]{3,2,1,0:T(8,128)S(1)} %get-tuple-element.54.g, f32[32,32,128]{2,1,0:T(8,128)S(1)} %get-tuple-element.77.s2, f32[32,32,128]{2,1,0:T(8,128)S(1)} %get-tuple-element.78.d1, f32[32,32,128]{2,1,0:T(8,128)S(1)} %get-tuple-element.79.acc, f32[2,99,128]{2,1,0:T(8,128)S(1)} %get-tuple-element.58.zp, ...), custom_call_target="tpu_custom_call" | custom-call | bytes 7500000 | tf_op jit(solution)/shard_map/last_steps/pallas_call | solution.py:691
  (12 shorter events, 1.5 us)
Async XLA Ops:
  2.0 25.7 %collective-permute-start = (f32[104,128]{1,0:T(8,128)S(1)}, f32[104,128]{1,0:T(8,128)S(1)}, u32[]{:S(2)}, u32[]{:S(2)}) collective-permute-start(f32[104,128]{1,0:T(8,128)S(1)} %get-tuple-element.62), channel_id=1, source_target_pairs={{64,128},{128,64},{192,256},{256,192},{320,384},{384,320},{448,512... | collective-permute-start | bytes 159752 | tf_op jit(solution)/shard_map/ppermute | solution.py:650
  4.1 23.7 %collective-permute-start.1 = (f32[104,128]{1,0:T(8,128)S(1)}, f32[104,128]{1,0:T(8,128)S(1)}, u32[]{:S(2)}, u32[]{:S(2)}) collective-permute-start(f32[104,128]{1,0:T(8,128)S(1)} %get-tuple-element.63), channel_id=1, source_target_pairs={{0,64},{64,0},{128,192},{192,128},{256,320},{320,256},{384,448},{4... | collective-permute-start | bytes 159752 | tf_op jit(solution)/shard_map/ppermute | solution.py:650
  20.1 6.3 %collective-permute-start.2 = (f32[99,128]{1,0:T(8,128)S(1)}, f32[99,128]{1,0:T(8,128)S(1)}, u32[]{:S(2)}, u32[]{:S(2)}) collective-permute-start(f32[99,128]{1,0:T(8,128)S(1)} %get-tuple-element.64), channel_id=1, source_target_pairs={{0,1},{1,0},{2,3},{3,2},{4,5},{5,4},{6,7},{7,6},{8,9},{9,8},{10,11... | collective-permute-start | bytes 152072 | tf_op jit(solution)/shard_map/ppermute | solution.py:650
  22.9 4.9 %collective-permute-start.3 = (f32[99,128]{1,0:T(8,128)S(1)}, f32[99,128]{1,0:T(8,128)S(1)}, u32[]{:S(2)}, u32[]{:S(2)}) collective-permute-start(f32[99,128]{1,0:T(8,128)S(1)} %get-tuple-element.65), channel_id=1, source_target_pairs={{1,2},{2,1},{5,6},{6,5},{9,10},{10,9},{13,14},{14,13},{17,18},{18,... | collective-permute-start | bytes 152072 | tf_op jit(solution)/shard_map/ppermute | solution.py:650
  28.0 7.1 %collective-permute-start.4 = (f32[40,128]{1,0:T(8,128)S(1)}, f32[40,128]{1,0:T(8,128)S(1)}, u32[]{:S(2)}, u32[]{:S(2)}) collective-permute-start(f32[40,128]{1,0:T(8,128)S(1)} %get-tuple-element.68), channel_id=1, source_target_pairs={{4,8},{8,4},{12,16},{16,12},{20,24},{24,20},{28,32},{32,28},{36,40... | collective-permute-start | bytes 61448 | tf_op jit(solution)/shard_map/ppermute | solution.py:650
  33.2 3.1 %collective-permute-start.5 = (f32[40,128]{1,0:T(8,128)S(1)}, f32[40,128]{1,0:T(8,128)S(1)}, u32[]{:S(2)}, u32[]{:S(2)}) collective-permute-start(f32[40,128]{1,0:T(8,128)S(1)} %get-tuple-element.69), channel_id=1, source_target_pairs={{0,4},{4,0},{8,12},{12,8},{16,20},{20,16},{24,28},{28,24},{32,36},... | collective-permute-start | bytes 61448 | tf_op jit(solution)/shard_map/ppermute | solution.py:650
  37.3 22.5 %collective-permute-start.8 = (f32[80,128]{1,0:T(8,128)S(1)}, f32[80,128]{1,0:T(8,128)S(1)}, u32[]{:S(2)}, u32[]{:S(2)}) collective-permute-start(f32[80,128]{1,0:T(8,128)S(1)} %get-tuple-element.84), channel_id=1, source_target_pairs={{64,128},{128,64},{192,256},{256,192},{320,384},{384,320},{448,512... | collective-permute-start | bytes 122888 | tf_op jit(solution)/shard_map/ppermute | solution.py:650
  39.2 20.6 %collective-permute-start.9 = (f32[80,128]{1,0:T(8,128)S(1)}, f32[80,128]{1,0:T(8,128)S(1)}, u32[]{:S(2)}, u32[]{:S(2)}) collective-permute-start(f32[80,128]{1,0:T(8,128)S(1)} %get-tuple-element.85), channel_id=1, source_target_pairs={{0,64},{64,0},{128,192},{192,128},{256,320},{320,256},{384,448},{4... | collective-permute-start | bytes 122888 | tf_op jit(solution)/shard_map/ppermute | solution.py:650
  50.9 4.8 %collective-permute-start.6 = (f32[8,128]{1,0:T(8,128)S(1)}, f32[8,128]{1,0:T(8,128)S(1)}, u32[]{:S(2)}, u32[]{:S(2)}) collective-permute-start(f32[8,128]{1,0:T(8,128)S(1)} %get-tuple-element.75), channel_id=1, source_target_pairs={{0,1},{1,0},{2,3},{3,2},{4,5},{5,4},{6,7},{7,6},{8,9},{9,8},{10,11... | collective-permute-start | bytes 12296 | tf_op jit(solution)/shard_map/ppermute | solution.py:650
  53.8 4.4 %collective-permute-start.7 = (f32[8,128]{1,0:T(8,128)S(1)}, f32[8,128]{1,0:T(8,128)S(1)}, u32[]{:S(2)}, u32[]{:S(2)}) collective-permute-start(f32[8,128]{1,0:T(8,128)S(1)} %get-tuple-element.76), channel_id=1, source_target_pairs={{1,2},{2,1},{5,6},{6,5},{9,10},{10,9},{13,14},{14,13},{17,18},{18,... | collective-permute-start | bytes 12296 | tf_op jit(solution)/shard_map/ppermute | solution.py:650
  59.9 4.8 %collective-permute-start.10 = (f32[88,128]{1,0:T(8,128)S(1)}, f32[88,128]{1,0:T(8,128)S(1)}, u32[]{:S(2)}, u32[]{:S(2)}) collective-permute-start(f32[88,128]{1,0:T(8,128)S(1)} %get-tuple-element.89), channel_id=1, source_target_pairs={{0,1},{1,0},{2,3},{3,2},{4,5},{5,4},{6,7},{7,6},{8,9},{9,8},{10,11... | collective-permute-start | bytes 135176 | tf_op jit(solution)/shard_map/ppermute | solution.py:650
  61.8 4.8 %collective-permute-start.11 = (f32[88,128]{1,0:T(8,128)S(1)}, f32[88,128]{1,0:T(8,128)S(1)}, u32[]{:S(2)}, u32[]{:S(2)}) collective-permute-start(f32[88,128]{1,0:T(8,128)S(1)} %get-tuple-element.90), channel_id=1, source_target_pairs={{1,2},{2,1},{5,6},{6,5},{9,10},{10,9},{13,14},{14,13},{17,18},{18,... | collective-permute-start | bytes 135176 | tf_op jit(solution)/shard_map/ppermute | solution.py:650
  66.8 8.7 %collective-permute-start.12 = (f32[56,128]{1,0:T(8,128)S(1)}, f32[56,128]{1,0:T(8,128)S(1)}, u32[]{:S(2)}, u32[]{:S(2)}) collective-permute-start(f32[56,128]{1,0:T(8,128)S(1)} %get-tuple-element.93), channel_id=1, source_target_pairs={{4,8},{8,4},{12,16},{16,12},{20,24},{24,20},{28,32},{32,28},{36,40... | collective-permute-start | bytes 86024 | tf_op jit(solution)/shard_map/ppermute | solution.py:650
  73.6 3.1 %collective-permute-start.13 = (f32[56,128]{1,0:T(8,128)S(1)}, f32[56,128]{1,0:T(8,128)S(1)}, u32[]{:S(2)}, u32[]{:S(2)}) collective-permute-start(f32[56,128]{1,0:T(8,128)S(1)} %get-tuple-element.94), channel_id=1, source_target_pairs={{0,4},{4,0},{8,12},{12,8},{16,20},{20,16},{24,28},{28,24},{32,36},... | collective-permute-start | bytes 86024 | tf_op jit(solution)/shard_map/ppermute | solution.py:650

commit v8 on v7

--- a/solution.py
+++ b/solution.py
@@ -22,9 +22,11 @@
 B = (2.0 * RHO1 / DELTA, 2.0 * RHO2 / DELTA, 2.0 * RHO3 / DELTA)
 
 XM1 = 104
-ZM1 = 99
+ZM1 = 104
 YM1 = 40
 XM2 = 80
+XE2 = 77
+LINES = 78
 ZM2 = 88
 YM2 = 56
 
@@ -43,13 +45,13 @@
 
 def put_out(stage, even, odd, axis):
     odd_one = parity(axis)
-    even[...] = stage[1 - odd_one]
+    even[...] = stage[1 - odd_one, 0 : even.shape[0], :]
     odd[...] = stage[odd_one]
 
 
 def take_in(halo, even, odd, axis):
     odd_one = parity(axis)
-    halo[1 - odd_one] = even[...]
+    halo[1 - odd_one, 0 : even.shape[0], :] = even[...]
     halo[odd_one] = odd[...]
 
 
@@ -208,6 +210,7 @@
         zp[side, 96:97, :] = combined_row(jnp.where(lane == 0, c[4], c[5]))
         zp[side, 97:98, :] = c[2][0:1]
         zp[side, 98:99, :] = c[3][NX - 1 :]
+        zp[side, 99:ZM1, :] = jnp.zeros((ZM1 - 99, NY), F32)
     put_out(zp, z_even, z_odd, "gz")
 
 
@@ -286,9 +289,9 @@
 
 
 def first_y_kernel(
-    xodd, xeven, zeven, zodd, xp, zp, yp,
-    xh, zh, even, odd, line_even, line_odd,
-    stage, lines,
+    xodd, zeven, zodd, xeven, xp, zp, yp,
+    xh, zh, even, odd,
+    stage,
 ):
     take_in(xh, xeven, xodd, "gx")
     take_in(zh, zeven, zodd, "gz")
@@ -296,12 +299,6 @@
     for side in (0, 1):
         stage[side, 0:32, :], stage[side, 32:40, :] = messages[side]
     put_out(stage, even, odd, "gy")
-    for side, z in ((0, 0), (1, NZ - 1)):
-        for end in (0, 1):
-            lines[side, end : end + 1, :] = xh[end, z : z + 1, :]
-            lines[side, 2 + end : 3 + end, :] = xh[end, 64 + z : 65 + z, :]
-        lines[side, 4:8, :] = jnp.zeros((4, NY), F32)
-    put_out(lines, line_even, line_odd, "gz")
 
 
 def z_halo_residual(side, res, zh1, yh, mine):
@@ -332,8 +329,8 @@
 
 def second_kernel(
     u, g, diag, s1, perm_sum, zp, yp, xp, last_coupling, xh, zh, yodd, yeven,
-    yh, s0, d0, b, xp2, cross2, zy2, even, odd,
-    cross, rsum, rows, edge_s, edge_d, stage,
+    yh, s0, d0, b, xp2, cross2, zy2, even, odd, line_even, line_odd,
+    cross, rsum, rows, edge_s, edge_d, stage, lines,
 ):
     take_in(yh, yeven, yodd, "gy")
     scale = 1.0 / THETA
@@ -406,6 +403,12 @@
             stage[side, 64 + 3 * z : 67 + 3 * z, :] = rhs[4 * z + side : 4 * z + side + 3]
         stage[side, 76:80, :] = last_coupling[side, 0:4, :]
     put_out(stage, even, odd, "gx")
+    for side, z in ((0, 0), (1, NZ - 1)):
+        for end in (0, 1):
+            lines[side, end : end + 1, :] = xh[end, z : z + 1, :]
+            lines[side, 2 + end : 3 + end, :] = xh[end, 64 + z : 65 + z, :]
+        lines[side, 4:LINES, :] = jnp.zeros((LINES - 4, NY), F32)
+    put_out(lines, line_even, line_odd, "gz")
 
 
 def edge_neighbours(rows_of, g, z):
@@ -664,21 +667,21 @@
     )(u, f, p, w)
     even, odd = swap(even, odd, "gx")
     zeven, zodd = swap(zeven, zodd, "gz")
-    xh, zh, yeven, yodd, line_even, line_odd = call(
+    xh, zh, yeven, yodd = call(
         first_y_kernel, "y_message", 7,
-        [(2, XM1, NY), (2, ZM1, NY), (YM1, NY), (YM1, NY), (8, NY), (8, NY)],
-        [(2, YM1, NY), (2, 8, NY)],
-    )(odd, even, zeven, zodd, xp, zp, yp)
+        [(2, XM1, NY), (2, ZM1, NY), (YM1, NY), (YM1, NY)],
+        [(2, YM1, NY)],
+    )(odd, zeven, zodd, even, xp, zp, yp)
     yeven, yodd = swap(yeven, yodd, "gy")
-    yh, s, d, b, xp2, cross2, zy2, even, odd = call(
+    yh, s, d, b, xp2, cross2, zy2, even, odd, line_even, line_odd = call(
         second_kernel, "two_steps", 13,
-        [(2, YM1, NY), FULL, FULL, (16, NY), (2, 64, NY), face, (3, NX, NY), (XM2, NY), (XM2, NY)],
-        [face, (4, NX, NY), (2, 16, NY), (2, NZ, 8, NY), (2, NZ, 8, NY), (2, XM2, NY)], 1.5,
+        [(2, YM1, NY), FULL, FULL, (16, NY), (2, 64, NY), face, (3, NX, NY), (XE2, NY), (XM2, NY), (LINES, NY), (LINES, NY)],
+        [face, (4, NX, NY), (2, 16, NY), (2, NZ, 8, NY), (2, NZ, 8, NY), (2, XM2, NY), (2, LINES, NY)], 1.5,
     )(u, g, diag, s, perm_sum, zp, yp, xp, last_coupling, xh, zh, yodd, yeven)
     even, odd = swap(even, odd, "gx")
     line_even, line_odd = swap(line_even, line_odd, "gz")
     s, d1, acc, zp2, yp2, xm, lh = call(
-        second_block_kernel, "block_2", 13, [FULL, FULL, FULL, (2, 64, NY), (64, NY), face, (2, 8, NY)], [FULL], 2.0
+        second_block_kernel, "block_2", 13, [FULL, FULL, FULL, (2, 64, NY), (64, NY), face, (2, LINES, NY)], [FULL], 0.01
     )(u, g, s, d, cross2, zy2, xp, xp2, zp, xh, zh, line_even, line_odd)
     xh2, even, odd, b3 = call(
         second_z_kernel, "z_message_2", 9, [(2, XM2, NY), (ZM2, NY), (ZM2, NY), (16, NY)], [(2, ZM2, NY), (16, NY)]

time: 79.1 us -> 78.1 us (0.987)
  the two profiles are of different devices: /device:TPU:277 before, /device:TPU:283 now
where the time goes in v8:
time: 78.1 us; the launch traced here: 77.6 us
  starting transfers between devices  60.4 us (77%)
  Pallas kernels  8.62 us (11%)
  waiting for transfers between devices  8.32 us (11%)
    ppermute x14, starting transfers between devices, swap(): results.append(lax.ppermute(values, axis, pairs))  60.4 us
    ppermute x14, waiting for transfers between devices, swap(): results.append(lax.ppermute(values, axis, pairs))  8.32 us
    pallas_call x1, Pallas kernels, per_device(): call(face_kernel, 'faces', 4, [FULL, FULL, FULL, BF16_FIELD, (2, XM1, NY)...  2.04 us
    pallas_call x1, Pallas kernels, per_device(): call(third_kernel, 'last_steps', 18, [FULL], [(2, YM2, NY), FULL, FULL, f...  1.93 us
    pallas_call x1, Pallas kernels, per_device(): call(second_block_kernel, 'block_2', 13, [FULL, FULL, FULL, (2, 64, NY),...  1.67 us
  transfers between devices with their start and end apart: 14, of which 6 were waited for; matrix products, arithmetic and copies ran while one was open for 0% of the time, Pallas kernels for 4%

profile of v8, /device:TPU:283, one launch (start us, length us, event | category | flops | bytes accessed | tf_op | source)
XLA Modules:
  0.0 77.6 jit_solution(17957685558559598904)
XLA Ops:
  0.0 2.0 %faces.1 = (f32[32,32,128]{2,1,0:T(8,128)S(1)}, f32[32,32,128]{2,1,0:T(8,128)S(1)}, f32[32,32,128]{2,1,0:T(8,128)S(1)}, bf16[3,32,32,128]{3,2,1,0:T(8,128)(2,1)S...) custom-call(f32[32,32,128]{2,1,0:T(8,128)} %u_far.1, ...), custom_call_target="tpu_custom_call" | custom-call | bytes 6000000 | tf_op jit(solution)/shard_map/faces/pallas_call | solution.py:660
  2.0 15.1 %collective-permute-start = (f32[104,128]{1,0:T(8,128)S(1)}, f32[104,128]{1,0:T(8,128)S(1)}, u32[]{:S(2)}, u32[]{:S(2)}) collective-permute-start(f32[104,128]{1,0:T(8,128)S(1)} %get-tuple-element.62), channel_id=1, source_target_pairs={{64,128},{128,64},{192,256},{256,192},{320,384},{384,320},{448,512... | collective-permute-start | bytes 159752 | tf_op jit(solution)/shard_map/ppermute | solution.py:653
  17.2 2.2 %collective-permute-start.1 = (f32[104,128]{1,0:T(8,128)S(1)}, f32[104,128]{1,0:T(8,128)S(1)}, u32[]{:S(2)}, u32[]{:S(2)}) collective-permute-start(f32[104,128]{1,0:T(8,128)S(1)} %get-tuple-element.63), channel_id=1, source_target_pairs={{0,1},{1,0},{2,3},{3,2},{4,5},{5,4},{6,7},{7,6},{8,9},{9,8},{10,11... | collective-permute-start | bytes 159752 | tf_op jit(solution)/shard_map/ppermute | solution.py:653
  19.3 3.8 %collective-permute-start.2 = (f32[104,128]{1,0:T(8,128)S(1)}, f32[104,128]{1,0:T(8,128)S(1)}, u32[]{:S(2)}, u32[]{:S(2)}) collective-permute-start(f32[104,128]{1,0:T(8,128)S(1)} %get-tuple-element.64), channel_id=1, source_target_pairs={{1,2},{2,1},{5,6},{6,5},{9,10},{10,9},{13,14},{14,13},{17,18},{18,... | collective-permute-start | bytes 159752 | tf_op jit(solution)/shard_map/ppermute | solution.py:653
  23.1 1.9 %collective-permute-start.3 = (f32[104,128]{1,0:T(8,128)S(1)}, f32[104,128]{1,0:T(8,128)S(1)}, u32[]{:S(2)}, u32[]{:S(2)}) collective-permute-start(f32[104,128]{1,0:T(8,128)S(1)} %get-tuple-element.65), channel_id=1, source_target_pairs={{0,64},{64,0},{128,192},{192,128},{256,320},{320,256},{384,448},{4... | collective-permute-start | bytes 159752 | tf_op jit(solution)/shard_map/ppermute | solution.py:653
  25.0 1.5 %block.1 = (f32[6,32,32,128]{3,2,1,0:T(8,128)S(1)}, f32[32,32,128]{2,1,0:T(8,128)S(1)}, f32[32,32,128]{2,1,0:T(8,128)S(1)}, f32[4,32,128]{2,1,0:T(8,128)S(1)}, f32[96,128]{1,0:T(8,128)S(1)}) custom-call(f32[32,32,128]{2,1,0:T(8,128)S(1)} %get-tuple-element.50.u, f32[32,32,128]{2,1,0:T(8,128)S(1)} %get-tuple-element.51.f, ...), custom_call_target="tpu_custom_call" | custom-call | bytes 7500000 | tf_op jit(solution)/shard_map/block/pallas_call | solution.py:665
  26.6 1.4 %collective-permute-done.3.xeven = f32[104,128]{1,0:T(8,128)S(1)} collective-permute-done((f32[104,128]{1,0:T(8,128)S(1)}, f32[104,128]{1,0:T(8,128)S(1)}, u32[]{:S(2)}, u32[]{:S(2)}) %collective-permute-start.3) | collective-permute-done | bytes 53280 | tf_op jit(solution)/shard_map/ppermute | solution.py:653
  28.2 5.2 %collective-permute-start.4 = (f32[40,128]{1,0:T(8,128)S(1)}, f32[40,128]{1,0:T(8,128)S(1)}, u32[]{:S(2)}, u32[]{:S(2)}) collective-permute-start(f32[40,128]{1,0:T(8,128)S(1)} %get-tuple-element.68), channel_id=1, source_target_pairs={{4,8},{8,4},{12,16},{16,12},{20,24},{24,20},{28,32},{32,28},{36,40... | collective-permute-start | bytes 61448 | tf_op jit(solution)/shard_map/ppermute | solution.py:653
  33.4 1.9 %collective-permute-start.5 = (f32[40,128]{1,0:T(8,128)S(1)}, f32[40,128]{1,0:T(8,128)S(1)}, u32[]{:S(2)}, u32[]{:S(2)}) collective-permute-start(f32[40,128]{1,0:T(8,128)S(1)} %get-tuple-element.69), channel_id=1, source_target_pairs={{0,4},{4,0},{8,12},{12,8},{16,20},{20,16},{24,28},{28,24},{32,36},... | collective-permute-start | bytes 61448 | tf_op jit(solution)/shard_map/ppermute | solution.py:653
  35.4 1.1 %collective-permute-done.5.yeven = f32[40,128]{1,0:T(8,128)S(1)} collective-permute-done((f32[40,128]{1,0:T(8,128)S(1)}, f32[40,128]{1,0:T(8,128)S(1)}, u32[]{:S(2)}, u32[]{:S(2)}) %collective-permute-start.5) | collective-permute-done | bytes 20512 | tf_op jit(solution)/shard_map/ppermute | solution.py:653
  36.5 1.0 %two_steps.1 = (f32[2,40,128]{2,1,0:T(8,128)S(1)}, f32[32,32,128]{2,1,0:T(8,128)S(1)}, f32[32,32,128]{2,1,0:T(8,128)S(1)}, f32[16,128]{1,0:T(8,128)S(1)}, f32[2,...) custom-call(f32[32,32,128]{2,1,0:T(8,128)S(1)} %get-tuple-element.50, ...), custom_call_target="tpu_custom_call" | custom-call | bytes 4500000 | tf_op jit(solution)/shard_map/two_steps/pallas_call | solution.py:676
  37.5 10.5 %collective-permute-start.8 = (f32[80,128]{1,0:T(8,128)S(1)}, f32[80,128]{1,0:T(8,128)S(1)}, u32[]{:S(2)}, u32[]{:S(2)}) collective-permute-start(f32[80,128]{1,0:T(8,128)S(1)} %get-tuple-element.84), channel_id=1, source_target_pairs={{64,128},{128,64},{192,256},{256,192},{320,384},{384,320},{448,512... | collective-permute-start | bytes 122888 | tf_op jit(solution)/shard_map/ppermute | solution.py:653
  48.0 2.2 %collective-permute-start.6 = (f32[78,128]{1,0:T(8,128)S(1)}, f32[78,128]{1,0:T(8,128)S(1)}, u32[]{:S(2)}, u32[]{:S(2)}) collective-permute-start(f32[78,128]{1,0:T(8,128)S(1)} %get-tuple-element.75), channel_id=1, source_target_pairs={{0,1},{1,0},{2,3},{3,2},{4,5},{5,4},{6,7},{7,6},{8,9},{9,8},{10,11... | collective-permute-start | bytes 119816 | tf_op jit(solution)/shard_map/ppermute | solution.py:653
  50.2 3.8 %collective-permute-start.7 = (f32[78,128]{1,0:T(8,128)S(1)}, f32[78,128]{1,0:T(8,128)S(1)}, u32[]{:S(2)}, u32[]{:S(2)}) collective-permute-start(f32[78,128]{1,0:T(8,128)S(1)} %get-tuple-element.76), channel_id=1, source_target_pairs={{1,2},{2,1},{5,6},{6,5},{9,10},{10,9},{13,14},{14,13},{17,18},{18,... | collective-permute-start | bytes 119816 | tf_op jit(solution)/shard_map/ppermute | solution.py:653
  54.0 1.9 %collective-permute-start.9 = (f32[77,128]{1,0:T(8,128)S(1)}, f32[77,128]{1,0:T(8,128)S(1)}, u32[]{:S(2)}, u32[]{:S(2)}) collective-permute-start(f32[77,128]{1,0:T(8,128)S(1)} %get-tuple-element.85), channel_id=1, source_target_pairs={{0,64},{64,0},{128,192},{192,128},{256,320},{320,256},{384,448},{4... | collective-permute-start | bytes 118280 | tf_op jit(solution)/shard_map/ppermute | solution.py:653
  55.9 1.7 %block_2.1 = (f32[32,32,128]{2,1,0:T(8,128)S(1)}, f32[32,32,128]{2,1,0:T(8,128)S(1)}, f32[32,32,128]{2,1,0:T(8,128)S(1)}, f32[2,64,128]{2,1,0:T(8,128)S(1)}, f32...) custom-call(f32[32,32,128]{2,1,0:T(8,128)S(1)} %get-tuple-element.50.u, ...), custom_call_target="tpu_custom_call" | custom-call | bytes 30000 | tf_op jit(solution)/shard_map/block_2/pallas_call | solution.py:683
  57.6 1.4 %collective-permute-done.9.xeven = f32[77,128]{1,0:T(8,128)S(1)} collective-permute-done((f32[77,128]{1,0:T(8,128)S(1)}, f32[77,128]{1,0:T(8,128)S(1)}, u32[]{:S(2)}, u32[]{:S(2)}) %collective-permute-start.9) | collective-permute-done | bytes 39456 | tf_op jit(solution)/shard_map/ppermute | solution.py:653
  59.1 1.9 %collective-permute-start.10 = (f32[88,128]{1,0:T(8,128)S(1)}, f32[88,128]{1,0:T(8,128)S(1)}, u32[]{:S(2)}, u32[]{:S(2)}) collective-permute-start(f32[88,128]{1,0:T(8,128)S(1)} %get-tuple-element.89), channel_id=1, source_target_pairs={{0,1},{1,0},{2,3},{3,2},{4,5},{5,4},{6,7},{7,6},{8,9},{9,8},{10,11... | collective-permute-start | bytes 135176 | tf_op jit(solution)/shard_map/ppermute | solution.py:653
  61.1 1.9 %collective-permute-start.11 = (f32[88,128]{1,0:T(8,128)S(1)}, f32[88,128]{1,0:T(8,128)S(1)}, u32[]{:S(2)}, u32[]{:S(2)}) collective-permute-start(f32[88,128]{1,0:T(8,128)S(1)} %get-tuple-element.90), channel_id=1, source_target_pairs={{1,2},{2,1},{5,6},{6,5},{9,10},{10,9},{13,14},{14,13},{17,18},{18,... | collective-permute-start | bytes 135176 | tf_op jit(solution)/shard_map/ppermute | solution.py:653
  63.9 2.2 %collective-permute-done.11.zodd = f32[88,128]{1,0:T(8,128)S(1)} collective-permute-done((f32[88,128]{1,0:T(8,128)S(1)}, f32[88,128]{1,0:T(8,128)S(1)}, u32[]{:S(2)}, u32[]{:S(2)}) %collective-permute-start.11) | collective-permute-done | bytes 45088 | tf_op jit(solution)/shard_map/ppermute | solution.py:653
  66.3 6.2 %collective-permute-start.12 = (f32[56,128]{1,0:T(8,128)S(1)}, f32[56,128]{1,0:T(8,128)S(1)}, u32[]{:S(2)}, u32[]{:S(2)}) collective-permute-start(f32[56,128]{1,0:T(8,128)S(1)} %get-tuple-element.93), channel_id=1, source_target_pairs={{4,8},{8,4},{12,16},{16,12},{20,24},{24,20},{28,32},{32,28},{36,40... | collective-permute-start | bytes 86024 | tf_op jit(solution)/shard_map/ppermute | solution.py:653
  72.5 1.9 %collective-permute-start.13 = (f32[56,128]{1,0:T(8,128)S(1)}, f32[56,128]{1,0:T(8,128)S(1)}, u32[]{:S(2)}, u32[]{:S(2)}) collective-permute-start(f32[56,128]{1,0:T(8,128)S(1)} %get-tuple-element.94), channel_id=1, source_target_pairs={{0,4},{4,0},{8,12},{12,8},{16,20},{20,16},{24,28},{28,24},{32,36},... | collective-permute-start | bytes 86024 | tf_op jit(solution)/shard_map/ppermute | solution.py:653
  74.5 1.2 %collective-permute-done.13.yeven = f32[56,128]{1,0:T(8,128)S(1)} collective-permute-done((f32[56,128]{1,0:T(8,128)S(1)}, f32[56,128]{1,0:T(8,128)S(1)}, u32[]{:S(2)}, u32[]{:S(2)}) %collective-permute-start.13) | collective-permute-done | bytes 28704 | tf_op jit(solution)/shard_map/ppermute | solution.py:653
  75.6 1.9 %last_steps.1 = f32[32,32,128]{2,1,0:T(8,128)} custom-call(f32[6,32,32,128]{3,2,1,0:T(8,128)S(1)} %get-tuple-element.54.g, f32[32,32,128]{2,1,0:T(8,128)S(1)} %get-tuple-element.77.s2, f32[32,32,128]{2,1,0:T(8,128)S(1)} %get-tuple-element.78.d1, f32[32,32,128]{2,1,0:T(8,128)S(1)} %get-tuple-element.79.acc, f32[2,104,128]{2,1,0:T(8,128)S(1)} %get-tuple-element.58.zp, ...), custom_call_target="tpu_custom_call" | custom-call | bytes 7500000 | tf_op jit(solution)/shard_map/last_steps/pallas_call | solution.py:694
  (12 shorter events, 1.5 us)
Async XLA Ops:
  2.0 24.5 %collective-permute-start = (f32[104,128]{1,0:T(8,128)S(1)}, f32[104,128]{1,0:T(8,128)S(1)}, u32[]{:S(2)}, u32[]{:S(2)}) collective-permute-start(f32[104,128]{1,0:T(8,128)S(1)} %get-tuple-element.62), channel_id=1, source_target_pairs={{64,128},{128,64},{192,256},{256,192},{320,384},{384,320},{448,512... | collective-permute-start | bytes 159752 | tf_op jit(solution)/shard_map/ppermute | solution.py:653
  17.2 9.4 %collective-permute-start.1 = (f32[104,128]{1,0:T(8,128)S(1)}, f32[104,128]{1,0:T(8,128)S(1)}, u32[]{:S(2)}, u32[]{:S(2)}) collective-permute-start(f32[104,128]{1,0:T(8,128)S(1)} %get-tuple-element.63), channel_id=1, source_target_pairs={{0,1},{1,0},{2,3},{3,2},{4,5},{5,4},{6,7},{7,6},{8,9},{9,8},{10,11... | collective-permute-start | bytes 159752 | tf_op jit(solution)/shard_map/ppermute | solution.py:653
  19.3 7.2 %collective-permute-start.2 = (f32[104,128]{1,0:T(8,128)S(1)}, f32[104,128]{1,0:T(8,128)S(1)}, u32[]{:S(2)}, u32[]{:S(2)}) collective-permute-start(f32[104,128]{1,0:T(8,128)S(1)} %get-tuple-element.64), channel_id=1, source_target_pairs={{1,2},{2,1},{5,6},{6,5},{9,10},{10,9},{13,14},{14,13},{17,18},{18,... | collective-permute-start | bytes 159752 | tf_op jit(solution)/shard_map/ppermute | solution.py:653
  23.1 4.9 %collective-permute-start.3 = (f32[104,128]{1,0:T(8,128)S(1)}, f32[104,128]{1,0:T(8,128)S(1)}, u32[]{:S(2)}, u32[]{:S(2)}) collective-permute-start(f32[104,128]{1,0:T(8,128)S(1)} %get-tuple-element.65), channel_id=1, source_target_pairs={{0,64},{64,0},{128,192},{192,128},{256,320},{320,256},{384,448},{4... | collective-permute-start | bytes 159752 | tf_op jit(solution)/shard_map/ppermute | solution.py:653
  28.2 7.1 %collective-permute-start.4 = (f32[40,128]{1,0:T(8,128)S(1)}, f32[40,128]{1,0:T(8,128)S(1)}, u32[]{:S(2)}, u32[]{:S(2)}) collective-permute-start(f32[40,128]{1,0:T(8,128)S(1)} %get-tuple-element.68), channel_id=1, source_target_pairs={{4,8},{8,4},{12,16},{16,12},{20,24},{24,20},{28,32},{32,28},{36,40... | collective-permute-start | bytes 61448 | tf_op jit(solution)/shard_map/ppermute | solution.py:653
  33.4 3.1 %collective-permute-start.5 = (f32[40,128]{1,0:T(8,128)S(1)}, f32[40,128]{1,0:T(8,128)S(1)}, u32[]{:S(2)}, u32[]{:S(2)}) collective-permute-start(f32[40,128]{1,0:T(8,128)S(1)} %get-tuple-element.69), channel_id=1, source_target_pairs={{0,4},{4,0},{8,12},{12,8},{16,20},{20,16},{24,28},{28,24},{32,36},... | collective-permute-start | bytes 61448 | tf_op jit(solution)/shard_map/ppermute | solution.py:653
  37.5 21.6 %collective-permute-start.8 = (f32[80,128]{1,0:T(8,128)S(1)}, f32[80,128]{1,0:T(8,128)S(1)}, u32[]{:S(2)}, u32[]{:S(2)}) collective-permute-start(f32[80,128]{1,0:T(8,128)S(1)} %get-tuple-element.84), channel_id=1, source_target_pairs={{64,128},{128,64},{192,256},{256,192},{320,384},{384,320},{448,512... | collective-permute-start | bytes 122888 | tf_op jit(solution)/shard_map/ppermute | solution.py:653
  48.0 7.9 %collective-permute-start.6 = (f32[78,128]{1,0:T(8,128)S(1)}, f32[78,128]{1,0:T(8,128)S(1)}, u32[]{:S(2)}, u32[]{:S(2)}) collective-permute-start(f32[78,128]{1,0:T(8,128)S(1)} %get-tuple-element.75), channel_id=1, source_target_pairs={{0,1},{1,0},{2,3},{3,2},{4,5},{5,4},{6,7},{7,6},{8,9},{9,8},{10,11... | collective-permute-start | bytes 119816 | tf_op jit(solution)/shard_map/ppermute | solution.py:653
  50.2 5.7 %collective-permute-start.7 = (f32[78,128]{1,0:T(8,128)S(1)}, f32[78,128]{1,0:T(8,128)S(1)}, u32[]{:S(2)}, u32[]{:S(2)}) collective-permute-start(f32[78,128]{1,0:T(8,128)S(1)} %get-tuple-element.76), channel_id=1, source_target_pairs={{1,2},{2,1},{5,6},{6,5},{9,10},{10,9},{13,14},{14,13},{17,18},{18,... | collective-permute-start | bytes 119816 | tf_op jit(solution)/shard_map/ppermute | solution.py:653
  54.0 5.0 %collective-permute-start.9 = (f32[77,128]{1,0:T(8,128)S(1)}, f32[77,128]{1,0:T(8,128)S(1)}, u32[]{:S(2)}, u32[]{:S(2)}) collective-permute-start(f32[77,128]{1,0:T(8,128)S(1)} %get-tuple-element.85), channel_id=1, source_target_pairs={{0,64},{64,0},{128,192},{192,128},{256,320},{320,256},{384,448},{4... | collective-permute-start | bytes 118280 | tf_op jit(solution)/shard_map/ppermute | solution.py:653
  59.1 4.8 %collective-permute-start.10 = (f32[88,128]{1,0:T(8,128)S(1)}, f32[88,128]{1,0:T(8,128)S(1)}, u32[]{:S(2)}, u32[]{:S(2)}) collective-permute-start(f32[88,128]{1,0:T(8,128)S(1)} %get-tuple-element.89), channel_id=1, source_target_pairs={{0,1},{1,0},{2,3},{3,2},{4,5},{5,4},{6,7},{7,6},{8,9},{9,8},{10,11... | collective-permute-start | bytes 135176 | tf_op jit(solution)/shard_map/ppermute | solution.py:653
  61.1 5.1 %collective-permute-start.11 = (f32[88,128]{1,0:T(8,128)S(1)}, f32[88,128]{1,0:T(8,128)S(1)}, u32[]{:S(2)}, u32[]{:S(2)}) collective-permute-start(f32[88,128]{1,0:T(8,128)S(1)} %get-tuple-element.90), channel_id=1, source_target_pairs={{1,2},{2,1},{5,6},{6,5},{9,10},{10,9},{13,14},{14,13},{17,18},{18,... | collective-permute-start | bytes 135176 | tf_op jit(solution)/shard_map/ppermute | solution.py:653
  66.3 8.1 %collective-permute-start.12 = (f32[56,128]{1,0:T(8,128)S(1)}, f32[56,128]{1,0:T(8,128)S(1)}, u32[]{:S(2)}, u32[]{:S(2)}) collective-permute-start(f32[56,128]{1,0:T(8,128)S(1)} %get-tuple-element.93), channel_id=1, source_target_pairs={{4,8},{8,4},{12,16},{16,12},{20,24},{24,20},{28,32},{32,28},{36,40... | collective-permute-start | bytes 86024 | tf_op jit(solution)/shard_map/ppermute | solution.py:653
  72.5 3.1 %collective-permute-start.13 = (f32[56,128]{1,0:T(8,128)S(1)}, f32[56,128]{1,0:T(8,128)S(1)}, u32[]{:S(2)}, u32[]{:S(2)}) collective-permute-start(f32[56,128]{1,0:T(8,128)S(1)} %get-tuple-element.94), channel_id=1, source_target_pairs={{0,4},{4,0},{8,12},{12,8},{16,20},{20,16},{24,28},{28,24},{32,36},... | collective-permute-start | bytes 86024 | tf_op jit(solution)/shard_map/ppermute | solution.py:653

commit v9 on v8

--- a/solution.py
+++ b/solution.py
@@ -289,7 +289,7 @@
 
 
 def first_y_kernel(
-    xodd, zeven, zodd, xeven, xp, zp, yp,
+    xodd, zodd, zeven, xeven, xp, zp, yp,
     xh, zh, even, odd,
     stage,
 ):
@@ -423,7 +423,7 @@
 
 
 def second_block_kernel(
-    u, g, s0, d0, cross2, zy2, xp, xp2, zp, xh, zh, line_even, line_odd,
+    u, g, s0, d0, cross2, zy2, xp, xp2, zp, xh, zh, line_odd, line_even,
     s, d, acc, zp2, yp2, xm, lh,
     s1,
 ):
@@ -507,7 +507,7 @@
     put_out(stage, even, odd, "gz")
 
 
-def second_y_kernel(zeven, zodd, xp, zp, yp2, xh2, b3, zh2, even, odd, stage):
+def second_y_kernel(zodd, zeven, xp, zp, yp2, xh2, b3, zh2, even, odd, stage):
     take_in(zh2, zeven, zodd, "gz")
     messages = y_part(yp2[0:32, :], yp2[32:64, :], None, zp, zh2, xp, xh2)
     within = lax.rem(iota((16, NY), 1), 32)
@@ -671,7 +671,7 @@
         first_y_kernel, "y_message", 7,
         [(2, XM1, NY), (2, ZM1, NY), (YM1, NY), (YM1, NY)],
         [(2, YM1, NY)],
-    )(odd, zeven, zodd, even, xp, zp, yp)
+    )(odd, zodd, zeven, even, xp, zp, yp)
     yeven, yodd = swap(yeven, yodd, "gy")
     yh, s, d, b, xp2, cross2, zy2, even, odd, line_even, line_odd = call(
         second_kernel, "two_steps", 13,
@@ -682,14 +682,14 @@
     line_even, line_odd = swap(line_even, line_odd, "gz")
     s, d1, acc, zp2, yp2, xm, lh = call(
         second_block_kernel, "block_2", 13, [FULL, FULL, FULL, (2, 64, NY), (64, NY), face, (2, LINES, NY)], [FULL], 0.01
-    )(u, g, s, d, cross2, zy2, xp, xp2, zp, xh, zh, line_even, line_odd)
+    )(u, g, s, d, cross2, zy2, xp, xp2, zp, xh, zh, line_odd, line_even)
     xh2, even, odd, b3 = call(
         second_z_kernel, "z_message_2", 9, [(2, XM2, NY), (ZM2, NY), (ZM2, NY), (16, NY)], [(2, ZM2, NY), (16, NY)]
     )(odd, even, xp, zp, zp2, b, xh, zh, lh)
     even, odd = swap(even, odd, "gz")
     zh2, even, odd = call(
         second_y_kernel, "y_message_2", 7, [(2, ZM2, NY), (YM2, NY), (YM2, NY)], [(2, YM2, NY)]
-    )(even, odd, xp, zp, yp2, xh2, b3)
+    )(odd, even, xp, zp, yp2, xh2, b3)
     even, odd = swap(even, odd, "gy")
     (out,) = call(
         third_kernel, "last_steps", 18, [FULL],

time: 78.1 us -> 77.4 us (level)
  transfers between devices with their start and end apart: 14 -> 14, of which waited for: 6 -> 7; matrix products, arithmetic and copies ran while one was open for 0% -> 0% of each run, Pallas kernels for 4% -> 4%
where the time goes in v9:
time: 77.4 us; the launch traced here: 76.9 us
  starting transfers between devices  59.8 us (77%)
  Pallas kernels  8.61 us (11%)
  waiting for transfers between devices  8.26 us (11%)
    ppermute x14, starting transfers between devices, swap(): results.append(lax.ppermute(values, axis, pairs))  59.8 us
    ppermute x14, waiting for transfers between devices, swap(): results.append(lax.ppermute(values, axis, pairs))  8.26 us
    pallas_call x1, Pallas kernels, per_device(): call(face_kernel, 'faces', 4, [FULL, FULL, FULL, BF16_FIELD, (2, XM1, NY)...  2.04 us
    pallas_call x1, Pallas kernels, per_device(): call(third_kernel, 'last_steps', 18, [FULL], [(2, YM2, NY), FULL, FULL, f...  1.93 us
    pallas_call x1, Pallas kernels, per_device(): call(second_block_kernel, 'block_2', 13, [FULL, FULL, FULL, (2, 64, NY),...  1.67 us
  transfers between devices with their start and end apart: 14, of which 7 were waited for; matrix products, arithmetic and copies ran while one was open for 0% of the time, Pallas kernels for 4%

profile of v9, /device:TPU:283, one launch (start us, length us, event | category | flops | bytes accessed | tf_op | source)
XLA Modules:
  0.0 76.9 jit_solution(2841050549070416074)
XLA Ops:
  0.0 2.0 %faces.1 = (f32[32,32,128]{2,1,0:T(8,128)S(1)}, f32[32,32,128]{2,1,0:T(8,128)S(1)}, f32[32,32,128]{2,1,0:T(8,128)S(1)}, bf16[3,32,32,128]{3,2,1,0:T(8,128)(2,1)S...) custom-call(f32[32,32,128]{2,1,0:T(8,128)} %u_far.1, ...), custom_call_target="tpu_custom_call" | custom-call | bytes 6000000 | tf_op jit(solution)/shard_map/faces/pallas_call | solution.py:660
  2.0 15.1 %collective-permute-start = (f32[104,128]{1,0:T(8,128)S(1)}, f32[104,128]{1,0:T(8,128)S(1)}, u32[]{:S(2)}, u32[]{:S(2)}) collective-permute-start(f32[104,128]{1,0:T(8,128)S(1)} %get-tuple-element.62), channel_id=1, source_target_pairs={{64,128},{128,64},{192,256},{256,192},{320,384},{384,320},{448,512... | collective-permute-start | bytes 159752 | tf_op jit(solution)/shard_map/ppermute | solution.py:653
  17.2 3.1 %collective-permute-start.1 = (f32[104,128]{1,0:T(8,128)S(1)}, f32[104,128]{1,0:T(8,128)S(1)}, u32[]{:S(2)}, u32[]{:S(2)}) collective-permute-start(f32[104,128]{1,0:T(8,128)S(1)} %get-tuple-element.63), channel_id=1, source_target_pairs={{1,2},{2,1},{5,6},{6,5},{9,10},{10,9},{13,14},{14,13},{17,18},{18,... | collective-permute-start | bytes 159752 | tf_op jit(solution)/shard_map/ppermute | solution.py:653
  20.3 1.9 %collective-permute-start.2 = (f32[104,128]{1,0:T(8,128)S(1)}, f32[104,128]{1,0:T(8,128)S(1)}, u32[]{:S(2)}, u32[]{:S(2)}) collective-permute-start(f32[104,128]{1,0:T(8,128)S(1)} %get-tuple-element.64), channel_id=1, source_target_pairs={{0,1},{1,0},{2,3},{3,2},{4,5},{5,4},{6,7},{7,6},{8,9},{9,8},{10,11... | collective-permute-start | bytes 159752 | tf_op jit(solution)/shard_map/ppermute | solution.py:653
  22.2 1.9 %collective-permute-start.3 = (f32[104,128]{1,0:T(8,128)S(1)}, f32[104,128]{1,0:T(8,128)S(1)}, u32[]{:S(2)}, u32[]{:S(2)}) collective-permute-start(f32[104,128]{1,0:T(8,128)S(1)} %get-tuple-element.65), channel_id=1, source_target_pairs={{0,64},{64,0},{128,192},{192,128},{256,320},{320,256},{384,448},{4... | collective-permute-start | bytes 159752 | tf_op jit(solution)/shard_map/ppermute | solution.py:653
  24.1 1.5 %block.1 = (f32[6,32,32,128]{3,2,1,0:T(8,128)S(1)}, f32[32,32,128]{2,1,0:T(8,128)S(1)}, f32[32,32,128]{2,1,0:T(8,128)S(1)}, f32[4,32,128]{2,1,0:T(8,128)S(1)}, f32[96,128]{1,0:T(8,128)S(1)}) custom-call(f32[32,32,128]{2,1,0:T(8,128)S(1)} %get-tuple-element.50.u, f32[32,32,128]{2,1,0:T(8,128)S(1)} %get-tuple-element.51.f, ...), custom_call_target="tpu_custom_call" | custom-call | bytes 7500000 | tf_op jit(solution)/shard_map/block/pallas_call | solution.py:665
  25.7 1.5 %collective-permute-done.3.xeven = f32[104,128]{1,0:T(8,128)S(1)} collective-permute-done((f32[104,128]{1,0:T(8,128)S(1)}, f32[104,128]{1,0:T(8,128)S(1)}, u32[]{:S(2)}, u32[]{:S(2)}) %collective-permute-start.3) | collective-permute-done | bytes 53280 | tf_op jit(solution)/shard_map/ppermute | solution.py:653
  27.4 4.9 %collective-permute-start.4 = (f32[40,128]{1,0:T(8,128)S(1)}, f32[40,128]{1,0:T(8,128)S(1)}, u32[]{:S(2)}, u32[]{:S(2)}) collective-permute-start(f32[40,128]{1,0:T(8,128)S(1)} %get-tuple-element.68), channel_id=1, source_target_pairs={{4,8},{8,4},{12,16},{16,12},{20,24},{24,20},{28,32},{32,28},{36,40... | collective-permute-start | bytes 61448 | tf_op jit(solution)/shard_map/ppermute | solution.py:653
  32.2 1.9 %collective-permute-start.5 = (f32[40,128]{1,0:T(8,128)S(1)}, f32[40,128]{1,0:T(8,128)S(1)}, u32[]{:S(2)}, u32[]{:S(2)}) collective-permute-start(f32[40,128]{1,0:T(8,128)S(1)} %get-tuple-element.69), channel_id=1, source_target_pairs={{0,4},{4,0},{8,12},{12,8},{16,20},{20,16},{24,28},{28,24},{32,36},... | collective-permute-start | bytes 61448 | tf_op jit(solution)/shard_map/ppermute | solution.py:653
  34.2 1.1 %collective-permute-done.5.yeven = f32[40,128]{1,0:T(8,128)S(1)} collective-permute-done((f32[40,128]{1,0:T(8,128)S(1)}, f32[40,128]{1,0:T(8,128)S(1)}, u32[]{:S(2)}, u32[]{:S(2)}) %collective-permute-start.5) | collective-permute-done | bytes 20512 | tf_op jit(solution)/shard_map/ppermute | solution.py:653
  35.3 1.0 %two_steps.1 = (f32[2,40,128]{2,1,0:T(8,128)S(1)}, f32[32,32,128]{2,1,0:T(8,128)S(1)}, f32[32,32,128]{2,1,0:T(8,128)S(1)}, f32[16,128]{1,0:T(8,128)S(1)}, f32[2,...) custom-call(f32[32,32,128]{2,1,0:T(8,128)S(1)} %get-tuple-element.50, ...), custom_call_target="tpu_custom_call" | custom-call | bytes 4500000 | tf_op jit(solution)/shard_map/two_steps/pallas_call | solution.py:676
  36.3 11.7 %collective-permute-start.8 = (f32[80,128]{1,0:T(8,128)S(1)}, f32[80,128]{1,0:T(8,128)S(1)}, u32[]{:S(2)}, u32[]{:S(2)}) collective-permute-start(f32[80,128]{1,0:T(8,128)S(1)} %get-tuple-element.84), channel_id=1, source_target_pairs={{64,128},{128,64},{192,256},{256,192},{320,384},{384,320},{448,512... | collective-permute-start | bytes 122888 | tf_op jit(solution)/shard_map/ppermute | solution.py:653
  48.0 3.1 %collective-permute-start.6 = (f32[78,128]{1,0:T(8,128)S(1)}, f32[78,128]{1,0:T(8,128)S(1)}, u32[]{:S(2)}, u32[]{:S(2)}) collective-permute-start(f32[78,128]{1,0:T(8,128)S(1)} %get-tuple-element.75), channel_id=1, source_target_pairs={{1,2},{2,1},{5,6},{6,5},{9,10},{10,9},{13,14},{14,13},{17,18},{18,... | collective-permute-start | bytes 119816 | tf_op jit(solution)/shard_map/ppermute | solution.py:653
  51.1 1.9 %collective-permute-start.7 = (f32[78,128]{1,0:T(8,128)S(1)}, f32[78,128]{1,0:T(8,128)S(1)}, u32[]{:S(2)}, u32[]{:S(2)}) collective-permute-start(f32[78,128]{1,0:T(8,128)S(1)} %get-tuple-element.76), channel_id=1, source_target_pairs={{0,1},{1,0},{2,3},{3,2},{4,5},{5,4},{6,7},{7,6},{8,9},{9,8},{10,11... | collective-permute-start | bytes 119816 | tf_op jit(solution)/shard_map/ppermute | solution.py:653
  53.1 1.9 %collective-permute-start.9 = (f32[77,128]{1,0:T(8,128)S(1)}, f32[77,128]{1,0:T(8,128)S(1)}, u32[]{:S(2)}, u32[]{:S(2)}) collective-permute-start(f32[77,128]{1,0:T(8,128)S(1)} %get-tuple-element.85), channel_id=1, source_target_pairs={{0,64},{64,0},{128,192},{192,128},{256,320},{320,256},{384,448},{4... | collective-permute-start | bytes 118280 | tf_op jit(solution)/shard_map/ppermute | solution.py:653
  55.0 1.2 %collective-permute-done.7.line_even = f32[78,128]{1,0:T(8,128)S(1)} collective-permute-done((f32[78,128]{1,0:T(8,128)S(1)}, f32[78,128]{1,0:T(8,128)S(1)}, u32[]{:S(2)}, u32[]{:S(2)}) %collective-permute-start.7) | collective-permute-done | bytes 39968 | tf_op jit(solution)/shard_map/ppermute | solution.py:653
  56.2 1.7 %block_2.1 = (f32[32,32,128]{2,1,0:T(8,128)S(1)}, f32[32,32,128]{2,1,0:T(8,128)S(1)}, f32[32,32,128]{2,1,0:T(8,128)S(1)}, f32[2,64,128]{2,1,0:T(8,128)S(1)}, f32...) custom-call(f32[32,32,128]{2,1,0:T(8,128)S(1)} %get-tuple-element.50.u, ...), custom_call_target="tpu_custom_call" | custom-call | bytes 30000 | tf_op jit(solution)/shard_map/block_2/pallas_call | solution.py:683
  58.2 2.2 %collective-permute-start.10 = (f32[88,128]{1,0:T(8,128)S(1)}, f32[88,128]{1,0:T(8,128)S(1)}, u32[]{:S(2)}, u32[]{:S(2)}) collective-permute-start(f32[88,128]{1,0:T(8,128)S(1)} %get-tuple-element.89), channel_id=1, source_target_pairs={{1,2},{2,1},{5,6},{6,5},{9,10},{10,9},{13,14},{14,13},{17,18},{18,... | collective-permute-start | bytes 135176 | tf_op jit(solution)/shard_map/ppermute | solution.py:653
  60.4 1.9 %collective-permute-start.11 = (f32[88,128]{1,0:T(8,128)S(1)}, f32[88,128]{1,0:T(8,128)S(1)}, u32[]{:S(2)}, u32[]{:S(2)}) collective-permute-start(f32[88,128]{1,0:T(8,128)S(1)} %get-tuple-element.90), channel_id=1, source_target_pairs={{0,1},{1,0},{2,3},{3,2},{4,5},{5,4},{6,7},{7,6},{8,9},{9,8},{10,11... | collective-permute-start | bytes 135176 | tf_op jit(solution)/shard_map/ppermute | solution.py:653
  63.0 2.3 %collective-permute-done.11.zeven = f32[88,128]{1,0:T(8,128)S(1)} collective-permute-done((f32[88,128]{1,0:T(8,128)S(1)}, f32[88,128]{1,0:T(8,128)S(1)}, u32[]{:S(2)}, u32[]{:S(2)}) %collective-permute-start.11) | collective-permute-done | bytes 45088 | tf_op jit(solution)/shard_map/ppermute | solution.py:653
  65.6 6.3 %collective-permute-start.12 = (f32[56,128]{1,0:T(8,128)S(1)}, f32[56,128]{1,0:T(8,128)S(1)}, u32[]{:S(2)}, u32[]{:S(2)}) collective-permute-start(f32[56,128]{1,0:T(8,128)S(1)} %get-tuple-element.93), channel_id=1, source_target_pairs={{4,8},{8,4},{12,16},{16,12},{20,24},{24,20},{28,32},{32,28},{36,40... | collective-permute-start | bytes 86024 | tf_op jit(solution)/shard_map/ppermute | solution.py:653
  71.9 1.9 %collective-permute-start.13 = (f32[56,128]{1,0:T(8,128)S(1)}, f32[56,128]{1,0:T(8,128)S(1)}, u32[]{:S(2)}, u32[]{:S(2)}) collective-permute-start(f32[56,128]{1,0:T(8,128)S(1)} %get-tuple-element.94), channel_id=1, source_target_pairs={{0,4},{4,0},{8,12},{12,8},{16,20},{20,16},{24,28},{28,24},{32,36},... | collective-permute-start | bytes 86024 | tf_op jit(solution)/shard_map/ppermute | solution.py:653
  73.8 1.2 %collective-permute-done.13.yeven = f32[56,128]{1,0:T(8,128)S(1)} collective-permute-done((f32[56,128]{1,0:T(8,128)S(1)}, f32[56,128]{1,0:T(8,128)S(1)}, u32[]{:S(2)}, u32[]{:S(2)}) %collective-permute-start.13) | collective-permute-done | bytes 28704 | tf_op jit(solution)/shard_map/ppermute | solution.py:653
  75.0 1.9 %last_steps.1 = f32[32,32,128]{2,1,0:T(8,128)} custom-call(f32[6,32,32,128]{3,2,1,0:T(8,128)S(1)} %get-tuple-element.54.g, f32[32,32,128]{2,1,0:T(8,128)S(1)} %get-tuple-element.77.s2, f32[32,32,128]{2,1,0:T(8,128)S(1)} %get-tuple-element.78.d1, f32[32,32,128]{2,1,0:T(8,128)S(1)} %get-tuple-element.79.acc, f32[2,104,128]{2,1,0:T(8,128)S(1)} %get-tuple-element.58.zp, ...), custom_call_target="tpu_custom_call" | custom-call | bytes 7500000 | tf_op jit(solution)/shard_map/last_steps/pallas_call | solution.py:694
  (12 shorter events, 1.5 us)
Async XLA Ops:
  2.0 23.6 %collective-permute-start = (f32[104,128]{1,0:T(8,128)S(1)}, f32[104,128]{1,0:T(8,128)S(1)}, u32[]{:S(2)}, u32[]{:S(2)}) collective-permute-start(f32[104,128]{1,0:T(8,128)S(1)} %get-tuple-element.62), channel_id=1, source_target_pairs={{64,128},{128,64},{192,256},{256,192},{320,384},{384,320},{448,512... | collective-permute-start | bytes 159752 | tf_op jit(solution)/shard_map/ppermute | solution.py:653
  17.2 8.5 %collective-permute-start.1 = (f32[104,128]{1,0:T(8,128)S(1)}, f32[104,128]{1,0:T(8,128)S(1)}, u32[]{:S(2)}, u32[]{:S(2)}) collective-permute-start(f32[104,128]{1,0:T(8,128)S(1)} %get-tuple-element.63), channel_id=1, source_target_pairs={{1,2},{2,1},{5,6},{6,5},{9,10},{10,9},{13,14},{14,13},{17,18},{18,... | collective-permute-start | bytes 159752 | tf_op jit(solution)/shard_map/ppermute | solution.py:653
  20.3 5.4 %collective-permute-start.2 = (f32[104,128]{1,0:T(8,128)S(1)}, f32[104,128]{1,0:T(8,128)S(1)}, u32[]{:S(2)}, u32[]{:S(2)}) collective-permute-start(f32[104,128]{1,0:T(8,128)S(1)} %get-tuple-element.64), channel_id=1, source_target_pairs={{0,1},{1,0},{2,3},{3,2},{4,5},{5,4},{6,7},{7,6},{8,9},{9,8},{10,11... | collective-permute-start | bytes 159752 | tf_op jit(solution)/shard_map/ppermute | solution.py:653
  22.2 4.9 %collective-permute-start.3 = (f32[104,128]{1,0:T(8,128)S(1)}, f32[104,128]{1,0:T(8,128)S(1)}, u32[]{:S(2)}, u32[]{:S(2)}) collective-permute-start(f32[104,128]{1,0:T(8,128)S(1)} %get-tuple-element.65), channel_id=1, source_target_pairs={{0,64},{64,0},{128,192},{192,128},{256,320},{320,256},{384,448},{4... | collective-permute-start | bytes 159752 | tf_op jit(solution)/shard_map/ppermute | solution.py:653
  27.4 6.8 %collective-permute-start.4 = (f32[40,128]{1,0:T(8,128)S(1)}, f32[40,128]{1,0:T(8,128)S(1)}, u32[]{:S(2)}, u32[]{:S(2)}) collective-permute-start(f32[40,128]{1,0:T(8,128)S(1)} %get-tuple-element.68), channel_id=1, source_target_pairs={{4,8},{8,4},{12,16},{16,12},{20,24},{24,20},{28,32},{32,28},{36,40... | collective-permute-start | bytes 61448 | tf_op jit(solution)/shard_map/ppermute | solution.py:653
  32.2 3.1 %collective-permute-start.5 = (f32[40,128]{1,0:T(8,128)S(1)}, f32[40,128]{1,0:T(8,128)S(1)}, u32[]{:S(2)}, u32[]{:S(2)}) collective-permute-start(f32[40,128]{1,0:T(8,128)S(1)} %get-tuple-element.69), channel_id=1, source_target_pairs={{0,4},{4,0},{8,12},{12,8},{16,20},{20,16},{24,28},{28,24},{32,36},... | collective-permute-start | bytes 61448 | tf_op jit(solution)/shard_map/ppermute | solution.py:653
  36.3 21.8 %collective-permute-start.8 = (f32[80,128]{1,0:T(8,128)S(1)}, f32[80,128]{1,0:T(8,128)S(1)}, u32[]{:S(2)}, u32[]{:S(2)}) collective-permute-start(f32[80,128]{1,0:T(8,128)S(1)} %get-tuple-element.84), channel_id=1, source_target_pairs={{64,128},{128,64},{192,256},{256,192},{320,384},{384,320},{448,512... | collective-permute-start | bytes 122888 | tf_op jit(solution)/shard_map/ppermute | solution.py:653
  48.0 7.0 %collective-permute-start.6 = (f32[78,128]{1,0:T(8,128)S(1)}, f32[78,128]{1,0:T(8,128)S(1)}, u32[]{:S(2)}, u32[]{:S(2)}) collective-permute-start(f32[78,128]{1,0:T(8,128)S(1)} %get-tuple-element.75), channel_id=1, source_target_pairs={{1,2},{2,1},{5,6},{6,5},{9,10},{10,9},{13,14},{14,13},{17,18},{18,... | collective-permute-start | bytes 119816 | tf_op jit(solution)/shard_map/ppermute | solution.py:653
  51.1 5.0 %collective-permute-start.7 = (f32[78,128]{1,0:T(8,128)S(1)}, f32[78,128]{1,0:T(8,128)S(1)}, u32[]{:S(2)}, u32[]{:S(2)}) collective-permute-start(f32[78,128]{1,0:T(8,128)S(1)} %get-tuple-element.76), channel_id=1, source_target_pairs={{0,1},{1,0},{2,3},{3,2},{4,5},{5,4},{6,7},{7,6},{8,9},{9,8},{10,11... | collective-permute-start | bytes 119816 | tf_op jit(solution)/shard_map/ppermute | solution.py:653
  53.1 5.0 %collective-permute-start.9 = (f32[77,128]{1,0:T(8,128)S(1)}, f32[77,128]{1,0:T(8,128)S(1)}, u32[]{:S(2)}, u32[]{:S(2)}) collective-permute-start(f32[77,128]{1,0:T(8,128)S(1)} %get-tuple-element.85), channel_id=1, source_target_pairs={{0,64},{64,0},{128,192},{192,128},{256,320},{320,256},{384,448},{4... | collective-permute-start | bytes 118280 | tf_op jit(solution)/shard_map/ppermute | solution.py:653
  58.2 4.8 %collective-permute-start.10 = (f32[88,128]{1,0:T(8,128)S(1)}, f32[88,128]{1,0:T(8,128)S(1)}, u32[]{:S(2)}, u32[]{:S(2)}) collective-permute-start(f32[88,128]{1,0:T(8,128)S(1)} %get-tuple-element.89), channel_id=1, source_target_pairs={{1,2},{2,1},{5,6},{6,5},{9,10},{10,9},{13,14},{14,13},{17,18},{18,... | collective-permute-start | bytes 135176 | tf_op jit(solution)/shard_map/ppermute | solution.py:653
  60.4 5.0 %collective-permute-start.11 = (f32[88,128]{1,0:T(8,128)S(1)}, f32[88,128]{1,0:T(8,128)S(1)}, u32[]{:S(2)}, u32[]{:S(2)}) collective-permute-start(f32[88,128]{1,0:T(8,128)S(1)} %get-tuple-element.90), channel_id=1, source_target_pairs={{0,1},{1,0},{2,3},{3,2},{4,5},{5,4},{6,7},{7,6},{8,9},{9,8},{10,11... | collective-permute-start | bytes 135176 | tf_op jit(solution)/shard_map/ppermute | solution.py:653
  65.6 8.3 %collective-permute-start.12 = (f32[56,128]{1,0:T(8,128)S(1)}, f32[56,128]{1,0:T(8,128)S(1)}, u32[]{:S(2)}, u32[]{:S(2)}) collective-permute-start(f32[56,128]{1,0:T(8,128)S(1)} %get-tuple-element.93), channel_id=1, source_target_pairs={{4,8},{8,4},{12,16},{16,12},{20,24},{24,20},{28,32},{32,28},{36,40... | collective-permute-start | bytes 86024 | tf_op jit(solution)/shard_map/ppermute | solution.py:653
  71.9 3.1 %collective-permute-start.13 = (f32[56,128]{1,0:T(8,128)S(1)}, f32[56,128]{1,0:T(8,128)S(1)}, u32[]{:S(2)}, u32[]{:S(2)}) collective-permute-start(f32[56,128]{1,0:T(8,128)S(1)} %get-tuple-element.94), channel_id=1, source_target_pairs={{0,4},{4,0},{8,12},{12,8},{16,20},{20,16},{24,28},{28,24},{32,36},... | collective-permute-start | bytes 86024 | tf_op jit(solution)/shard_map/ppermute | solution.py:653

commit v10 on v9

--- a/solution.py
+++ b/solution.py
@@ -422,11 +422,7 @@
     return (coupling_x * edge_z + coupling_z * edge_x) * corner * (1.0 / THETA)
 
 
-def second_block_kernel(
-    u, g, s0, d0, cross2, zy2, xp, xp2, zp, xh, zh, line_odd, line_even,
-    s, d, acc, zp2, yp2, xm, lh,
-    s1,
-):
+def second_step_kernel(u, g, s0, d0, cross2, zy2, s1, d, acc):
     yq2 = zy2[2]
 
     def step(z, carry):
@@ -443,6 +439,18 @@
         s1[z] += zy2[side]
         d[z] += B[0] * zy2[side]
         acc[z] += B[0] * zy2[side]
+
+
+def second_block_kernel(
+    g, s1_in, d_in, acc_in, xp, xp2, zp, xh, zh, line_odd, line_even,
+    s, d, acc, zp2, yp2, xm, lh,
+    s1,
+):
+    def keep(z, carry):
+        s1[z], d[z], acc[z] = s1_in[z], d_in[z], acc_in[z]
+        return carry
+
+    lax.fori_loop(0, NZ, keep, 0, unroll=32)
     take_in(lh, line_even, line_odd, "gz")
     xm[...] = xp2[:, 0:32, :]
     for end, z in ((0, 0), (1, NZ - 1)):
@@ -680,9 +688,10 @@
     )(u, g, diag, s, perm_sum, zp, yp, xp, last_coupling, xh, zh, yodd, yeven)
     even, odd = swap(even, odd, "gx")
     line_even, line_odd = swap(line_even, line_odd, "gz")
+    s, d, acc = call(second_step_kernel, "step", 6, [FULL, FULL, FULL], (), 0.01)(u, g, s, d, cross2, zy2)
     s, d1, acc, zp2, yp2, xm, lh = call(
-        second_block_kernel, "block_2", 13, [FULL, FULL, FULL, (2, 64, NY), (64, NY), face, (2, LINES, NY)], [FULL], 0.01
-    )(u, g, s, d, cross2, zy2, xp, xp2, zp, xh, zh, line_odd, line_even)
+        second_block_kernel, "block_2", 11, [FULL, FULL, FULL, (2, 64, NY), (64, NY), face, (2, LINES, NY)], [FULL], 0.01
+    )(g, s, d, acc, xp, xp2, zp, xh, zh, line_odd, line_even)
     xh2, even, odd, b3 = call(
         second_z_kernel, "z_message_2", 9, [(2, XM2, NY), (ZM2, NY), (ZM2, NY), (16, NY)], [(2, ZM2, NY), (16, NY)]
     )(odd, even, xp, zp, zp2, b, xh, zh, lh)

time: 77.4 us -> 77.4 us (level)
    pallas_call x1 -> x2, Pallas kernels: 1.67 us -> 1.76 us  [the longest x1 1.18 us: per_device(): call(second_block_kernel, 'block_2', 11, [FULL, FULL, FULL, (2, 64, NY),...]
where the time goes in v10:
time: 77.4 us; the launch traced here: 76.9 us
  starting transfers between devices  59.8 us (77%)
  Pallas kernels  8.7 us (11%)
  waiting for transfers between devices  8.16 us (11%)
    ppermute x14, starting transfers between devices, swap(): results.append(lax.ppermute(values, axis, pairs))  59.8 us
    ppermute x14, waiting for transfers between devices, swap(): results.append(lax.ppermute(values, axis, pairs))  8.16 us
    pallas_call x1, Pallas kernels, per_device(): call(face_kernel, 'faces', 4, [FULL, FULL, FULL, BF16_FIELD, (2, XM1, NY)...  2.04 us
    pallas_call x1, Pallas kernels, per_device(): call(third_kernel, 'last_steps', 18, [FULL], [(2, YM2, NY), FULL, FULL, f...  1.92 us
  transfers between devices with their start and end apart: 14, of which 7 were waited for; matrix products, arithmetic and copies ran while one was open for 0% of the time, Pallas kernels for 4%

profile of v10, /device:TPU:283, one launch (start us, length us, event | category | flops | bytes accessed | tf_op | source)
XLA Modules:
  0.0 76.9 jit_solution(8754304161806693437)
XLA Ops:
  0.0 2.0 %faces.1 = (f32[32,32,128]{2,1,0:T(8,128)S(1)}, f32[32,32,128]{2,1,0:T(8,128)S(1)}, f32[32,32,128]{2,1,0:T(8,128)S(1)}, bf16[3,32,32,128]{3,2,1,0:T(8,128)(2,1)S...) custom-call(f32[32,32,128]{2,1,0:T(8,128)} %u_far.1, ...), custom_call_target="tpu_custom_call" | custom-call | bytes 6000000 | tf_op jit(solution)/shard_map/faces/pallas_call | solution.py:668
  2.0 15.1 %collective-permute-start = (f32[104,128]{1,0:T(8,128)S(1)}, f32[104,128]{1,0:T(8,128)S(1)}, u32[]{:S(2)}, u32[]{:S(2)}) collective-permute-start(f32[104,128]{1,0:T(8,128)S(1)} %get-tuple-element.65), channel_id=1, source_target_pairs={{64,128},{128,64},{192,256},{256,192},{320,384},{384,320},{448,512... | collective-permute-start | bytes 159752 | tf_op jit(solution)/shard_map/ppermute | solution.py:661
  17.2 3.1 %collective-permute-start.1 = (f32[104,128]{1,0:T(8,128)S(1)}, f32[104,128]{1,0:T(8,128)S(1)}, u32[]{:S(2)}, u32[]{:S(2)}) collective-permute-start(f32[104,128]{1,0:T(8,128)S(1)} %get-tuple-element.66), channel_id=1, source_target_pairs={{1,2},{2,1},{5,6},{6,5},{9,10},{10,9},{13,14},{14,13},{17,18},{18,... | collective-permute-start | bytes 159752 | tf_op jit(solution)/shard_map/ppermute | solution.py:661
  20.3 1.9 %collective-permute-start.2 = (f32[104,128]{1,0:T(8,128)S(1)}, f32[104,128]{1,0:T(8,128)S(1)}, u32[]{:S(2)}, u32[]{:S(2)}) collective-permute-start(f32[104,128]{1,0:T(8,128)S(1)} %get-tuple-element.67), channel_id=1, source_target_pairs={{0,1},{1,0},{2,3},{3,2},{4,5},{5,4},{6,7},{7,6},{8,9},{9,8},{10,11... | collective-permute-start | bytes 159752 | tf_op jit(solution)/shard_map/ppermute | solution.py:661
  22.2 1.9 %collective-permute-start.3 = (f32[104,128]{1,0:T(8,128)S(1)}, f32[104,128]{1,0:T(8,128)S(1)}, u32[]{:S(2)}, u32[]{:S(2)}) collective-permute-start(f32[104,128]{1,0:T(8,128)S(1)} %get-tuple-element.68), channel_id=1, source_target_pairs={{0,64},{64,0},{128,192},{192,128},{256,320},{320,256},{384,448},{4... | collective-permute-start | bytes 159752 | tf_op jit(solution)/shard_map/ppermute | solution.py:661
  24.1 1.5 %block.1 = (f32[6,32,32,128]{3,2,1,0:T(8,128)S(1)}, f32[32,32,128]{2,1,0:T(8,128)S(1)}, f32[32,32,128]{2,1,0:T(8,128)S(1)}, f32[4,32,128]{2,1,0:T(8,128)S(1)}, f32[96,128]{1,0:T(8,128)S(1)}) custom-call(f32[32,32,128]{2,1,0:T(8,128)S(1)} %get-tuple-element.53.u, f32[32,32,128]{2,1,0:T(8,128)S(1)} %get-tuple-element.54.f, ...), custom_call_target="tpu_custom_call" | custom-call | bytes 7500000 | tf_op jit(solution)/shard_map/block/pallas_call | solution.py:673
  25.7 1.5 %collective-permute-done.3.xeven = f32[104,128]{1,0:T(8,128)S(1)} collective-permute-done((f32[104,128]{1,0:T(8,128)S(1)}, f32[104,128]{1,0:T(8,128)S(1)}, u32[]{:S(2)}, u32[]{:S(2)}) %collective-permute-start.3) | collective-permute-done | bytes 53280 | tf_op jit(solution)/shard_map/ppermute | solution.py:661
  27.4 4.9 %collective-permute-start.4 = (f32[40,128]{1,0:T(8,128)S(1)}, f32[40,128]{1,0:T(8,128)S(1)}, u32[]{:S(2)}, u32[]{:S(2)}) collective-permute-start(f32[40,128]{1,0:T(8,128)S(1)} %get-tuple-element.71), channel_id=1, source_target_pairs={{4,8},{8,4},{12,16},{16,12},{20,24},{24,20},{28,32},{32,28},{36,40... | collective-permute-start | bytes 61448 | tf_op jit(solution)/shard_map/ppermute | solution.py:661
  32.2 1.9 %collective-permute-start.5 = (f32[40,128]{1,0:T(8,128)S(1)}, f32[40,128]{1,0:T(8,128)S(1)}, u32[]{:S(2)}, u32[]{:S(2)}) collective-permute-start(f32[40,128]{1,0:T(8,128)S(1)} %get-tuple-element.72), channel_id=1, source_target_pairs={{0,4},{4,0},{8,12},{12,8},{16,20},{20,16},{24,28},{28,24},{32,36},... | collective-permute-start | bytes 61448 | tf_op jit(solution)/shard_map/ppermute | solution.py:661
  34.2 1.1 %collective-permute-done.5.yeven = f32[40,128]{1,0:T(8,128)S(1)} collective-permute-done((f32[40,128]{1,0:T(8,128)S(1)}, f32[40,128]{1,0:T(8,128)S(1)}, u32[]{:S(2)}, u32[]{:S(2)}) %collective-permute-start.5) | collective-permute-done | bytes 20512 | tf_op jit(solution)/shard_map/ppermute | solution.py:661
  35.3 1.0 %two_steps.1 = (f32[2,40,128]{2,1,0:T(8,128)S(1)}, f32[32,32,128]{2,1,0:T(8,128)S(1)}, f32[32,32,128]{2,1,0:T(8,128)S(1)}, f32[16,128]{1,0:T(8,128)S(1)}, f32[2,...) custom-call(f32[32,32,128]{2,1,0:T(8,128)S(1)} %get-tuple-element.53, ...), custom_call_target="tpu_custom_call" | custom-call | bytes 4500000 | tf_op jit(solution)/shard_map/two_steps/pallas_call | solution.py:684
  36.3 11.7 %collective-permute-start.8 = (f32[80,128]{1,0:T(8,128)S(1)}, f32[80,128]{1,0:T(8,128)S(1)}, u32[]{:S(2)}, u32[]{:S(2)}) collective-permute-start(f32[80,128]{1,0:T(8,128)S(1)} %get-tuple-element.90), channel_id=1, source_target_pairs={{64,128},{128,64},{192,256},{256,192},{320,384},{384,320},{448,512... | collective-permute-start | bytes 122888 | tf_op jit(solution)/shard_map/ppermute | solution.py:661
  48.0 3.1 %collective-permute-start.6 = (f32[78,128]{1,0:T(8,128)S(1)}, f32[78,128]{1,0:T(8,128)S(1)}, u32[]{:S(2)}, u32[]{:S(2)}) collective-permute-start(f32[78,128]{1,0:T(8,128)S(1)} %get-tuple-element.81), channel_id=1, source_target_pairs={{1,2},{2,1},{5,6},{6,5},{9,10},{10,9},{13,14},{14,13},{17,18},{18,... | collective-permute-start | bytes 119816 | tf_op jit(solution)/shard_map/ppermute | solution.py:661
  51.1 1.9 %collective-permute-start.7 = (f32[78,128]{1,0:T(8,128)S(1)}, f32[78,128]{1,0:T(8,128)S(1)}, u32[]{:S(2)}, u32[]{:S(2)}) collective-permute-start(f32[78,128]{1,0:T(8,128)S(1)} %get-tuple-element.82), channel_id=1, source_target_pairs={{0,1},{1,0},{2,3},{3,2},{4,5},{5,4},{6,7},{7,6},{8,9},{9,8},{10,11... | collective-permute-start | bytes 119816 | tf_op jit(solution)/shard_map/ppermute | solution.py:661
  53.1 1.9 %collective-permute-start.9 = (f32[77,128]{1,0:T(8,128)S(1)}, f32[77,128]{1,0:T(8,128)S(1)}, u32[]{:S(2)}, u32[]{:S(2)}) collective-permute-start(f32[77,128]{1,0:T(8,128)S(1)} %get-tuple-element.91), channel_id=1, source_target_pairs={{0,64},{64,0},{128,192},{192,128},{256,320},{320,256},{384,448},{4... | collective-permute-start | bytes 118280 | tf_op jit(solution)/shard_map/ppermute | solution.py:661
  56.2 1.2 %block_2.1 = (f32[32,32,128]{2,1,0:T(8,128)S(1)}, f32[32,32,128]{2,1,0:T(8,128)S(1)}, f32[32,32,128]{2,1,0:T(8,128)S(1)}, f32[2,64,128]{2,1,0:T(8,128)S(1)}, f32...) custom-call(f32[6,32,32,128]{3,2,1,0:T(8,128)S(1)} %get-tuple-element.57.g, ...), custom_call_target="tpu_custom_call" | custom-call | bytes 30000 | tf_op jit(solution)/shard_map/block_2/pallas_call | solution.py:692
  57.4 0.7 collective-permute-done.9.xeven
  58.2 2.2 %collective-permute-start.10 = (f32[88,128]{1,0:T(8,128)S(1)}, f32[88,128]{1,0:T(8,128)S(1)}, u32[]{:S(2)}, u32[]{:S(2)}) collective-permute-start(f32[88,128]{1,0:T(8,128)S(1)} %get-tuple-element.95), channel_id=1, source_target_pairs={{1,2},{2,1},{5,6},{6,5},{9,10},{10,9},{13,14},{14,13},{17,18},{18,... | collective-permute-start | bytes 135176 | tf_op jit(solution)/shard_map/ppermute | solution.py:661
  60.4 1.9 %collective-permute-start.11 = (f32[88,128]{1,0:T(8,128)S(1)}, f32[88,128]{1,0:T(8,128)S(1)}, u32[]{:S(2)}, u32[]{:S(2)}) collective-permute-start(f32[88,128]{1,0:T(8,128)S(1)} %get-tuple-element.96), channel_id=1, source_target_pairs={{0,1},{1,0},{2,3},{3,2},{4,5},{5,4},{6,7},{7,6},{8,9},{9,8},{10,11... | collective-permute-start | bytes 135176 | tf_op jit(solution)/shard_map/ppermute | solution.py:661
  63.0 2.3 %collective-permute-done.11.zeven = f32[88,128]{1,0:T(8,128)S(1)} collective-permute-done((f32[88,128]{1,0:T(8,128)S(1)}, f32[88,128]{1,0:T(8,128)S(1)}, u32[]{:S(2)}, u32[]{:S(2)}) %collective-permute-start.11) | collective-permute-done | bytes 45088 | tf_op jit(solution)/shard_map/ppermute | solution.py:661
  65.6 6.3 %collective-permute-start.12 = (f32[56,128]{1,0:T(8,128)S(1)}, f32[56,128]{1,0:T(8,128)S(1)}, u32[]{:S(2)}, u32[]{:S(2)}) collective-permute-start(f32[56,128]{1,0:T(8,128)S(1)} %get-tuple-element.99), channel_id=1, source_target_pairs={{4,8},{8,4},{12,16},{16,12},{20,24},{24,20},{28,32},{32,28},{36,40... | collective-permute-start | bytes 86024 | tf_op jit(solution)/shard_map/ppermute | solution.py:661
  71.9 1.9 %collective-permute-start.13 = (f32[56,128]{1,0:T(8,128)S(1)}, f32[56,128]{1,0:T(8,128)S(1)}, u32[]{:S(2)}, u32[]{:S(2)}) collective-permute-start(f32[56,128]{1,0:T(8,128)S(1)} %get-tuple-element.100), channel_id=1, source_target_pairs={{0,4},{4,0},{8,12},{12,8},{16,20},{20,16},{24,28},{28,24},{32,36},... | collective-permute-start | bytes 86024 | tf_op jit(solution)/shard_map/ppermute | solution.py:661
  73.8 1.2 %collective-permute-done.13.yeven = f32[56,128]{1,0:T(8,128)S(1)} collective-permute-done((f32[56,128]{1,0:T(8,128)S(1)}, f32[56,128]{1,0:T(8,128)S(1)}, u32[]{:S(2)}, u32[]{:S(2)}) %collective-permute-start.13) | collective-permute-done | bytes 28704 | tf_op jit(solution)/shard_map/ppermute | solution.py:661
  75.0 1.9 %last_steps.1 = f32[32,32,128]{2,1,0:T(8,128)} custom-call(f32[6,32,32,128]{3,2,1,0:T(8,128)S(1)} %get-tuple-element.57.g, f32[32,32,128]{2,1,0:T(8,128)S(1)} %get-tuple-element.83.s2, f32[32,32,128]{2,1,0:T(8,128)S(1)} %get-tuple-element.84.d1, f32[32,32,128]{2,1,0:T(8,128)S(1)} %get-tuple-element.85.acc, f32[2,104,128]{2,1,0:T(8,128)S(1)} %get-tuple-element.61.zp, ...), custom_call_target="tpu_custom_call" | custom-call | bytes 7500000 | tf_op jit(solution)/shard_map/last_steps/pallas_call | solution.py:703
  (13 shorter events, 2.4 us)
Async XLA Ops:
  2.0 23.6 %collective-permute-start = (f32[104,128]{1,0:T(8,128)S(1)}, f32[104,128]{1,0:T(8,128)S(1)}, u32[]{:S(2)}, u32[]{:S(2)}) collective-permute-start(f32[104,128]{1,0:T(8,128)S(1)} %get-tuple-element.65), channel_id=1, source_target_pairs={{64,128},{128,64},{192,256},{256,192},{320,384},{384,320},{448,512... | collective-permute-start | bytes 159752 | tf_op jit(solution)/shard_map/ppermute | solution.py:661
  17.2 8.5 %collective-permute-start.1 = (f32[104,128]{1,0:T(8,128)S(1)}, f32[104,128]{1,0:T(8,128)S(1)}, u32[]{:S(2)}, u32[]{:S(2)}) collective-permute-start(f32[104,128]{1,0:T(8,128)S(1)} %get-tuple-element.66), channel_id=1, source_target_pairs={{1,2},{2,1},{5,6},{6,5},{9,10},{10,9},{13,14},{14,13},{17,18},{18,... | collective-permute-start | bytes 159752 | tf_op jit(solution)/shard_map/ppermute | solution.py:661
  20.3 5.4 %collective-permute-start.2 = (f32[104,128]{1,0:T(8,128)S(1)}, f32[104,128]{1,0:T(8,128)S(1)}, u32[]{:S(2)}, u32[]{:S(2)}) collective-permute-start(f32[104,128]{1,0:T(8,128)S(1)} %get-tuple-element.67), channel_id=1, source_target_pairs={{0,1},{1,0},{2,3},{3,2},{4,5},{5,4},{6,7},{7,6},{8,9},{9,8},{10,11... | collective-permute-start | bytes 159752 | tf_op jit(solution)/shard_map/ppermute | solution.py:661
  22.2 4.9 %collective-permute-start.3 = (f32[104,128]{1,0:T(8,128)S(1)}, f32[104,128]{1,0:T(8,128)S(1)}, u32[]{:S(2)}, u32[]{:S(2)}) collective-permute-start(f32[104,128]{1,0:T(8,128)S(1)} %get-tuple-element.68), channel_id=1, source_target_pairs={{0,64},{64,0},{128,192},{192,128},{256,320},{320,256},{384,448},{4... | collective-permute-start | bytes 159752 | tf_op jit(solution)/shard_map/ppermute | solution.py:661
  27.4 6.8 %collective-permute-start.4 = (f32[40,128]{1,0:T(8,128)S(1)}, f32[40,128]{1,0:T(8,128)S(1)}, u32[]{:S(2)}, u32[]{:S(2)}) collective-permute-start(f32[40,128]{1,0:T(8,128)S(1)} %get-tuple-element.71), channel_id=1, source_target_pairs={{4,8},{8,4},{12,16},{16,12},{20,24},{24,20},{28,32},{32,28},{36,40... | collective-permute-start | bytes 61448 | tf_op jit(solution)/shard_map/ppermute | solution.py:661
  32.2 3.1 %collective-permute-start.5 = (f32[40,128]{1,0:T(8,128)S(1)}, f32[40,128]{1,0:T(8,128)S(1)}, u32[]{:S(2)}, u32[]{:S(2)}) collective-permute-start(f32[40,128]{1,0:T(8,128)S(1)} %get-tuple-element.72), channel_id=1, source_target_pairs={{0,4},{4,0},{8,12},{12,8},{16,20},{20,16},{24,28},{28,24},{32,36},... | collective-permute-start | bytes 61448 | tf_op jit(solution)/shard_map/ppermute | solution.py:661
  36.3 21.8 %collective-permute-start.8 = (f32[80,128]{1,0:T(8,128)S(1)}, f32[80,128]{1,0:T(8,128)S(1)}, u32[]{:S(2)}, u32[]{:S(2)}) collective-permute-start(f32[80,128]{1,0:T(8,128)S(1)} %get-tuple-element.90), channel_id=1, source_target_pairs={{64,128},{128,64},{192,256},{256,192},{320,384},{384,320},{448,512... | collective-permute-start | bytes 122888 | tf_op jit(solution)/shard_map/ppermute | solution.py:661
  48.0 7.6 %collective-permute-start.6 = (f32[78,128]{1,0:T(8,128)S(1)}, f32[78,128]{1,0:T(8,128)S(1)}, u32[]{:S(2)}, u32[]{:S(2)}) collective-permute-start(f32[78,128]{1,0:T(8,128)S(1)} %get-tuple-element.81), channel_id=1, source_target_pairs={{1,2},{2,1},{5,6},{6,5},{9,10},{10,9},{13,14},{14,13},{17,18},{18,... | collective-permute-start | bytes 119816 | tf_op jit(solution)/shard_map/ppermute | solution.py:661
  51.1 5.0 %collective-permute-start.7 = (f32[78,128]{1,0:T(8,128)S(1)}, f32[78,128]{1,0:T(8,128)S(1)}, u32[]{:S(2)}, u32[]{:S(2)}) collective-permute-start(f32[78,128]{1,0:T(8,128)S(1)} %get-tuple-element.82), channel_id=1, source_target_pairs={{0,1},{1,0},{2,3},{3,2},{4,5},{5,4},{6,7},{7,6},{8,9},{9,8},{10,11... | collective-permute-start | bytes 119816 | tf_op jit(solution)/shard_map/ppermute | solution.py:661
  53.1 5.0 %collective-permute-start.9 = (f32[77,128]{1,0:T(8,128)S(1)}, f32[77,128]{1,0:T(8,128)S(1)}, u32[]{:S(2)}, u32[]{:S(2)}) collective-permute-start(f32[77,128]{1,0:T(8,128)S(1)} %get-tuple-element.91), channel_id=1, source_target_pairs={{0,64},{64,0},{128,192},{192,128},{256,320},{320,256},{384,448},{4... | collective-permute-start | bytes 118280 | tf_op jit(solution)/shard_map/ppermute | solution.py:661
  58.2 4.8 %collective-permute-start.10 = (f32[88,128]{1,0:T(8,128)S(1)}, f32[88,128]{1,0:T(8,128)S(1)}, u32[]{:S(2)}, u32[]{:S(2)}) collective-permute-start(f32[88,128]{1,0:T(8,128)S(1)} %get-tuple-element.95), channel_id=1, source_target_pairs={{1,2},{2,1},{5,6},{6,5},{9,10},{10,9},{13,14},{14,13},{17,18},{18,... | collective-permute-start | bytes 135176 | tf_op jit(solution)/shard_map/ppermute | solution.py:661
  60.4 5.0 %collective-permute-start.11 = (f32[88,128]{1,0:T(8,128)S(1)}, f32[88,128]{1,0:T(8,128)S(1)}, u32[]{:S(2)}, u32[]{:S(2)}) collective-permute-start(f32[88,128]{1,0:T(8,128)S(1)} %get-tuple-element.96), channel_id=1, source_target_pairs={{0,1},{1,0},{2,3},{3,2},{4,5},{5,4},{6,7},{7,6},{8,9},{9,8},{10,11... | collective-permute-start | bytes 135176 | tf_op jit(solution)/shard_map/ppermute | solution.py:661
  65.6 8.3 %collective-permute-start.12 = (f32[56,128]{1,0:T(8,128)S(1)}, f32[56,128]{1,0:T(8,128)S(1)}, u32[]{:S(2)}, u32[]{:S(2)}) collective-permute-start(f32[56,128]{1,0:T(8,128)S(1)} %get-tuple-element.99), channel_id=1, source_target_pairs={{4,8},{8,4},{12,16},{16,12},{20,24},{24,20},{28,32},{32,28},{36,40... | collective-permute-start | bytes 86024 | tf_op jit(solution)/shard_map/ppermute | solution.py:661
  71.9 3.1 %collective-permute-start.13 = (f32[56,128]{1,0:T(8,128)S(1)}, f32[56,128]{1,0:T(8,128)S(1)}, u32[]{:S(2)}, u32[]{:S(2)}) collective-permute-start(f32[56,128]{1,0:T(8,128)S(1)} %get-tuple-element.100), channel_id=1, source_target_pairs={{0,4},{4,0},{8,12},{12,8},{16,20},{20,16},{24,28},{28,24},{32,36},... | collective-permute-start | bytes 86024 | tf_op jit(solution)/shard_map/ppermute | solution.py:661
